TPU v7x, 128 devices: a whole 4x4x4 slice. The times are simulated.
128 devices in a mesh: seq: 16 (over x, y_lo, core), fsdp: 8 (over z, y_hi).
Axes of the slice: x: 4, y: 4 (y_hi: 2, y_lo: 2; y = y_hi * 2 + y_lo), z: 4, core: 2. Of those that a mesh axis runs over, the one named last changes fastest.
Arguments:
- hidden_in: bfloat16 [8, 2048, 1024], P('fsdp', 'seq'), may hold values from -6 to 6
- norm1_gain: bfloat16 [1024], P('seq'), may hold values from 0.099609375 to 1.8984375
- norm1_shift: bfloat16 [1024], P('seq'), may hold values from -3 to 3
- qkv_weight: bfloat16 [1024, 3072], P('fsdp', 'seq'), may hold values from -0.1875 to 0.1875
- query_bias: bfloat16 [1024], P('seq'), may hold values from -4 to 4
- value_bias: bfloat16 [1024], P('seq'), may hold values from -4 to 4
- proj_weight: bfloat16 [1024, 1024], P('fsdp', 'seq'), may hold values from -0.75 to 0.75
- proj_bias: bfloat16 [1024], P('seq'), may hold values from -4 to 4
- norm2_gain: bfloat16 [1024], P('seq'), may hold values from 0.099609375 to 1.8984375
- norm2_shift: bfloat16 [1024], P('seq'), may hold values from -3 to 3
- up_weight: bfloat16 [1024, 4096], P('fsdp', 'seq'), may hold values from -0.1875 to 0.1875
- up_bias: bfloat16 [4096], P('seq'), may hold values from -4 to 4
- down_weight: bfloat16 [4096, 1024], P('fsdp', 'seq'), may hold values from -0.09375 to 0.09375
- down_bias: bfloat16 [1024], P('seq'), may hold values from -4 to 4
- out_cotangent: bfloat16 [8, 2048, 1024], P('fsdp', 'seq'), may hold values from -6 to 6
Outputs:
- layer_out: bfloat16 [8, 2048, 1024], P('fsdp', 'seq')
- input_grad: bfloat16 [8, 2048, 1024], P('fsdp', 'seq')
- grad_norm1_gain: float32 [1024], P('seq')
- grad_norm1_shift: float32 [1024], P('seq')
- grad_qkv_weight: float32 [1024, 3072], P('fsdp', 'seq')
- grad_query_bias: float32 [1024], P('seq')
- grad_value_bias: float32 [1024], P('seq')
- grad_proj_weight: float32 [1024, 1024], P('fsdp', 'seq')
- grad_proj_bias: float32 [1024], P('seq')
- grad_norm2_gain: float32 [1024], P('seq')
- grad_norm2_shift: float32 [1024], P('seq')
- grad_up_weight: float32 [1024, 4096], P('fsdp', 'seq')
- grad_up_bias: float32 [4096], P('seq')
- grad_down_weight: float32 [4096, 1024], P('fsdp', 'seq')
- grad_down_bias: float32 [1024], P('seq')
All inputs are finite; a program needn't handle non-finite values.
Results may differ from a plain program's by a relative error of at most 0.022.
Values may be sent and summed in bfloat16 or wider, within the bound.
A program may use at most 128 MiB of HBM per device.

v0:
```python
import jax
import jax.numpy as jnp
from jax import lax
from jax.sharding import PartitionSpec as P

H = 16
HD = 64
FF = 4096


def layer_norm(values, gain, shift):
    average = jnp.mean(values, axis=-1, keepdims=True)
    centered = values - average
    spread = jnp.mean(centered * centered, axis=-1, keepdims=True)
    return centered * lax.rsqrt(spread + 1e-05) * gain + shift


def gelu_tanh(values):
    return jax.nn.gelu(values, approximate=True)


def plain_dot(left, right):
    return jnp.dot(left, right, preferred_element_type=jnp.float32)


def lead_dot(left, right):
    return lax.dot_general(
        left, right, (((0,), (0,)), ((), ())), preferred_element_type=jnp.float32
    )


def tail_dot(left, right):
    return lax.dot_general(
        left, right, (((1,), (1,)), ((), ())), preferred_element_type=jnp.float32
    )


def attn_rows(first, second):
    return (
        lax.all_gather(first, "fsdp", axis=0, tiled=True),
        lax.all_gather(second, "fsdp", axis=0, tiled=True),
    )


def attn_cols(first, second, smalls):
    return (
        lax.all_gather(first, "seq", axis=1, tiled=True),
        lax.all_gather(second, "seq", axis=1, tiled=True),
        lax.all_gather(smalls[0], "seq", axis=0, tiled=True),
        lax.all_gather(smalls[1], "seq", axis=0, tiled=True),
        lax.all_gather(smalls[2], "seq", axis=0, tiled=True),
        lax.all_gather(smalls[3], "seq", axis=0, tiled=True),
        lax.all_gather(smalls[4], "seq", axis=0, tiled=True),
        lax.all_gather(smalls[5], "seq", axis=0, tiled=True),
        lax.all_gather(smalls[6], "seq", axis=0, tiled=True),
        lax.all_gather(smalls[7], "seq", axis=0, tiled=True),
    )


def mlp_rows(first, second):
    return (
        lax.all_gather(first, "fsdp", axis=0, tiled=True),
        lax.all_gather(second, "fsdp", axis=0, tiled=True),
    )


def attn_grad_rows(first, second):
    return (
        lax.psum_scatter(
            first.astype(jnp.bfloat16), "fsdp", scatter_dimension=0, tiled=True
        ).astype(jnp.float32),
        lax.psum_scatter(
            second.astype(jnp.bfloat16), "fsdp", scatter_dimension=0, tiled=True
        ).astype(jnp.float32),
    )


def attn_grad_cols(first, second):
    return (
        lax.psum_scatter(first.astype(jnp.bfloat16), "seq", scatter_dimension=1, tiled=True).astype(
            jnp.float32
        ),
        lax.psum_scatter(
            second.astype(jnp.bfloat16), "seq", scatter_dimension=1, tiled=True
        ).astype(jnp.float32),
    )


def mlp_grad_rows(first, second):
    return (
        lax.psum_scatter(
            first.astype(jnp.bfloat16), "fsdp", scatter_dimension=0, tiled=True
        ).astype(jnp.float32),
        lax.psum_scatter(
            second.astype(jnp.bfloat16), "fsdp", scatter_dimension=0, tiled=True
        ).astype(jnp.float32),
    )


def gather_block(rows_fn, cols_fn, first, second, smalls):
    gathered = cols_fn(first, second, smalls)
    return (rows_fn(gathered[0], gathered[1]), gathered[2:])


def reduce_block(rows_fn, cols_fn, first, second):
    first, second = rows_fn(first, second)
    return cols_fn(first, second)


def mlp_local(up_weight, down_weight):
    up_part, down_part = mlp_rows(up_weight, down_weight)
    down_rows = lax.all_to_all(down_part, "seq", split_axis=0, concat_axis=1, tiled=True)
    return (up_part, down_rows)


def block_scores(rows, keys, start, slopes, positions):
    raw = jnp.einsum("qhd,khd->hqk", rows, keys, preferred_element_type=jnp.float32)
    row_pos = start + jnp.arange(rows.shape[0])
    offset = (positions[None, :] - row_pos[:, None]).astype(jnp.float32)
    scores = raw * rows.shape[2] ** (-0.5) + slopes[:, None, None] * offset[None]
    return jnp.where((offset <= 0.0)[None], scores, -1e30)


def attend_forward(queries, keys, values, slopes):
    length, heads, size = queries.shape
    block = min(512, length)
    positions = jnp.arange(length)

    def one_block(index):
        start = index * block
        rows = lax.dynamic_slice_in_dim(queries, start, block, 0)
        scores = block_scores(rows, keys, start, slopes, positions)
        peak = jnp.max(scores, axis=-1, keepdims=True)
        expo = jnp.exp(scores - peak)
        total = jnp.sum(expo, axis=-1, keepdims=True)
        weights = (expo / total).astype(jnp.bfloat16)
        context = jnp.einsum("hqk,khd->qhd", weights, values, preferred_element_type=jnp.float32)
        return (context.astype(jnp.bfloat16), (peak + jnp.log(total))[..., 0])

    contexts, logsums = lax.map(one_block, jnp.arange(length // block))
    return (contexts.reshape(length, heads * size), logsums)


def attend_backward(queries, keys, values, grad_ctx, logsums, slopes):
    length, heads, size = queries.shape
    block = min(512, length)
    positions = jnp.arange(length)
    scale = size ** (-0.5)

    def one_block(carry, index):
        key_acc, value_acc = carry
        start = index * block
        rows = lax.dynamic_slice_in_dim(queries, start, block, 0)
        grad_rows = lax.dynamic_slice_in_dim(grad_ctx, start, block, 0)
        scores = block_scores(rows, keys, start, slopes, positions)
        probs = jnp.exp(scores - logsums[index][..., None])
        grad_probs = jnp.einsum(
            "qhd,khd->hqk", grad_rows, values, preferred_element_type=jnp.float32
        )
        inner = jnp.sum(probs * grad_probs, axis=-1, keepdims=True)
        grad_scores = (probs * (grad_probs - inner) * scale).astype(jnp.bfloat16)
        query_grad = jnp.einsum(
            "hqk,khd->qhd", grad_scores, keys, preferred_element_type=jnp.float32
        )
        key_acc = key_acc + jnp.einsum(
            "hqk,qhd->khd", grad_scores, rows, preferred_element_type=jnp.float32
        )
        value_acc = value_acc + jnp.einsum(
            "hqk,qhd->khd",
            probs.astype(jnp.bfloat16),
            grad_rows,
            preferred_element_type=jnp.float32,
        )
        return ((key_acc, value_acc), query_grad.astype(jnp.bfloat16))

    zeros = jnp.zeros((length, heads, size), jnp.float32)
    (key_acc, value_acc), query_grads = lax.scan(
        one_block, (zeros, zeros), jnp.arange(length // block)
    )
    return (
        query_grads.reshape(length, heads * size),
        key_acc.astype(jnp.bfloat16).reshape(length, heads * size),
        value_acc.astype(jnp.bfloat16).reshape(length, heads * size),
    )


def own_slice(vector):
    part = vector.shape[0] // lax.axis_size("seq")
    return lax.dynamic_slice_in_dim(vector, lax.axis_index("seq") * part, part, 0)


def per_device(
    hidden_in,
    norm1_gain,
    norm1_shift,
    qkv_weight,
    query_bias,
    value_bias,
    proj_weight,
    proj_bias,
    norm2_gain,
    norm2_shift,
    up_weight,
    up_bias,
    down_weight,
    down_bias,
    out_cotangent,
):
    inputs = hidden_in[0].astype(jnp.float32)
    cotangent = out_cotangent[0].astype(jnp.float32)
    cot_low = out_cotangent[0]
    width = inputs.shape[1]
    attn_smalls = (
        norm1_gain,
        norm1_shift,
        query_bias,
        value_bias,
        proj_bias,
        norm2_gain,
        norm2_shift,
        down_bias,
    )
    (qkv_full, proj_full), attn_params = gather_block(
        attn_rows, attn_cols, qkv_weight, proj_weight, attn_smalls
    )
    gain_one, shift_one, bias_query, bias_value, bias_proj, gain_two, shift_two, bias_down = [
        p.astype(jnp.float32) for p in attn_params
    ]
    normed_one = layer_norm(inputs, gain_one, shift_one).astype(jnp.bfloat16)
    joined = plain_dot(normed_one, qkv_full)
    queries = (joined[:, :width] + bias_query).astype(jnp.bfloat16)
    keys = joined[:, width : 2 * width].astype(jnp.bfloat16)
    values = (joined[:, 2 * width :] + bias_value).astype(jnp.bfloat16)
    head_q, head_k, head_v = (
        lax.all_to_all(queries, "seq", split_axis=1, concat_axis=0, tiled=True),
        lax.all_to_all(keys, "seq", split_axis=1, concat_axis=0, tiled=True),
        lax.all_to_all(values, "seq", split_axis=1, concat_axis=0, tiled=True),
    )
    length = head_q.shape[0]
    local_heads = head_q.shape[1] // HD
    head_ids = lax.axis_index("seq") * local_heads + jnp.arange(local_heads)
    slopes = jnp.exp2(-8.0 * (head_ids.astype(jnp.float32) + 1.0) / H)
    query_heads = head_q.reshape(length, local_heads, HD)
    key_heads = head_k.reshape(length, local_heads, HD)
    value_heads = head_v.reshape(length, local_heads, HD)
    context_heads, logsums = attend_forward(query_heads, key_heads, value_heads, slopes)
    context = lax.all_to_all(context_heads, "seq", split_axis=0, concat_axis=1, tiled=True)
    middle = inputs + plain_dot(context, proj_full) + bias_proj
    normed_two = layer_norm(middle, gain_two, shift_two).astype(jnp.bfloat16)
    up_part, down_rows = mlp_local(up_weight, down_weight)
    normed_all, cot_all = (
        lax.all_gather(normed_two, "seq", axis=0, tiled=True),
        lax.all_gather(cot_low, "seq", axis=0, tiled=True),
    )
    upper = plain_dot(normed_all, up_part) + up_bias.astype(jnp.float32)
    activ = gelu_tanh(upper).astype(jnp.bfloat16)
    down_sum = lax.psum_scatter(
        plain_dot(activ, down_rows).astype(jnp.bfloat16), "seq", scatter_dimension=0, tiled=True
    ).astype(jnp.float32)
    layer_out = middle + down_sum + bias_down
    up_part, down_rows = mlp_local(up_weight, down_weight)
    grad_down_local = lead_dot(activ, cot_all)
    grad_activ = tail_dot(cot_all, down_rows)
    gelu_pull = jax.vjp(gelu_tanh, upper)[1]
    grad_upper = gelu_pull(grad_activ)[0].astype(jnp.bfloat16)
    grad_up_local = lead_dot(normed_all, grad_upper)
    bias_part = jnp.sum(grad_upper.astype(jnp.float32), axis=0)
    grad_up_bias = lax.dynamic_update_slice_in_dim(
        jnp.zeros((FF,), jnp.float32), bias_part, lax.axis_index("seq") * bias_part.shape[0], 0
    )
    grad_normed_two = lax.psum_scatter(
        tail_dot(grad_upper, up_part), "seq", scatter_dimension=0, tiled=True
    )
    down_back = lax.all_to_all(
        grad_down_local.astype(jnp.bfloat16), "seq", split_axis=1, concat_axis=0, tiled=True
    ).astype(grad_down_local.dtype)
    grad_up_shard, grad_down_shard = mlp_grad_rows(grad_up_local, down_back)
    grad_down_bias = jnp.sum(cot_low.astype(jnp.float32), axis=0)
    norm_two_pull = jax.vjp(layer_norm, middle, gain_two, shift_two)[1]
    grad_mid_norm, grad_gain_two, grad_shift_two = norm_two_pull(grad_normed_two)
    grad_middle = cotangent + grad_mid_norm
    (qkv_full, proj_full), attn_params = gather_block(
        attn_rows, attn_cols, qkv_weight, proj_weight, attn_smalls
    )
    grad_branch = grad_middle.astype(jnp.bfloat16)
    grad_proj = lead_dot(context, grad_branch)
    grad_proj_bias = jnp.sum(grad_branch.astype(jnp.float32), axis=0)
    grad_context = tail_dot(grad_branch, proj_full).astype(jnp.bfloat16)
    grad_ctx_heads = lax.all_to_all(grad_context, "seq", split_axis=1, concat_axis=0, tiled=True)
    grad_hq, grad_hk, grad_hv = attend_backward(
        query_heads,
        key_heads,
        value_heads,
        grad_ctx_heads.reshape(length, local_heads, HD),
        logsums,
        slopes,
    )
    grad_query, grad_key, grad_value = (
        lax.all_to_all(grad_hq, "seq", split_axis=0, concat_axis=1, tiled=True),
        lax.all_to_all(grad_hk, "seq", split_axis=0, concat_axis=1, tiled=True),
        lax.all_to_all(grad_hv, "seq", split_axis=0, concat_axis=1, tiled=True),
    )
    grad_joined = jnp.concatenate([grad_query, grad_key, grad_value], axis=1)
    grad_qkv = lead_dot(normed_one, grad_joined)
    grad_normed_one = tail_dot(grad_joined, qkv_full)
    norm_one_pull = jax.vjp(layer_norm, inputs, gain_one, shift_one)[1]
    grad_in_norm, grad_gain_one, grad_shift_one = norm_one_pull(grad_normed_one)
    input_grad = grad_middle + grad_in_norm
    grad_qkv_shard, grad_proj_shard = reduce_block(
        attn_grad_rows, attn_grad_cols, grad_qkv, grad_proj
    )
    summed = lax.psum(
        (
            grad_gain_one,
            grad_shift_one,
            jnp.sum(grad_query.astype(jnp.float32), axis=0),
            jnp.sum(grad_value.astype(jnp.float32), axis=0),
            grad_proj_bias,
            grad_gain_two,
            grad_shift_two,
            grad_up_bias,
            grad_down_bias,
        ),
        ("seq", "fsdp"),
    )
    owned = [own_slice(vector) for vector in summed]
    return (
        layer_out.astype(jnp.bfloat16)[None],
        input_grad.astype(jnp.bfloat16)[None],
        owned[0],
        owned[1],
        grad_qkv_shard,
        owned[2],
        owned[3],
        grad_proj_shard,
        owned[4],
        owned[5],
        owned[6],
        grad_up_shard,
        owned[7],
        grad_down_shard,
        owned[8],
    )


def solution(mesh):
    return jax.shard_map(
        per_device,
        mesh=mesh,
        in_specs=(
            P("fsdp", "seq", None),
            P("seq"),
            P("seq"),
            P("fsdp", "seq"),
            P("seq"),
            P("seq"),
            P("fsdp", "seq"),
            P("seq"),
            P("seq"),
            P("seq"),
            P("fsdp", "seq"),
            P("seq"),
            P("fsdp", "seq"),
            P("seq"),
            P("fsdp", "seq", None),
        ),
        out_specs=(
            P("fsdp", "seq", None),
            P("fsdp", "seq", None),
            P("seq"),
            P("seq"),
            P("fsdp", "seq"),
            P("seq"),
            P("seq"),
            P("fsdp", "seq"),
            P("seq"),
            P("seq"),
            P("seq"),
            P("fsdp", "seq"),
            P("seq"),
            P("fsdp", "seq"),
            P("seq"),
        ),
        check_vma=False,
    )
```

profile of v0, /device:TPU:0, one launch (start us, length us, event | category | flops | bytes accessed | tf_op | source)
XLA Modules:
  0.0 962.5 jit_solution(12750521069570471039)
XLA Ops:
  7.2 23.7 %all_gather.56 = bf16[128,3072]{0,1:T(8,128)(2,1)} all-gather(bf16[128,192]{0,1:T(8,128)(2,1)} %param.22), channel_id=1, replica_groups=mesh['seq'=16,'fsdp'=8] {'seq'}, dimensions={1}, use_global_device_ids=true | all-gather | bytes 835584 | tf_op jit(solution)/shard_map/all_gather | solution.py:47
  39.6 53.9 %all-reduce.9 = (bf16[1024]{0:T(1024)(128)(2,1)S(1)}, bf16[1024]{0:T(1024)(128)(2,1)S(1)}, bf16[1024]{0:T(1024)(128)(2,1)S(1)}, bf16[1024]{0:T(1024)(128)(2,1)S(...) all-reduce(bf16[1024]{0:T(1024)(128)(2,1)S(1)} %dynamic-update-slic, ...), channel_id=1, replica_groups=mesh['seq'=16,'fsdp'=8] {'seq'}, use_global_device_ids=true, to_apply=%add.1 | all-reduce | flops 8192 | bytes 32768
  94.9 30.4 %all-gather.6.cloned.1.call-done = bf16[1024,3072]{0,1:T(8,128)(2,1)} async-done(((bf16[128,3072]{0,1:T(8,128)(2,1)}), bf16[1024,3072]{0,1:T(8,128)(2,1)}) %all-gather.6.cloned.1.call-update) | async-done | bytes 6291472 | tf_op jit(solution)/shard_map/all_gather | solution.py:40
  136.5 6.7 all-to-all-done.1
  147.6 6.8 all-to-all-done.2
  158.0 22.0 %all_gather.60 = bf16[128,1024]{0,1:T(8,128)(2,1)} all-gather(bf16[128,64]{0,1:T(8,128)(2,1)S(1)} %copy-done.11), channel_id=1, replica_groups=mesh['seq'=16,'fsdp'=8] {'seq'}, dimensions={1}, use_global_device_ids=true | all-gather | bytes 278528 | tf_op jit(solution)/shard_map/all_gather | solution.py:48
  181.1 18.6 %while.28 = (s32[]{:T(128)}, bf16[4,512,1,64]{1,3,2,0:T(8,128)(2,1)S(1)}, f32[4,1,512]{2,1,0:T(1,128)S(1)}, s32[4]{0:T(128)S(1)}, bf16[2048,1,64]{0,2,1:T(8,128)...) while((s32[]{:T(128)}, ...), condition=%wide.region_5.6_spmd.clone, body=%wide.region_2.5_spmd.clone.sunk | while | flops 282099712 | bytes 13263051 | solution.py:140
  204.4 26.7 %all-gather.8.cloned.1.call-done = bf16[1024,1024]{0,1:T(8,128)(2,1)} async-done(((bf16[128,1024]{0,1:T(8,128)(2,1)}), bf16[1024,1024]{0,1:T(8,128)(2,1)}) %all-gather.8.cloned.1.call-update) | async-done | bytes 2097168 | tf_op jit(solution)/shard_map/all_gather | solution.py:41
  235.4 38.5 %all_gather.67 = bf16[4096,64]{0,1:T(8,128)(2,1)S(1)} all-gather(bf16[512,64]{0,1:T(8,128)(2,1)S(1)} %copy-done.9), channel_id=1, replica_groups=mesh['seq'=16,'fsdp'=8] {'fsdp'}, dimensions={0}, use_global_device_ids=true | all-gather | bytes 589824 | tf_op jit(solution)/shard_map/all_gather | solution.py:63
  278.8 40.6 %all_gather.66 = bf16[1024,256]{1,0:T(8,128)(2,1)S(1)} all-gather(bf16[128,256]{1,0:T(8,128)(2,1)S(1)} %copy-done.10), channel_id=1, replica_groups=mesh['seq'=16,'fsdp'=8] {'fsdp'}, dimensions={0}, use_global_device_ids=true | all-gather | bytes 589824 | tf_op jit(solution)/shard_map/all_gather | solution.py:62
  341.3 87.8 %reduce-scatter.15.cloned.1.call-done = f32[128,1024]{1,0:T(8,128)} async-done(((f32[2048,1024]{1,0:T(8,128)}), f32[128,1024]{1,0:T(8,128)}) %reduce-scatter.15.cloned.1.call-update) | async-done | bytes 524304 | tf_op jit(solution)/shard_map/reduce_scatter | solution.py:271
  430.4 71.5 %reduce-scatter.13.cloned.1.call-done = bf16[128,1024]{1,0:T(8,128)(2,1)} async-done(((bf16[2048,1024]{1,0:T(8,128)(2,1)}), bf16[128,1024]{1,0:T(8,128)(2,1)}) %reduce-scatter.13.cloned.1.call-update) | async-done | bytes 262160 | tf_op jit(solution)/shard_map/reduce_scatter | solution.py:257
  526.0 6.9 all-to-all-done.9
  536.5 9.5 reduce-scatter.23.cloned.1.call-start
  548.3 34.3 %while.29 = (s32[]{:T(128)}, f32[2048,1,64]{0,2,1:T(8,128)S(1)}, f32[2048,1,64]{0,2,1:T(8,128)S(1)}, bf16[4,512,1,64]{1,3,2,0:T(8,128)(2,1)S(1)}, s32[4]{0:T(128...) while((s32[]{:T(128)}, f32[2048,1,64]{0,2,1:T(8,128)S(1)}, ...), condition=%wide.region_14.15_spmd.clone, body=%wide.region_12.14_spmd.clone.sunk | while | flops 687374336 | bytes 34683168 | solution.py:177
  583.8 5.6 all-to-all-start.6
  590.3 6.8 all-to-all-done.6
  600.8 7.5 all-to-all-done.8
  608.3 10.5 %all_to_all.183 = bf16[16,128,64]{1,2,0:T(8,128)(2,1)S(1)} all-to-all(bf16[16,128,64]{1,2,0:T(8,128)(2,1)S(1)} %copy.105), channel_id=1, replica_groups=mesh['seq'=16,'fsdp'=8] {'seq'}, dimensions={0} | all-to-all | bytes 524288 | tf_op jit(solution)/shard_map/all_to_all | solution.py:300
  625.8 30.7 %reduce-scatter.21.cloned.1.call-done = bf16[128,256]{1,0:T(8,128)(2,1)} async-done(((bf16[1024,256]{1,0:T(8,128)(2,1)}), bf16[128,256]{1,0:T(8,128)(2,1)}) %reduce-scatter.21.cloned.1.call-update) | async-done | bytes 65552 | tf_op jit(solution)/shard_map/reduce_scatter | solution.py:91
  658.0 71.9 %reduce-scatter.23.cloned.1.call-done = bf16[512,64]{0,1:T(8,128)(2,1)} async-done(((bf16[4096,64]{0,1:T(8,128)(2,1)}), bf16[512,64]{0,1:T(8,128)(2,1)}) %reduce-scatter.23.cloned.1.call-update) | async-done | bytes 65552 | tf_op jit(solution)/shard_map/reduce_scatter | solution.py:94
  731.4 99.7 %reduce-scatter.17.cloned.1.call-done = bf16[128,3072]{1,0:T(8,128)(2,1)} async-done(((bf16[1024,3072]{1,0:T(8,128)(2,1)}), bf16[128,3072]{1,0:T(8,128)(2,1)}) %reduce-scatter.17.cloned.1.call-update) | async-done | bytes 786448 | tf_op jit(solution)/shard_map/reduce_scatter | solution.py:69
  838.2 64.9 %all-reduce.8 = (f32[1024]{0:T(1024)S(1)}, f32[1024]{0:T(1024)S(1)}, f32[1024]{0:T(1024)S(1)}, f32[1024]{0:T(1024)S(1)}, f32[1024]{0:T(1024)S(1)}, /*index=5*/f3...) all-reduce(f32[1024]{0:T(1024)S(1)} %get-tuple-element.265, ...), channel_id=1, replica_groups=mesh['seq'=16,'fsdp'=8] {'seq','fsdp'}, use_global_device_ids=true, to_apply=%region_18.19 | all-reduce | flops 12288 | bytes 98304 | tf_op jit(solution)/shard_map/psum | solution.py:312
  910.9 42.9 %reduce-scatter.25.cloned.1.call-done = bf16[192,128]{1,0:T(8,128)(2,1)} async-done(((bf16[3072,128]{1,0:T(8,128)(2,1)}), bf16[192,128]{1,0:T(8,128)(2,1)}) %reduce-scatter.25.cloned.1.call-update) | async-done | bytes 49168
  (243 shorter events, 167.6 us)
Async XLA Ops:
  7.2 87.5 %copy-start = (bf16[1,128,1024]{2,1,0:T(8,128)(2,1)S(1)}, bf16[1,128,1024]{2,1,0:T(8,128)(2,1)}, u32[]{:S(2)}) copy-start(bf16[1,128,1024]{2,1,0:T(8,128)(2,1)} %param.19) | copy-start | bytes 786436
  7.2 118.1 %all-gather.6.cloned.1.call-start = ((), (), s32[]{:S(2)}) async-start(), calls=%async_computation.18 | async-start | bytes 7077888 | tf_op jit(solution)/shard_map/all_gather | solution.py:40
  131.2 12.0 %all-to-all-start.1 = ((bf16[128,16,64]{0,2,1:T(8,128)(2,1)}), bf16[128,16,64]{0,2,1:T(8,128)(2,1)S(1)}, u32[]{:S(2)}, u32[]{:S(2)}) async-start(bf16[128,16,64]{0,2,1:T(8,128)(2,1)} %bitcast.4), calls=%async_computation.1 | async-start | bytes 524288 | tf_op jit(solution)/shard_map/all_to_all | solution.py:236
  143.2 11.2 %all-to-all-start.2 = ((bf16[128,16,64]{0,2,1:T(8,128)(2,1)}), bf16[128,16,64]{0,2,1:T(8,128)(2,1)S(1)}, u32[]{:S(2)}, u32[]{:S(2)}) async-start(bf16[128,16,64]{0,2,1:T(8,128)(2,1)} %bitcast.7), calls=%async_computation.2 | async-start | bytes 524288 | tf_op jit(solution)/shard_map/all_to_all | solution.py:237
  154.4 26.3 %all-to-all-start = ((bf16[128,16,64]{0,2,1:T(8,128)(2,1)}), bf16[128,16,64]{0,2,1:T(8,128)(2,1)S(1)}, u32[]{:S(2)}, u32[]{:S(2)}) async-start(bf16[128,16,64]{0,2,1:T(8,128)(2,1)} %bitcast.2), calls=%async_computation | async-start | bytes 524288 | tf_op jit(solution)/shard_map/all_to_all | solution.py:235
  158.0 73.2 %all-gather.8.cloned.1.call-start = ((), (), s32[]{:S(2)}) async-start(), calls=%async_computation.19 | async-start | bytes 2359296 | tf_op jit(solution)/shard_map/all_gather | solution.py:41
  200.8 30.4 %all-to-all-start.3 = ((bf16[16,128,64]{1,2,0:T(8,128)(2,1)}), bf16[16,128,64]{1,2,0:T(8,128)(2,1)S(1)}, u32[]{:S(2)}, u32[]{:S(2)}) async-start(bf16[16,128,64]{1,2,0:T(8,128)(2,1)} %copy.99), calls=%async_computation.3 | async-start | bytes 524288 | tf_op jit(solution)/shard_map/all_to_all | solution.py:247
  204.3 115.2 %all-gather.10.cloned.1.call-start = ((), (), s32[]{:S(2)}) async-start(), calls=%async_computation.20 | async-start | bytes 4456448 | tf_op jit(solution)/shard_map/all_gather | solution.py:252
  234.8 84.7 %copy-start.12 = (bf16[256]{0:T(256)(128)(2,1)S(1)}, bf16[256]{0:T(256)(128)(2,1)}, u32[]{:S(2)}) copy-start(bf16[256]{0:T(256)(128)(2,1)} %param.30) | copy-start | bytes 1540
  234.8 89.5 %all-gather.12.cloned.1.call-start = ((), (), s32[]{:S(2)}) async-start(), calls=%async_computation.27 | async-start | bytes 4456448 | tf_op jit(solution)/shard_map/all_gather | solution.py:253
  274.7 49.5 %all-to-all-start.4 = ((bf16[16,256,64]{1,2,0:T(8,128)(2,1)}), bf16[16,256,64]{1,2,0:T(8,128)(2,1)S(1)}, u32[]{:S(2)}, u32[]{:S(2)}) async-start(bf16[16,256,64]{1,2,0:T(8,128)(2,1)} %bitcast.215), calls=%async_computation.4 | async-start | bytes 1048576 | tf_op jit(solution)/shard_map/all_to_all | solution.py:112
  278.8 150.3 %reduce-scatter.15.cloned.1.call-start = ((), (), s32[]{:S(2)}) async-start(), calls=%async_computation.22 | async-start | bytes 8912896 | tf_op jit(solution)/shard_map/reduce_scatter | solution.py:271
  335.1 166.9 %reduce-scatter.13.cloned.1.call-start = ((), (), s32[]{:S(2)}) async-start(), calls=%async_computation.21 | async-start | bytes 4456448 | tf_op jit(solution)/shard_map/reduce_scatter | solution.py:257
  341.2 162.8 %copy-start.2 = (bf16[1,128,1024]{2,1,0:T(8,128)(2,1)S(1)}, bf16[1,128,1024]{2,1,0:T(8,128)(2,1)}, u32[]{:S(2)}) copy-start(bf16[1,128,1024]{2,1,0:T(8,128)(2,1)} %param.33) | copy-start | bytes 786436
  341.2 282.3 %reduce-scatter.19.cloned.1.call-start = ((), (), s32[]{:S(2)}) async-start(), calls=%async_computation.24 | async-start | bytes 2359296 | tf_op jit(solution)/shard_map/reduce_scatter | solution.py:72
  506.2 150.3 %reduce-scatter.21.cloned.1.call-start = ((), (), s32[]{:S(2)}) async-start(), calls=%async_computation.25 | async-start | bytes 589824 | tf_op jit(solution)/shard_map/reduce_scatter | solution.py:91
  517.8 15.1 %all-to-all-start.9 = ((bf16[256,16,64]{0,2,1:T(8,128)(2,1)}), bf16[256,16,64]{0,2,1:T(8,128)(2,1)}, u32[]{:S(2)}, u32[]{:S(2)}) async-start(bf16[256,16,64]{0,2,1:T(8,128)(2,1)} %bitcast.270), calls=%async_computation.14 | async-start | bytes 1048576 | tf_op jit(solution)/shard_map/all_to_all | solution.py:274
  532.9 15.0 %all-to-all-start.5 = ((bf16[128,16,64]{0,2,1:T(8,128)(2,1)}), bf16[128,16,64]{0,2,1:T(8,128)(2,1)S(1)}, u32[]{:S(2)}, u32[]{:S(2)}) async-start(bf16[128,16,64]{0,2,1:T(8,128)(2,1)} %bitcast.17), calls=%async_computation.7 | async-start | bytes 524288 | tf_op jit(solution)/shard_map/all_to_all | solution.py:289
  536.5 193.4 %reduce-scatter.23.cloned.1.call-start = ((), (), s32[]{:S(2)}) async-start(), calls=%async_computation.26 | async-start | bytes 589824 | tf_op jit(solution)/shard_map/reduce_scatter | solution.py:94
  583.8 13.3 %all-to-all-start.6 = ((bf16[16,128,64]{1,2,0:T(8,128)(2,1)}), bf16[16,128,64]{1,2,0:T(8,128)(2,1)S(1)}, u32[]{:S(2)}, u32[]{:S(2)}) async-start(bf16[16,128,64]{1,2,0:T(8,128)(2,1)} %copy.104), calls=%async_computation.8 | async-start | bytes 524288 | tf_op jit(solution)/shard_map/all_to_all | solution.py:299
  597.1 11.2 %all-to-all-start.8 = ((bf16[16,128,64]{1,2,0:T(8,128)(2,1)}), bf16[16,128,64]{1,2,0:T(8,128)(2,1)S(1)}, u32[]{:S(2)}, u32[]{:S(2)}) async-start(bf16[16,128,64]{1,2,0:T(8,128)(2,1)} %copy.106), calls=%async_computation.10 | async-start | bytes 524288 | tf_op jit(solution)/shard_map/all_to_all | solution.py:301
  600.6 230.4 %reduce-scatter.17.cloned.1.call-start = ((), (), s32[]{:S(2)}) async-start(), calls=%async_computation.23 | async-start | bytes 7077888 | tf_op jit(solution)/shard_map/reduce_scatter | solution.py:69
  623.5 285.9 %reduce-scatter.27.cloned.1.call-start = ((), (), s32[]{:S(2)}) async-start(), calls=%async_computation.29 | async-start | bytes 278528
  625.4 328.5 %reduce-scatter.25.cloned.1.call-start = ((), (), s32[]{:S(2)}) async-start(), calls=%async_computation.28 | async-start | bytes 835584
  (10 other events, 146.5 us)
Sparse Core Ops, SparseCore 0:
  31.1 94.1 all-gather.5
  180.2 50.9 all-gather.7
  234.9 38.1 all-gather.9
  274.7 44.0 all-gather.11
  335.2 93.8 reduce-scatter.14
  431.3 70.5 reduce-scatter.12
  506.3 77.3 reduce-scatter.18
  587.2 69.2 reduce-scatter.20
  660.4 69.4 reduce-scatter.22
  733.6 97.4 reduce-scatter.16
  833.4 58.3 reduce-scatter.26
  894.2 59.5 reduce-scatter.24
where the time goes:
time: 973 us; the launch traced here: 963 us
  waiting for transfers between devices  497 us (51%)
  blocking collectives  254 us (26%)
  matrix products  79 us (8%)
  starting transfers between devices  45.8 us (5%)
  local copies, waits for them, and re-layouts  41.2 us (4%)
  other arithmetic  16 us (2%)
  between operations  15.7 us (2%)
  loops' own time  13.4 us (1%)
    reduce_scatter x1, waiting for transfers between devices, attn_grad_rows(): lax.psum_scatter(first.astype(jnp.bfloat16), 'fsdp', scatter_dimension=0,...  99.7 us
    reduce_scatter x1, waiting for transfers between devices, per_device(): lax.psum_scatter(tail_dot(grad_upper, up_part), 'seq', scatter_dimension=...  87.8 us
    reduce_scatter x1, waiting for transfers between devices, mlp_grad_rows(): lax.psum_scatter(second.astype(jnp.bfloat16), 'fsdp', scatter_dimension=0...  71.9 us
    reduce_scatter x1, waiting for transfers between devices, per_device(): lax.psum_scatter(plain_dot(activ, down_rows).astype(jnp.bfloat16), 'seq',...  71.5 us
    psum x1, blocking collectives, per_device(): lax.psum((grad_gain_one, grad_shift_one, jnp.sum(grad_query.astype(jnp.fl...  64.9 us
    unnamed x1, blocking collectives  53.9 us
    unnamed x14, waiting for transfers between devices  43.6 us
    all_gather x1, blocking collectives, mlp_rows(): lax.all_gather(first, 'fsdp', axis=0, tiled=True)  40.6 us
  transfers between devices with their start and end apart: 21, of which 13 were waited for; matrix products, arithmetic and copies ran while one was open for 11% of the time, Pallas kernels for 0%

commit v1 on v0

v1 whole, which is shorter than its diff:
```python
import functools

import jax
import jax.numpy as jnp
from jax import lax
from jax.experimental import pallas as pl
from jax.experimental.pallas import tpu as pltpu
from jax.sharding import PartitionSpec as P

H = 16
HD = 64
D = 1024
HID = 256
TOK = 128
NS = 16
NF = 8
PACK = 768
MESH = pl.DeviceIdType.MESH
F32 = jnp.float32
BF16 = jnp.bfloat16
MIB = 1024 * 1024


def dot(left, right, lc=1, rc=0):
    return lax.dot_general(left, right, (((lc,), (rc,)), ((), ())), preferred_element_type=F32)


def layer_norm(values, gain, shift):
    average = jnp.mean(values, axis=-1, keepdims=True)
    centered = values - average
    spread = jnp.mean(centered * centered, axis=-1, keepdims=True)
    return centered * lax.rsqrt(spread + 1e-05) * gain + shift


def remote(src, dst, send, recv, **where):
    return pltpu.make_async_remote_copy(
        src_ref=src, dst_ref=dst, send_sem=send, recv_sem=recv, device_id=where, device_id_type=MESH
    )


def places():
    me = lax.axis_index("seq")
    core = lax.rem(me, 2)
    return me, core, me + 1 - 2 * core, lax.axis_index("fsdp")


def barrier_seq_all(me):
    sem = pltpu.get_barrier_semaphore()

    def body(k, carry):
        pl.semaphore_signal(sem, inc=1, device_id={"seq": lax.rem(me + k, NS)}, device_id_type=MESH)
        return carry

    lax.fori_loop(1, NS, body, 0)
    return sem


def barrier_fsdp(sem, row):
    def body(k, carry):
        pl.semaphore_signal(sem, inc=1, device_id={"fsdp": lax.rem(row + k, NF)}, device_id_type=MESH)
        return carry

    lax.fori_loop(1, NF, body, 0)


def loop(low, high, body):
    def step(k, carry):
        body(k)
        return carry

    lax.fori_loop(low, high, step, 0)


class Gather:
    def __init__(self, own, out, send, recv, hop):
        self.own, self.out, self.send, self.recv, self.hop = own, out, send, recv, hop
        self.me, self.core, self.sib, _ = places()

    def far(self, k):
        return lax.rem(self.me + 2 * k, NS)

    def start(self):
        me = self.me
        remote(self.own, self.out.at[me], self.send.at[0], self.recv.at[me], seq=self.sib).start()

        def body(k):
            remote(self.own, self.out.at[me], self.send.at[k], self.recv.at[me], seq=self.far(k)).start()

        loop(1, NF, body)

    def arrive(self, block):
        remote(self.out.at[block], self.out.at[block], self.send.at[0], self.recv.at[block], seq=self.sib).wait_recv()

    def relay(self, k):
        block = self.far(k)
        self.arrive(block)
        remote(self.out.at[block], self.out.at[block], self.hop.at[k], self.recv.at[block], seq=self.sib).start()

    def near(self, k):
        self.arrive(lax.rem(self.sib + 2 * k, NS))

    def drain(self):
        def body(k):
            remote(self.own, self.out.at[self.me], self.send.at[k], self.recv.at[self.me], seq=self.sib).wait_send()

        loop(0, NF, body)

        def hops(k):
            block = self.far(k)
            remote(self.out.at[block], self.out.at[block], self.hop.at[k], self.recv.at[block], seq=self.sib).wait_send()

        loop(1, NF, hops)


class Reduce:
    def __init__(self, part, pair, total, got, hop, hoprecv, send, recv):
        self.part, self.pair, self.total, self.got = part, pair, total, got
        self.hop, self.hoprecv, self.send, self.recv = hop, hoprecv, send, recv
        self.me, self.core, self.sib, _ = places()

    def put(self, k, values):
        self.part[pl.ds(2 * k, 2)] = values.astype(BF16).reshape(2, TOK, D)
        self.first(k).start()

    def first(self, k):
        return remote(
            self.part.at[2 * k + 1 - self.core], self.pair.at[k], self.hop.at[k], self.hoprecv.at[k], seq=self.sib
        )

    def second(self, k):
        return remote(
            self.total.at[k], self.got.at[k], self.send.at[k], self.recv.at[k], seq=lax.rem(self.me + 2 * k, NS)
        )

    def merge(self, k):
        self.first(k).wait_recv()
        both = self.part[2 * k + self.core].astype(F32) + self.pair[k].astype(F32)
        self.total[k] = both.astype(BF16)

        @pl.when(k > 0)
        def _():
            self.second(k).start()

    def finish(self, out):
        out[...] = self.total[0].astype(F32)

        def body(k):
            self.second(k).wait_recv()
            out[...] += self.got[k].astype(F32)

        loop(1, NF, body)

    def drain(self):
        loop(0, NF, lambda k: self.first(k).wait_send())
        loop(1, NF, lambda k: self.second(k).wait_send())


def key_extras(rows):
    lane = lax.broadcasted_iota(jnp.int32, (rows, HD), 1)
    pos = lax.broadcasted_iota(jnp.int32, (rows, HD), 0)
    high = (pos // 256) * 256
    value = jnp.where(lane < 3, high, jnp.where(lane < 6, pos - high, 0))
    return value.astype(F32).astype(BF16)


def query_extras(slope_ref):
    return jnp.broadcast_to(slope_ref[...], (HD, 256))


def kernel_a(
    hid_ref, cot_ref, pack_ref, sml_ref, qvb_ref, slope_ref,
    nrm, cota, qkvt, qkvr, lse, mid, n2, ctxr, wq, up, dn, pj, sm,
    hid, wf, smb, wqo, dno, pjo, kr, ctxo, ctxt,
    h_s, h_r, h_h, c_s, c_r, c_h, p_s, p_r, p_h, w_s, w_r, m_s, m_r, q_s, q_r, d_s, d_r, x_s, x_r, l_s,
):
    me, core, sib, row = places()
    sem = barrier_seq_all(me)
    barrier_fsdp(sem, row)
    pl.semaphore_wait(sem, NS - 1 + NF - 1)

    def to_row(k):
        return remote(pack_ref, wf.at[row], w_s.at[k], w_r.at[row], fsdp=lax.rem(row + k, NF))

    def small_to(k):
        return remote(sml_ref, smb.at[me], m_s.at[k], m_r.at[me], seq=lax.rem(me + k, NS))

    loop(1, NF, lambda k: to_row(k).start())
    loop(1, NS, lambda k: small_to(k).start())
    hidden = Gather(hid_ref, hid, h_s, h_r, h_h)
    hidden.start()
    cot_own = pltpu.make_async_copy(cot_ref, cota.at[me], l_s)
    cot_own.start()
    wf[row] = pack_ref[...]
    smb[me] = sml_ref[...]
    hid[me] = hid_ref[...]
    kr[:, HD:] = key_extras(NS * TOK)

    def from_row(k):
        other = lax.rem(row + k, NF)
        remote(pack_ref, wf.at[other], w_s.at[k], w_r.at[other], fsdp=other).wait_recv()

    loop(1, NF, from_row)
    for f in range(NF):
        lanes = slice(f * 128, f * 128 + 128)
        wqo[:, lanes] = wf[f, 0:192, :]
        pjo[:, lanes] = wf[f, 192:256, :]
        up[lanes, 0:128] = wf[f, 512:640, :]
        up[lanes, 128:256] = wf[f, 640:768, :]
        for half in range(2):
            for piece in range(2):
                at = 256 + (2 * half + piece) * 64
                dno[2 * f + half, :, piece * 128 : piece * 128 + 128] = wf[f, at : at + 64, :]

    def q_block(j):
        block = 3 * me + j
        kind, head = block // H, lax.rem(block, H)
        src = wqo.at[pl.ds(j * HD, HD), :]
        dst = wq.at[pl.ds(pl.multiple_of(kind * HD, HD), HD), :]
        return head, kind, src, dst

    for j in range(3):
        head, kind, src, dst = q_block(j)

        @pl.when(head != me)
        def _():
            remote(src, dst, q_s.at[j], q_r.at[kind], seq=head).start()

        @pl.when(head == me)
        def _():
            dst[...] = src[...]

    def down_to(k):
        other = lax.rem(me + k, NS)
        return remote(
            dno.at[other], dn.at[pl.ds(pl.multiple_of(me * HD, HD), HD), :], d_s.at[k], d_r.at[me], seq=other
        )

    def down_from(k):
        other = lax.rem(me + k, NS)
        remote(
            dno.at[me], dn.at[pl.ds(pl.multiple_of(other * HD, HD), HD), :], d_s.at[k], d_r.at[other], seq=other
        ).wait_recv()

    loop(1, NS, lambda k: down_to(k).start())
    dn[pl.ds(pl.multiple_of(me * HD, HD), HD), :] = dno[me]
    proj = Gather(pjo, pj, p_s, p_r, p_h)
    proj.start()
    pj[me] = pjo[...]

    def small_from(k):
        other = lax.rem(me + k, NS)
        remote(sml_ref, smb.at[other], m_s.at[k], m_r.at[other], seq=other).wait_recv()

    loop(1, NS, small_from)
    for t in range(NF):
        sm[:, t * 128 : t * 128 + 128] = smb[2 * t].astype(F32) + smb[2 * t + 1].astype(F32)

    for kind in range(3):

        @pl.when((kind * H + me) // 3 != me)
        def _():
            remote(
                wqo.at[pl.ds(0, HD), :], wq.at[pl.ds(kind * HD, HD), :], q_s.at[0], q_r.at[kind], seq=sib
            ).wait_recv()

    def norm_and_project(k):
        @pl.when(k > 0)
        def _():
            hidden.relay(k)

        hidden.near(k)
        m = lax.rem(me // 2 + k, NF)
        values = hid[pl.ds(2 * m, 2)].reshape(2 * TOK, D).astype(F32)
        normed = layer_norm(values, sm[0:1, :], sm[1:2, :]).astype(BF16)
        nrm[pl.ds(2 * m, 2)] = normed.reshape(2, TOK, D)
        block = dot(wq[...], normed, 1, 1) + qvb_ref[:, 0:1]
        qkvt[m] = block.astype(BF16)
        at = pl.ds(pl.multiple_of(m * 256, 256), 256)
        qkvr[0, at, :] = block[0:64].T.astype(BF16)
        keys = block[64:128].T.astype(BF16)
        qkvr[1, at, :] = keys
        kr[at, 0:HD] = keys
        qkvr[2, at, :] = block[128:192].T.astype(BF16)

    loop(0, NF, norm_and_project)
    cot = Gather(cot_ref, cota, c_s, c_r, c_h)
    cot.start()

    extras = query_extras(slope_ref)

    def ctx_to(j):
        return remote(ctxo.at[j], ctxt.at[me], x_s.at[j], x_r.at[me], seq=j)

    for j in range(NF):
        n = (j + 1) * 256
        queries = jnp.concatenate([(qkvt[j, 0:64, :].astype(F32) * 0.125).astype(BF16), extras], axis=0)
        scores = dot(kr[0:n, :], queries)
        kpos = lax.broadcasted_iota(jnp.int32, (256, 256), 0)
        qpos = lax.broadcasted_iota(jnp.int32, (256, 256), 1)
        last = jnp.where(kpos <= qpos, scores[n - 256 :], -1e30)
        scores = last if j == 0 else jnp.concatenate([scores[: n - 256], last], axis=0)
        peak = jnp.max(scores, axis=0, keepdims=True)
        expo = jnp.exp(scores - peak)
        total = jnp.sum(expo, axis=0, keepdims=True)
        lse[j : j + 1, :] = peak + jnp.log(total)
        weights = expo.astype(BF16)
        acc = dot(qkvt[0, 128:192, :], weights[0:256])
        for i in range(1, j + 1):
            acc += dot(qkvt[i, 128:192, :], weights[i * 256 : i * 256 + 256])
        context = (acc / total).astype(BF16)
        for half in range(2):
            target = 2 * j + half
            ctxo[target] = context[:, half * 128 : half * 128 + 128]

            @pl.when(me != target)
            def _():
                ctx_to(target).start()

            @pl.when(me == target)
            def _():
                ctxt[target] = ctxo[target]

    loop(1, NF, proj.relay)
    loop(0, NF, proj.near)

    def ctx_from(k):
        other = lax.rem(me + k, NS)
        remote(ctxo.at[other], ctxt.at[other], x_s.at[other], x_r.at[other], seq=other).wait_recv()

    loop(1, NS, ctx_from)
    context = ctxt[...].reshape(D, TOK).astype(F32).T.astype(BF16)
    ctxr[...] = context
    middle = hid_ref[...].astype(F32) + dot(context, pj[...].reshape(D, D), 1, 1) + sm[2:3, :]
    mid[...] = middle
    n2[...] = layer_norm(middle, sm[3:4, :], sm[4:5, :]).astype(BF16)

    loop(1, NS, down_from)
    loop(1, NF, cot.relay)
    loop(0, NF, cot.near)
    cot_own.wait()
    hidden.drain()
    cot.drain()
    proj.drain()
    loop(1, NF, lambda k: to_row(k).wait_send())
    loop(1, NS, lambda k: small_to(k).wait_send())
    loop(1, NS, lambda k: down_to(k).wait_send())
    for j in range(3):
        head, kind, src, dst = q_block(j)

        @pl.when(head != me)
        def _():
            remote(src, dst, q_s.at[j], q_r.at[kind], seq=head).wait_send()

    def ctx_sent(k):
        other = lax.rem(me + k, NS)
        remote(ctxo.at[other], ctxt.at[me], x_s.at[other], x_r.at[me], seq=other).wait_send()

    loop(1, NS, ctx_sent)


def vm():
    return pl.BlockSpec(memory_space=pltpu.VMEM)


def hbm():
    return pl.BlockSpec(memory_space=pl.ANY)


def sems(*counts):
    return [pltpu.SemaphoreType.DMA((n,)) for n in counts]


def params(number):
    return pltpu.CompilerParams(collective_id=number, has_side_effects=True, vmem_limit_bytes=56 * MIB)


def run_a(hid, cot, pack, small, qvb, slope):
    shapes = [
        ((NS, TOK, D), BF16), ((NS, TOK, D), BF16), ((NF, 192, 256), BF16), ((3, NS * TOK, HD), BF16),
        ((NF, 256), F32), ((TOK, D), F32), ((TOK, D), BF16), ((TOK, D), BF16), ((192, D), BF16),
        ((D, HID), BF16), ((D, HID), BF16), ((NS, HD, D), BF16), ((16, D), F32),
    ]
    specs = [vm() for _ in shapes]
    specs[1] = hbm()
    return pl.pallas_call(
        kernel_a,
        out_shape=[jax.ShapeDtypeStruct(*s) for s in shapes],
        in_specs=[vm(), hbm(), vm(), vm(), vm(), vm()],
        out_specs=specs,
        scratch_shapes=[
            pltpu.VMEM((NS, TOK, D), BF16),
            pltpu.VMEM((NF, PACK, 128), BF16),
            pltpu.VMEM((NS, 16, 128), BF16),
            pltpu.VMEM((192, D), BF16),
            pltpu.VMEM((NS, HD, HID), BF16),
            pltpu.VMEM((HD, D), BF16),
            pltpu.VMEM((NS * TOK, 128), BF16),
            pltpu.VMEM((NS, HD, TOK), BF16),
            pltpu.VMEM((NS, HD, TOK), BF16),
        ]
        + sems(8, 16, 8, 8, 16, 8, 8, 16, 8, 8, 8, 16, 16, 3, 3, 16, 16, 16, 16)
        + [pltpu.SemaphoreType.DMA],
        compiler_params=params(0),
        name="gather_attend",
    )(hid, cot, pack, small, qvb, slope)


def kernel_m(
    n2_ref, cot_ref, up_ref, dn_ref, ub_ref,
    gn2, dsum, gup, gdn, gub,
    xa, act, gu, g_part, g_pair, g_total, g_got, d_part, d_pair, d_total, d_got,
    n_s, n_r, n_h, g1s, g1r, g2s, g2r, d1s, d1r, d2s, d2r,
):
    me, core, sib, _ = places()
    sem = pltpu.get_barrier_semaphore()
    pl.semaphore_signal(sem, inc=1, device_id={"seq": sib}, device_id_type=MESH)

    def greet(k):
        pl.semaphore_signal(sem, inc=1, device_id={"seq": lax.rem(me + 2 * k, NS)}, device_id_type=MESH)

    loop(1, NF, greet)
    pl.semaphore_wait(sem, NF)
    tokens = Gather(n2_ref, xa, n_s, n_r, n_h)
    tokens.start()
    xa[me] = n2_ref[...]
    grads = Reduce(g_part, g_pair, g_total, g_got, g1s, g1r, g2s, g2r)
    downs = Reduce(d_part, d_pair, d_total, d_got, d1s, d1r, d2s, d2r)
    gub[...] = jnp.zeros_like(gub)

    def step(k):
        @pl.when(k > 0)
        def _():
            tokens.relay(k)

        tokens.near(k)
        m = lax.rem(me // 2 + k, NF)
        rows = xa[pl.ds(2 * m, 2)].reshape(2 * TOK, D)
        upper = dot(rows, up_ref[...]) + ub_ref[...]
        square = upper * upper
        bend = jnp.tanh(0.7978845608 * upper * (1.0 + 0.044715 * square))
        half = 0.5 * (1.0 + bend)
        active = (upper * half).astype(BF16)
        slope = half + 0.5 * upper * (1.0 - bend * bend) * (0.7978845608 * (1.0 + 0.134145 * square))
        cots = cot_ref[pl.ds(2 * m, 2)].reshape(2 * TOK, D)
        grad = (dot(cots, dn_ref[...]) * slope).astype(BF16)
        at = pl.ds(pl.multiple_of(m * 256, 256), 256)
        act[at, :] = active
        gu[at, :] = grad
        gub[0:1, :] += jnp.sum(grad.astype(F32), axis=0, keepdims=True)
        grads.put(k, dot(grad, up_ref[...], 1, 1))
        downs.put(k, dot(active, dn_ref[...], 1, 1))

        @pl.when(k > 0)
        def _():
            grads.merge(k - 1)
            downs.merge(k - 1)

    loop(0, NF, step)
    grads.merge(NF - 1)
    downs.merge(NF - 1)
    gup[...] = dot(xa[...].reshape(NS * TOK, D), gu[...], 0, 0).astype(BF16)
    gdn[...] = dot(cot_ref[...].reshape(NS * TOK, D), act[...], 0, 0).astype(BF16)
    grads.finish(gn2)
    downs.finish(dsum)
    tokens.drain()
    grads.drain()
    downs.drain()


def reduce_scratch():
    return [
        pltpu.VMEM((NS, TOK, D), BF16),
        pltpu.VMEM((NF, TOK, D), BF16),
        pltpu.VMEM((NF, TOK, D), BF16),
        pltpu.VMEM((NF, TOK, D), BF16),
    ]


def run_m(n2, cot, up, dn, ub):
    shapes = [((TOK, D), F32), ((TOK, D), F32), ((D, HID), BF16), ((D, HID), BF16), ((8, HID), F32)]
    return pl.pallas_call(
        kernel_m,
        out_shape=[jax.ShapeDtypeStruct(*s) for s in shapes],
        in_specs=[vm()] * 5,
        out_specs=[vm()] * 5,
        scratch_shapes=[
            pltpu.VMEM((NS, TOK, D), BF16),
            pltpu.VMEM((NS * TOK, HID), BF16),
            pltpu.VMEM((NS * TOK, HID), BF16),
        ]
        + reduce_scratch()
        + reduce_scratch()
        + sems(8, 16, 8, 8, 8, 8, 8, 8, 8, 8, 8),
        compiler_params=params(1),
        name="feed_forward",
    )(n2, cot, up, dn, ub)


def kernel_b(
    gc_ref, qkvt, qkvr, lse, wq, nrm, slope_ref,
    gn1, gqkv, gsum,
    dct, gjt, kr, dk, dv, part, pair, total, got,
    x_s, x_r, r1s, r1r, r2s, r2r,
):
    me, core, sib, _ = places()
    sem = barrier_seq_all(me)
    pl.semaphore_wait(sem, NS - 1)

    def ctx_to(k):
        other = lax.rem(me + k, NS)
        return remote(gc_ref.at[other], dct.at[me], x_s.at[k], x_r.at[me], seq=other)

    def ctx_from(k):
        other = lax.rem(me + k, NS)
        remote(gc_ref.at[me], dct.at[other], x_s.at[k], x_r.at[other], seq=other).wait_recv()

    loop(1, NS, lambda k: ctx_to(k).start())
    dct[me] = gc_ref[me]
    kr[:, HD:] = key_extras(NS * TOK)
    kr[:, 0:HD] = qkvr[1]
    dk[...] = jnp.zeros_like(dk)
    dv[...] = jnp.zeros_like(dv)
    extras = query_extras(slope_ref)
    loop(1, NS, ctx_from)
    for j in range(NF):
        n = (j + 1) * 256
        at = slice(j * 256, n)
        queries = jnp.concatenate([(qkvt[j, 0:64, :].astype(F32) * 0.125).astype(BF16), extras], axis=0)
        scores = dot(kr[0:n, :], queries)
        probs = jnp.exp(scores - lse[j : j + 1, :])
        kpos = lax.broadcasted_iota(jnp.int32, (256, 256), 0)
        qpos = lax.broadcasted_iota(jnp.int32, (256, 256), 1)
        last = jnp.where(kpos <= qpos, probs[n - 256 :], 0.0)
        probs = last if j == 0 else jnp.concatenate([probs[: n - 256], last], axis=0)
        gctx = jnp.concatenate([dct[2 * j], dct[2 * j + 1]], axis=1)
        gprobs = dot(qkvr[2, 0:n, :], gctx)
        inner = jnp.sum(probs * gprobs, axis=0, keepdims=True)
        gscores = (probs * (gprobs - inner) * 0.125).astype(BF16)
        gq = dot(qkvt[0, 64:128, :], gscores[0:256])
        for i in range(1, j + 1):
            gq += dot(qkvt[i, 64:128, :], gscores[i * 256 : i * 256 + 256])
        gjt[j, 0:64, :] = gq.astype(BF16)
        dk[0:n, :] += dot(gscores, qkvr[0, at, :])
        dv[0:n, :] += dot(probs.astype(BF16), gctx.astype(F32).T.astype(BF16))
    for j in range(NF):
        at = slice(j * 256, j * 256 + 256)
        gjt[j, 64:128, :] = dk[at, :].T.astype(BF16)
        gjt[j, 128:192, :] = dv[at, :].T.astype(BF16)

    norms = Reduce(part, pair, total, got, r1s, r1r, r2s, r2r)

    def step(k):
        m = lax.rem(me // 2 + k, NF)
        rows = gjt[m].astype(F32).T.astype(BF16)
        norms.put(k, dot(rows, wq[...]))

        @pl.when(k > 0)
        def _():
            norms.merge(k - 1)

    loop(0, NF, step)
    norms.merge(NF - 1)
    acc = jnp.zeros((192, D), F32)
    sums = jnp.zeros((192, 1), F32)
    for j in range(NF):
        acc += dot(gjt[j], nrm[2 * j : 2 * j + 2].reshape(2 * TOK, D))
        sums += jnp.sum(gjt[j].astype(F32), axis=1, keepdims=True)
    gqkv[...] = acc.astype(BF16)
    gsum[...] = jnp.broadcast_to(sums, (192, 128))
    norms.finish(gn1)
    norms.drain()
    loop(1, NS, lambda k: ctx_to(k).wait_send())


def run_b(gc, qkvt, qkvr, lse, wq, nrm, slope):
    shapes = [((TOK, D), F32), ((192, D), BF16), ((192, 128), F32)]
    return pl.pallas_call(
        kernel_b,
        out_shape=[jax.ShapeDtypeStruct(*s) for s in shapes],
        in_specs=[vm()] * 7,
        out_specs=[vm()] * 3,
        scratch_shapes=[
            pltpu.VMEM((NS, HD, TOK), BF16),
            pltpu.VMEM((NF, 192, 256), BF16),
            pltpu.VMEM((NS * TOK, 128), BF16),
            pltpu.VMEM((NS * TOK, HD), F32),
            pltpu.VMEM((NS * TOK, HD), F32),
        ]
        + reduce_scratch()
        + sems(16, 16, 8, 8, 8, 8),
        compiler_params=params(2),
        name="attend_back",
    )(gc, qkvt, qkvr, lse, wq, nrm, slope)


def kernel_c(
    gdn, gup, gqkv, gpj, token_ref, local_ref,
    out, small,
    d1, j1, q1, m1, pack, got, m2, sgot,
    d_s, d_r, j_s, j_r, q_s, q_r, m_s, m_r, w_s, w_r, v_s, v_r,
):
    me, core, sib, row = places()
    sem = barrier_seq_all(me)
    barrier_fsdp(sem, row)
    pl.semaphore_wait(sem, NS - 1 + NF - 1)

    def block(other):
        return pl.ds(pl.multiple_of(other * HD, HD), HD)

    def down(k):
        other = lax.rem(me + k, NS)
        return remote(gdn.at[block(other), :], d1.at[me], d_s.at[k], d_r.at[me], seq=other)

    def proj(k):
        other = lax.rem(me + k, NS)
        return remote(gpj.at[block(other), :], j1.at[me], j_s.at[k], j_r.at[me], seq=other)

    def tokens(k):
        other = lax.rem(me + k, NS)
        return remote(token_ref.at[other // 2], m1.at[me], m_s.at[k], m_r.at[me], seq=other)

    def q_block(kind):
        index = kind * H + me
        holder, slot = index // 3, lax.rem(index, 3)
        src = gqkv.at[pl.ds(kind * HD, HD), :]
        dst = q1.at[block(slot), :]
        return holder, slot, src, dst

    for kind in range(3):
        holder, slot, src, dst = q_block(kind)

        @pl.when(holder != me)
        def _():
            remote(src, dst, q_s.at[kind], q_r.at[slot], seq=holder).start()

        @pl.when(holder == me)
        def _():
            dst[...] = src[...]

    def send(k):
        tokens(k).start()
        down(k).start()
        proj(k).start()

    loop(1, NS, send)
    d1[me] = gdn[block(me), :]
    j1[me] = gpj[block(me), :]
    m1[me] = token_ref[me // 2]

    def receive(k):
        other = lax.rem(me + k, NS)
        remote(token_ref.at[0], m1.at[other], m_s.at[k], m_r.at[other], seq=other).wait_recv()
        remote(gdn.at[block(me), :], d1.at[other], d_s.at[k], d_r.at[other], seq=other).wait_recv()
        remote(gpj.at[block(me), :], j1.at[other], j_s.at[k], j_r.at[other], seq=other).wait_recv()

    loop(1, NS, receive)
    for slot in range(3):

        @pl.when(lax.rem(3 * me + slot, H) != me)
        def _():
            remote(
                gqkv.at[pl.ds(0, HD), :], q1.at[pl.ds(slot * HD, HD), :], q_s.at[0], q_r.at[slot], seq=sib
            ).wait_recv()

    projs = j1[0].astype(F32)
    local = m1[0]
    for p in range(1, NS):
        projs += j1[p].astype(F32)
        local += m1[p]
    m2[0:8, :] = local
    m2[8:16, :] = local_ref[...]
    for f in range(NF):
        lanes = slice(f * 128, f * 128 + 128)
        pack[f, 0:192, :] = q1[:, lanes]
        pack[f, 192:256, :] = projs[:, lanes].astype(BF16)
        for half in range(2):
            for piece in range(2):
                at = 256 + (2 * half + piece) * 64
                pack[f, at : at + 64, :] = d1[2 * f + half, :, piece * 128 : piece * 128 + 128]
        pack[f, 512:640, :] = gup[lanes, 0:128]
        pack[f, 640:768, :] = gup[lanes, 128:256]

    def rows(k):
        other = lax.rem(row + k, NF)
        return remote(pack.at[other], got.at[row], w_s.at[k], w_r.at[row], fsdp=other)

    def vectors(k):
        other = lax.rem(row + k, NF)
        return remote(m2, sgot.at[row], v_s.at[k], v_r.at[row], fsdp=other)

    def send_rows(k):
        vectors(k).start()
        rows(k).start()

    loop(1, NF, send_rows)
    got[row] = pack[row]
    sgot[row] = m2[...]

    def receive_rows(k):
        other = lax.rem(row + k, NF)
        remote(m2, sgot.at[other], v_s.at[k], v_r.at[other], fsdp=other).wait_recv()
        remote(pack.at[other], got.at[other], w_s.at[k], w_r.at[other], fsdp=other).wait_recv()

    loop(1, NF, receive_rows)
    total = got[0].astype(F32)
    vector = sgot[0]
    for f in range(1, NF):
        total += got[f].astype(F32)
        vector += sgot[f]
    out[...] = total
    small[...] = vector

    def sent(k):
        tokens(k).wait_send()
        down(k).wait_send()
        proj(k).wait_send()

    loop(1, NS, sent)

    def rows_sent(k):
        vectors(k).wait_send()
        rows(k).wait_send()

    loop(1, NF, rows_sent)
    for kind in range(3):
        holder, slot, src, dst = q_block(kind)

        @pl.when(holder != me)
        def _():
            remote(src, dst, q_s.at[kind], q_r.at[slot], seq=holder).wait_send()


def run_c(gdn, gup, gqkv, gpj, token, local):
    shapes = [((PACK, 128), F32), ((16, 128), F32)]
    return pl.pallas_call(
        kernel_c,
        out_shape=[jax.ShapeDtypeStruct(*s) for s in shapes],
        in_specs=[vm()] * 6,
        out_specs=[vm()] * 2,
        scratch_shapes=[
            pltpu.VMEM((NS, HD, HID), BF16),
            pltpu.VMEM((NS, HD, D), BF16),
            pltpu.VMEM((192, D), BF16),
            pltpu.VMEM((NS, 8, 128), F32),
            pltpu.VMEM((NF, PACK, 128), BF16),
            pltpu.VMEM((NF, PACK, 128), BF16),
            pltpu.VMEM((16, 128), F32),
            pltpu.VMEM((NF, 16, 128), F32),
        ]
        + sems(16, 16, 16, 16, 3, 3, 16, 16, 8, 8, 8, 8),
        compiler_params=params(3),
        name="sum_weights",
    )(gdn, gup, gqkv, gpj, token, local)


def per_device(
    hidden_in, norm1_gain, norm1_shift, qkv_weight, query_bias, value_bias, proj_weight, proj_bias,
    norm2_gain, norm2_shift, up_weight, up_bias, down_weight, down_bias, out_cotangent,
):
    hid, cot = hidden_in[0], out_cotangent[0]
    me = lax.axis_index("seq")
    even = lax.rem(me, 2) == 0
    down_t = down_weight.T.reshape(HD, 4, 128).transpose(1, 0, 2).reshape(256, 128)
    up_r = up_weight.reshape(128, 2, 128).transpose(1, 0, 2).reshape(256, 128)
    pack = jnp.concatenate([qkv_weight.T, proj_weight.T, down_t, up_r], axis=0)
    vectors = jnp.stack([norm1_gain, norm1_shift, proj_bias, norm2_gain, norm2_shift, down_bias])
    none = jnp.zeros_like(vectors)
    vectors = jnp.concatenate([jnp.where(even, vectors, none), jnp.where(even, none, vectors)], axis=1)
    small = jnp.pad(vectors, ((0, 10), (0, 0)))
    qvb = jnp.concatenate([query_bias, jnp.zeros_like(query_bias), value_bias]).astype(F32)
    qvb = jnp.broadcast_to(qvb[:, None], (192, 128))
    slope = jnp.exp2(-8.0 * (me.astype(F32) + 1.0) / H)
    first = lax.reduce_precision(slope, 8, 7)
    second = lax.reduce_precision(slope - first, 8, 7)
    third = lax.reduce_precision(slope - first - second, 8, 7)
    parts = jnp.stack([first, second, third, first, second, third])
    slopes = jnp.pad(parts, (0, HD - 6)).astype(BF16)
    slopes = jnp.broadcast_to(slopes[:, None], (HD, 256))

    (nrm, cota, qkvt, qkvr, lse, middle, n2, ctx, wq, up, dn, pj, sm) = run_a(hid, cot, pack, small, qvb, slopes)
    gn2, down_sum, gup, gdn, gub = run_m(n2, cota, up, dn, up_bias.astype(F32)[None])
    layer_out = middle + down_sum + sm[5]

    pull = jax.vjp(layer_norm, middle, sm[3], sm[4])[1]
    grad_mid_norm, grad_gain_two, grad_shift_two = pull(gn2)
    cot32 = cot.astype(F32)
    grad_middle = cot32 + grad_mid_norm
    branch = grad_middle.astype(BF16)
    projection = pj.reshape(D, D)
    gpj = dot(branch, ctx, 0, 0).astype(BF16)
    gctx = dot(projection, branch, 0, 1).astype(BF16).reshape(NS, HD, TOK)
    gn1, gqkv, gsum = run_b(gctx, qkvt, qkvr, lse, wq, nrm, slopes)
    pull = jax.vjp(layer_norm, hid.astype(F32), sm[0], sm[1])[1]
    grad_in_norm, grad_gain_one, grad_shift_one = pull(gn1)
    input_grad = grad_middle + grad_in_norm

    nothing = jnp.zeros((D,), F32)
    token = jnp.stack(
        [
            grad_gain_one, grad_shift_one, jnp.sum(branch.astype(F32), axis=0), grad_gain_two, grad_shift_two,
            jnp.sum(cot32, axis=0), nothing, nothing,
        ]
    )
    token = token.reshape(8, 8, 128).transpose(1, 0, 2)
    head = jnp.concatenate([gsum[0:64, 0], gsum[128:192, 0]])[None]
    local = jnp.concatenate([head, gub[0].reshape(2, 128), jnp.zeros((5, 128), F32)], axis=0)
    out, vecs = run_c(gdn, gup, gqkv, gpj, token, local)
    mine = jnp.where(even, vecs[:6, :64], vecs[:6, 64:])
    return (
        layer_out.astype(BF16)[None],
        input_grad.astype(BF16)[None],
        mine[0],
        mine[1],
        out[0:192].T,
        vecs[8, :64],
        vecs[8, 64:],
        out[192:256].T,
        mine[2],
        mine[3],
        mine[4],
        out[512:768].reshape(2, 128, 128).transpose(1, 0, 2).reshape(128, 256),
        vecs[9:11].reshape(256),
        out[256:512].reshape(4, HD, 128).transpose(0, 2, 1).reshape(512, HD),
        mine[5],
    )


def solution(mesh):
    act, vec, mat = P("fsdp", "seq", None), P("seq"), P("fsdp", "seq")
    return jax.shard_map(
        per_device,
        mesh=mesh,
        in_specs=(act, vec, vec, mat, vec, vec, mat, vec, vec, vec, mat, vec, mat, vec, act),
        out_specs=(act, act, vec, vec, mat, vec, vec, mat, vec, vec, vec, mat, vec, mat, vec),
        check_vma=False,
    )
```

time: 973 us -> 408 us (0.42)
  waiting for transfers between devices: 497 us -> 0 us
  Pallas kernels: 0 us -> 364 us
  blocking collectives: 254 us -> 0 us
  matrix products: 79 us -> 3.55 us
  starting transfers between devices: 45.8 us -> 0 us
  local copies, waits for them, and re-layouts: 41.2 us -> 16.6 us
  loops' own time: 13.4 us -> 0 us
  between operations: 15.7 us -> 5.01 us
    pallas_call x0 -> x4, Pallas kernels: none -> 364 us  [the longest x1 124 us: run_a(): pl.pallas_call(kernel_a, out_shape=[jax.ShapeDtypeStruct(*s) for s in sha...]
    reduce_scatter x6 -> x0, waiting for transfers between devices: 362 us -> none  [the longest x1 99.7 us: attn_grad_rows(): lax.psum_scatter(first.astype(jnp.bfloat16), 'fsdp', scatter_dimension=0,...]
    all_gather x4 -> x0, blocking collectives: 125 us -> none  [the longest x1 40.6 us: mlp_rows(): lax.all_gather(first, 'fsdp', axis=0, tiled=True)]
    dot_general x40 -> x2, matrix products: 79 us -> 3.55 us  [dot(): lax.dot_general(left, right, (((lc,), (rc,)), ((), ())), preferred_elemen...]
    psum x1 -> x0, blocking collectives: 64.9 us -> none  [per_device(): lax.psum((grad_gain_one, grad_shift_one, jnp.sum(grad_query.astype(jnp.fl...]
    all_gather x4 -> x0, waiting for transfers between devices: 57.2 us -> none  [the longest x1 30.4 us: attn_rows(): lax.all_gather(first, 'fsdp', axis=0, tiled=True)]
    unnamed x1 -> x0, blocking collectives: 53.9 us -> none
    unnamed x14 -> x0, waiting for transfers between devices: 43.6 us -> none
  transfers between devices with their start and end apart: 21 -> 0, of which waited for: 13 -> 0; matrix products, arithmetic and copies ran while one was open for 11% -> 0% of each run, Pallas kernels for 0% -> 0%
where the time goes in v1:
time: 408 us; the launch traced here: 402 us
  Pallas kernels  364 us (89%)
  local copies, waits for them, and re-layouts  16.6 us (4%)
  other arithmetic  13.4 us (3%)
  between operations  5.01 us (1%)
    pallas_call x1, Pallas kernels, run_a(): pl.pallas_call(kernel_a, out_shape=[jax.ShapeDtypeStruct(*s) for s in sha...  124 us
    pallas_call x1, Pallas kernels, run_m(): pl.pallas_call(kernel_m, out_shape=[jax.ShapeDtypeStruct(*s) for s in sha...  98.7 us
    pallas_call x1, Pallas kernels, run_c(): pl.pallas_call(kernel_c, out_shape=[jax.ShapeDtypeStruct(*s) for s in sha...  73.5 us
    pallas_call x1, Pallas kernels, run_b(): pl.pallas_call(kernel_b, out_shape=[jax.ShapeDtypeStruct(*s) for s in sha...  67.9 us

profile of v1, /device:TPU:0, one launch (start us, length us, event | category | flops | bytes accessed | tf_op | source)
XLA Modules:
  0.0 402.2 jit_solution(7771947727178875581)
XLA Ops:
  0.7 0.8 copy-done
  1.5 0.9 copy_bitcast_fusion.3
  2.4 1.5 pad_maximum_fusion.pack_ref
  3.9 0.8 stack.67
  11.0 1.4 stack.71
  13.1 123.6 %gather_attend.1 = (bf16[16,128,1024]{2,1,0:T(8,128)(2,1)}, bf16[16,128,1024]{2,1,0:T(8,128)(2,1)}, bf16[8,192,256]{2,1,0:T(8,128)(2,1)}, bf16[3,2048,64]{2,1,0:...) custom-call(bf16[128,1024]{1,0:T(8,128)(2,1)} %bitcast.103, ...), custom_call_target="tpu_custom_call" | custom-call | tf_op jit(solution)/shard_map/gather_attend/pallas_call | solution.py:385
  136.7 1.2 broadcast_in_dim.65
  137.9 98.7 %feed_forward.1 = (f32[128,1024]{1,0:T(8,128)}, f32[128,1024]{1,0:T(8,128)}, bf16[1024,256]{1,0:T(8,128)(2,1)}, bf16[1024,256]{1,0:T(8,128)(2,1)}, f32[8,256]{1,0:T(8,128)}) custom-call(bf16[128,1024]{1,0:T(8,128)(2,1)} %get-tuple-element.39.n2_ref, bf16[16,128,1024]{2,1,0:T(8,128)(2,1)} %get-tuple-element.40.cot_ref, ...), custom_call_target="tpu_custom_call" | custom-call | tf_op jit(solution)/shard_map/feed_forward/pallas_call | solution.py:481
  237.0 0.9 fusion.21
  237.8 1.3 multiply_reduce_fusion
  239.2 0.9 fusion.19
  240.9 1.5 convolution_convert_fusion.1
  242.3 67.9 %attend_back.1 = (f32[128,1024]{1,0:T(8,128)}, bf16[192,1024]{1,0:T(8,128)(2,1)}, f32[192,128]{1,0:T(8,128)}) custom-call(bf16[16,64,128]{2,1,0:T(8,128)(2,1)} %bitcast.106, bf16[8,192,256]{2,1,0:T(8,128)(2,1)} %get-tuple-element.47.qkvt, bf16[3,2048,64]{2,1,0:T(8,128)(2,1)} %get-tuple-element.48.qkvr, f32[8,256]{1,0:T(8,128)} %get-tuple-element.49.lse, ...), custom_call_target="tpu_custom_call" | custom-call | tf_op jit(solution)/shard_map/attend_back/pallas_call | solution.py:577
  310.2 1.3 fusion.17
  311.6 1.4 fusion.7
  313.0 2.1 fusion.10
  315.1 2.1 convolution_convert_fusion.gpj
  319.5 73.5 %sum_weights.1 = (f32[768,128]{1,0:T(8,128)}, f32[16,128]{1,0:T(8,128)}) custom-call(bf16[1024,256]{1,0:T(8,128)(2,1)} %get-tuple-element.53.gdn, bf16[1024,256]{1,0:T(8,128)(2,1)} %get-tuple-element.54.gup, bf16[192,1024]{1,0:T(8,128)(2,1)} %get-tuple-element.55.gqkv, bf16[1024,1024]{1,0:T(8,128)(2,1)} %convolution_convert_fusion.gpj, ...), custom_call_target="tpu_custom_call" | custom-call | tf_op jit(solution)/shard_map/sum_weights/pallas_call | solution.py:735
  393.0 0.8 slice_select_fusion
  394.3 1.5 slice_bitcast_fusion
  395.9 1.3 slice_bitcast_fusion.7
  397.2 1.4 slice_bitcast_fusion.1
  398.6 1.0 fusion.20
  400.3 1.2 slice_bitcast_fusion.2
  (46 shorter events, 8.2 us)
Async XLA Ops:
  0.6 0.8 copy-start
  137.9 98.7 %copy-start.1 = (f32[128,1024]{1,0:T(8,128)S(1)}, f32[128,1024]{1,0:T(8,128)}, u32[]{:S(2)}) copy-start(f32[128,1024]{1,0:T(8,128)} %get-tuple-element.38) | copy-start | bytes 1572868
  236.6 2.6 copy-start.5
  236.6 2.6 copy-start.6
  236.7 3.4 copy-start.2
  236.7 3.5 copy-start.4
  239.2 1.7 copy-start.3
  310.2 4.8 %copy-start.7 = (bf16[128,1024]{1,0:T(8,128)(2,1)S(1)}, bf16[128,1024]{1,0:T(8,128)(2,1)}, u32[]{:S(2)}) copy-start(bf16[128,1024]{1,0:T(8,128)(2,1)} %get-tuple-element.56) | copy-start | bytes 786436
  313.0 5.5 %copy-start.8 = (f32[192,128]{1,0:T(8,128)S(1)}, f32[192,128]{1,0:T(8,128)}, u32[]{:S(2)}) copy-start(f32[192,128]{1,0:T(8,128)} %get-tuple-element.57) | copy-start | bytes 294916

commit v2 on v1

v2 whole, which is shorter than its diff:
```python
import functools

import jax
import jax.numpy as jnp
from jax import lax
from jax.experimental import pallas as pl
from jax.experimental.pallas import tpu as pltpu
from jax.sharding import PartitionSpec as P

H = 16
HD = 64
D = 1024
HID = 256
TOK = 128
NS = 16
NF = 8
PACK = 768
MESH = pl.DeviceIdType.MESH
F32 = jnp.float32
BF16 = jnp.bfloat16
MIB = 1024 * 1024


def dot(left, right, lc=1, rc=0):
    return lax.dot_general(left, right, (((lc,), (rc,)), ((), ())), preferred_element_type=F32)


def layer_norm(values, gain, shift):
    average = jnp.mean(values, axis=-1, keepdims=True)
    centered = values - average
    spread = jnp.mean(centered * centered, axis=-1, keepdims=True)
    return centered * lax.rsqrt(spread + 1e-05) * gain + shift


def remote(src, dst, send, recv, **where):
    return pltpu.make_async_remote_copy(
        src_ref=src, dst_ref=dst, send_sem=send, recv_sem=recv, device_id=where, device_id_type=MESH
    )


def places():
    me = lax.axis_index("seq")
    core = lax.rem(me, 2)
    return me, core, me + 1 - 2 * core, lax.axis_index("fsdp")


def barrier_seq_all(me):
    sem = pltpu.get_barrier_semaphore()

    def body(k, carry):
        pl.semaphore_signal(sem, inc=1, device_id={"seq": lax.rem(me + k, NS)}, device_id_type=MESH)
        return carry

    lax.fori_loop(1, NS, body, 0)
    return sem


def barrier_fsdp(sem, row):
    def body(k, carry):
        pl.semaphore_signal(sem, inc=1, device_id={"fsdp": lax.rem(row + k, NF)}, device_id_type=MESH)
        return carry

    lax.fori_loop(1, NF, body, 0)


def loop(low, high, body):
    def step(k, carry):
        body(k)
        return carry

    lax.fori_loop(low, high, step, 0)


class Chips:
    def __init__(self):
        self.me, self.core, self.sib, self.row = places()
        self.own = self.me // 2
        step = 1 - 2 * lax.rem(self.own, 2)
        self.y = self.own + step
        self.r, self.f, self.l = (lax.rem(self.own + d, NF) for d in (2, 4, 6))
        self.ry, self.fy, self.ly = self.r + step, self.f + step, self.l + step

    def at(self, k):
        j = k // 2
        ring = lax.rem(self.own // 2 + j + (j // 2) * (5 - 2 * j), 4)
        return 2 * ring + lax.rem(self.own + k, 2)

    def device(self, chip):
        return 2 * chip + self.core


class Gather:
    def __init__(self, chips, own, out, send, recv, near):
        self.c, self.own, self.out, self.send, self.recv, self.near_sem = chips, own, out, send, recv, near
        rows = out.shape[1] // 2
        self.halves = (pl.ds(0, rows), pl.ds(rows, rows))

    def message(self, i, chip, half, to):
        c = self.c
        dst = self.out.at[c.device(chip), self.halves[half]]
        src = self.own.at[self.halves[half]] if i < 6 else dst
        return remote(src, dst, self.send.at[i], self.recv.at[chip, half], seq=c.device(to))

    def messages(self):
        c = self.c
        plan = [
            (c.own, 0, c.r), (c.own, 1, c.l), (c.own, 0, c.y), (c.own, 1, c.r), (c.own, 0, c.l), (c.own, 1, c.y),
            (c.l, 0, c.r), (c.r, 1, c.l), (c.y, 0, c.r), (c.y, 0, c.l), (c.y, 1, c.r), (c.y, 1, c.l),
            (c.f, 0, c.y), (c.f, 1, c.y),
        ]
        return [functools.partial(self.message, i, *p) for i, p in enumerate(plan)]

    def begin(self, *which):
        plan = self.messages()
        for i in which:
            plan[i]().start()

    def arrive(self, chip, half):
        self.message(6, chip, half, self.c.own).wait_recv()

    def hand(self, chip, first=False):
        block = self.c.device(chip)
        src = self.own if first else self.out.at[block]
        return remote(src, self.out.at[block], self.send.at[14 + chip], self.near_sem.at[chip], seq=self.c.sib)

    def near(self, chip):
        block = 2 * chip + 1 - self.c.core
        remote(
            self.out.at[block], self.out.at[block], self.send.at[0], self.near_sem.at[chip], seq=self.c.sib
        ).wait_recv()

    def start(self):
        self.begin(0, 1, 2, 3, 4, 5)
        self.hand(self.c.own, True).start()

    def pass_x(self):
        c = self.c
        self.arrive(c.l, 0)
        self.begin(6)
        self.arrive(c.r, 1)
        self.begin(7)

    def pass_y(self):
        c = self.c
        self.arrive(c.y, 0)
        self.begin(8, 9)
        self.arrive(c.y, 1)
        self.begin(10, 11)
        self.hand(c.y).start()

    def pass_f(self):
        c = self.c
        self.arrive(c.f, 0)
        self.begin(12)
        self.arrive(c.f, 1)
        self.begin(13)
        self.hand(c.f).start()

    def take(self, name):
        c = self.c
        chip = getattr(c, name)
        for half in {"r": (0,), "l": (1,)}.get(name, (0, 1)):
            self.arrive(chip, half)
        self.hand(chip).start()

    def step(self, k):
        @pl.when(k == 1)
        def _():
            self.pass_x()
            self.pass_y()

        @pl.when(k == 2)
        def _():
            self.take("r")

        @pl.when(k == 3)
        def _():
            self.pass_f()
            self.take("ry")

        @pl.when(k == 4)
        def _():
            self.take("l")

        @pl.when(k == 5)
        def _():
            self.take("ly")

        @pl.when(k == 7)
        def _():
            self.take("fy")

        self.near(self.c.at(k))

    def finish(self):
        for name in ("r", "ry", "l", "ly", "fy"):
            self.take(name)
        loop(0, NF, self.near)

    def drain(self):
        for message in self.messages():
            message().wait_send()
        loop(0, NF, lambda chip: self.hand(chip, True).wait_send())


class Reduce:
    def __init__(self, chips, part, pair, total, got, hop, hop_recv, send, recv):
        self.c, self.part, self.pair, self.total, self.got = chips, part, pair, total, got
        self.hop, self.hop_recv, self.send, self.recv = hop, hop_recv, send, recv
        rows = total.shape[1]
        self.low, self.high, self.all = pl.ds(0, rows // 2), pl.ds(rows // 2, rows // 2), pl.ds(0, rows)

    def pairing(self, chip):
        src = self.part.at[2 * chip + 1 - self.c.core]
        return remote(src, self.pair.at[chip], self.hop.at[chip], self.hop_recv.at[chip], seq=self.c.sib)

    def merge(self, chip):
        self.pairing(chip).wait_recv()
        both = self.part[self.c.device(chip)].astype(F32) + self.pair[chip].astype(F32)
        self.total[chip] = both.astype(BF16)

    def message(self, i):
        c = self.c
        chip, rows, slot, to = (
            (c.fy, self.low, 0, c.y), (c.fy, self.high, 0, c.y), (c.ly, self.all, 3, c.l), (c.ry, self.all, 2, c.r),
            (c.r, self.high, 4, c.r), (c.l, self.low, 5, c.l), (c.f, self.low, 1, c.r), (c.f, self.high, 1, c.l),
            (c.r, self.low, 4, c.r), (c.l, self.high, 5, c.l), (c.y, self.all, 6, c.y),
        )[i]
        return remote(
            self.total.at[chip, rows], self.got.at[slot, rows], self.send.at[i], self.recv.at[i], seq=c.device(to)
        )

    def begin(self, *which):
        for i in which:
            self.message(i).start()

    def add(self, i, chip, slot, rows):
        self.message(i).wait_recv()
        both = self.total[chip, rows].astype(F32) + self.got[slot, rows].astype(F32)
        self.total[chip, rows] = both.astype(BF16)

    def far(self):
        self.begin(0, 1)

    def sides(self):
        self.begin(2, 3, 4, 5)

    def turn(self):
        c = self.c
        self.add(0, c.f, 0, self.low)
        self.begin(6)
        self.add(1, c.f, 0, self.high)
        self.begin(7)

    def back(self):
        c = self.c
        self.add(6, c.r, 1, self.low)
        self.begin(8)
        self.add(7, c.l, 1, self.high)
        self.begin(9)

    def across(self):
        c = self.c
        self.add(2, c.y, 3, self.all)
        self.add(3, c.y, 2, self.all)
        self.begin(10)

    def finish(self):
        for i in (4, 5, 8, 9, 10):
            self.message(i).wait_recv()
        total = self.total[self.c.own].astype(F32)
        for slot in (4, 5, 6):
            total += self.got[slot].astype(F32)
        return total

    def drain(self, paired=True):
        if paired:
            loop(0, NF, lambda chip: self.pairing(chip).wait_send())
        for i in range(11):
            self.message(i).wait_send()


def key_extras(rows):
    lane = lax.broadcasted_iota(jnp.int32, (rows, HD), 1)
    pos = lax.broadcasted_iota(jnp.int32, (rows, HD), 0)
    high = (pos // 256) * 256
    value = jnp.where(lane < 3, high, jnp.where(lane < 6, pos - high, 0))
    return value.astype(F32).astype(BF16)


def query_extras(slope_ref):
    return jnp.broadcast_to(slope_ref[...], (HD, 256))


def kernel_a(
    hid_ref, cot_ref, pack_ref, sml_ref, qvb_ref, slope_ref,
    nrm, cota, qkvt, qkvr, lse, mid, n2, ctxr, wq, up, dn, pj, sm,
    hid, wf, smb, wqo, dno, pjo, kr, ctxo, ctxt,
    h_s, h_r, h_h, c_s, c_r, c_h, p_s, p_r, p_h, w_s, w_r, o_s, o_r, m_s, m_r, q_s, q_r, d_s, d_r, x_s, x_r, l_s,
):
    me, core, sib, row = places()
    sem = barrier_seq_all(me)
    barrier_fsdp(sem, row)
    pl.semaphore_wait(sem, NS - 1 + NF - 1)

    chips = Chips()
    first, others = pl.ds(0, 192), pl.ds(192, PACK - 192)

    def qkv_to(k):
        return remote(pack_ref.at[first], wf.at[row, first], w_s.at[k], w_r.at[row], fsdp=lax.rem(row + k, NF))

    def rest_to(k):
        return remote(pack_ref.at[others], wf.at[row, others], o_s.at[k], o_r.at[row], fsdp=lax.rem(row + k, NF))

    def small_to(k):
        return remote(sml_ref, smb.at[me], m_s.at[k], m_r.at[me], seq=lax.rem(me + k, NS))

    loop(1, NF, lambda k: qkv_to(k).start())
    loop(1, NS, lambda k: small_to(k).start())
    hidden = Gather(chips, hid_ref, hid, h_s, h_r, h_h)
    hidden.start()
    loop(1, NF, lambda k: rest_to(k).start())
    cot_own = pltpu.make_async_copy(cot_ref, cota.at[me], l_s)
    cot_own.start()
    wf[row] = pack_ref[...]
    smb[me] = sml_ref[...]
    hid[me] = hid_ref[...]
    kr[:, HD:] = key_extras(NS * TOK)

    def qkv_from(k):
        other = lax.rem(row + k, NF)
        remote(pack_ref.at[first], wf.at[other, first], w_s.at[k], w_r.at[other], fsdp=other).wait_recv()

    def rest_from(k):
        other = lax.rem(row + k, NF)
        remote(pack_ref.at[others], wf.at[other, others], o_s.at[k], o_r.at[other], fsdp=other).wait_recv()

    loop(1, NF, qkv_from)
    for f in range(NF):
        wqo[:, f * 128 : f * 128 + 128] = wf[f, 0:192, :]

    def q_block(j):
        block = 3 * me + j
        kind, head = block // H, lax.rem(block, H)
        src = wqo.at[pl.ds(j * HD, HD), :]
        dst = wq.at[pl.ds(pl.multiple_of(kind * HD, HD), HD), :]
        return head, kind, src, dst

    for j in range(3):
        head, kind, src, dst = q_block(j)

        @pl.when(head != me)
        def _():
            remote(src, dst, q_s.at[j], q_r.at[kind], seq=head).start()

        @pl.when(head == me)
        def _():
            dst[...] = src[...]

    def down_to(k):
        other = lax.rem(me + k, NS)
        return remote(
            dno.at[other], dn.at[pl.ds(pl.multiple_of(me * HD, HD), HD), :], d_s.at[k], d_r.at[me], seq=other
        )

    def down_from(k):
        other = lax.rem(me + k, NS)
        remote(
            dno.at[me], dn.at[pl.ds(pl.multiple_of(other * HD, HD), HD), :], d_s.at[k], d_r.at[other], seq=other
        ).wait_recv()

    def small_from(k):
        other = lax.rem(me + k, NS)
        remote(sml_ref, smb.at[other], m_s.at[k], m_r.at[other], seq=other).wait_recv()

    loop(1, NS, small_from)
    for t in range(NF):
        sm[:, t * 128 : t * 128 + 128] = smb[2 * t].astype(F32) + smb[2 * t + 1].astype(F32)

    for kind in range(3):

        @pl.when((kind * H + me) // 3 != me)
        def _():
            remote(
                wqo.at[pl.ds(0, HD), :], wq.at[pl.ds(kind * HD, HD), :], q_s.at[0], q_r.at[kind], seq=sib
            ).wait_recv()

    def norm_and_project(k):
        hidden.step(k)
        m = chips.at(k)
        values = hid[pl.ds(2 * m, 2)].reshape(2 * TOK, D).astype(F32)
        normed = layer_norm(values, sm[0:1, :], sm[1:2, :]).astype(BF16)
        nrm[pl.ds(2 * m, 2)] = normed.reshape(2, TOK, D)
        block = dot(wq[...], normed, 1, 1) + qvb_ref[:, 0:1]
        qkvt[m] = block.astype(BF16)
        at = pl.ds(pl.multiple_of(m * 256, 256), 256)
        qkvr[0, at, :] = block[0:64].T.astype(BF16)
        keys = block[64:128].T.astype(BF16)
        qkvr[1, at, :] = keys
        kr[at, 0:HD] = keys
        qkvr[2, at, :] = block[128:192].T.astype(BF16)

    loop(0, NF, norm_and_project)
    loop(1, NF, rest_from)
    for f in range(NF):
        lanes = slice(f * 128, f * 128 + 128)
        pjo[:, lanes] = wf[f, 192:256, :]
        up[lanes, 0:128] = wf[f, 512:640, :]
        up[lanes, 128:256] = wf[f, 640:768, :]
        for half in range(2):
            for piece in range(2):
                at = 256 + (2 * half + piece) * 64
                dno[2 * f + half, :, piece * 128 : piece * 128 + 128] = wf[f, at : at + 64, :]
    proj = Gather(chips, pjo, pj, p_s, p_r, p_h)
    proj.start()
    loop(1, NS, lambda k: down_to(k).start())
    dn[pl.ds(pl.multiple_of(me * HD, HD), HD), :] = dno[me]
    pj[me] = pjo[...]
    cot = Gather(chips, cot_ref, cota, c_s, c_r, c_h)
    cot.start()

    extras = query_extras(slope_ref)

    def ctx_to(j):
        return remote(ctxo.at[j], ctxt.at[me], x_s.at[j], x_r.at[me], seq=j)

    between = {1: [proj.pass_x], 2: [proj.pass_y], 4: [proj.pass_f], 5: [cot.pass_x], 6: [cot.pass_y]}
    for j in range(NF):
        for relay in between.get(j, []):
            relay()
        n = (j + 1) * 256
        queries = jnp.concatenate([(qkvt[j, 0:64, :].astype(F32) * 0.125).astype(BF16), extras], axis=0)
        scores = dot(kr[0:n, :], queries)
        kpos = lax.broadcasted_iota(jnp.int32, (256, 256), 0)
        qpos = lax.broadcasted_iota(jnp.int32, (256, 256), 1)
        last = jnp.where(kpos <= qpos, scores[n - 256 :], -1e30)
        scores = last if j == 0 else jnp.concatenate([scores[: n - 256], last], axis=0)
        peak = jnp.max(scores, axis=0, keepdims=True)
        expo = jnp.exp(scores - peak)
        total = jnp.sum(expo, axis=0, keepdims=True)
        lse[j : j + 1, :] = peak + jnp.log(total)
        weights = expo.astype(BF16)
        acc = dot(qkvt[0, 128:192, :], weights[0:256])
        for i in range(1, j + 1):
            acc += dot(qkvt[i, 128:192, :], weights[i * 256 : i * 256 + 256])
        context = (acc / total).astype(BF16)
        for half in range(2):
            target = 2 * j + half
            ctxo[target] = context[:, half * 128 : half * 128 + 128]

            @pl.when(me != target)
            def _():
                ctx_to(target).start()

            @pl.when(me == target)
            def _():
                ctxt[target] = ctxo[target]

    proj.finish()

    def ctx_from(k):
        other = lax.rem(me + k, NS)
        remote(ctxo.at[other], ctxt.at[other], x_s.at[other], x_r.at[other], seq=other).wait_recv()

    loop(1, NS, ctx_from)
    context = ctxt[...].reshape(D, TOK).astype(F32).T.astype(BF16)
    ctxr[...] = context
    middle = hid_ref[...].astype(F32) + dot(context, pj[...].reshape(D, D), 1, 1) + sm[2:3, :]
    mid[...] = middle
    n2[...] = layer_norm(middle, sm[3:4, :], sm[4:5, :]).astype(BF16)

    cot.pass_f()
    loop(1, NS, down_from)
    cot.finish()
    cot_own.wait()
    hidden.drain()
    cot.drain()
    proj.drain()
    loop(1, NF, lambda k: qkv_to(k).wait_send())
    loop(1, NF, lambda k: rest_to(k).wait_send())
    loop(1, NS, lambda k: small_to(k).wait_send())
    loop(1, NS, lambda k: down_to(k).wait_send())
    for j in range(3):
        head, kind, src, dst = q_block(j)

        @pl.when(head != me)
        def _():
            remote(src, dst, q_s.at[j], q_r.at[kind], seq=head).wait_send()

    def ctx_sent(k):
        other = lax.rem(me + k, NS)
        remote(ctxo.at[other], ctxt.at[me], x_s.at[other], x_r.at[me], seq=other).wait_send()

    loop(1, NS, ctx_sent)


def vm():
    return pl.BlockSpec(memory_space=pltpu.VMEM)


def hbm():
    return pl.BlockSpec(memory_space=pl.ANY)


def sems(*counts):
    return [pltpu.SemaphoreType.DMA(n if isinstance(n, tuple) else (n,)) for n in counts]


def params(number):
    return pltpu.CompilerParams(collective_id=number, has_side_effects=True, vmem_limit_bytes=56 * MIB)


def run_a(hid, cot, pack, small, qvb, slope):
    shapes = [
        ((NS, TOK, D), BF16), ((NS, TOK, D), BF16), ((NF, 192, 256), BF16), ((3, NS * TOK, HD), BF16),
        ((NF, 256), F32), ((TOK, D), F32), ((TOK, D), BF16), ((TOK, D), BF16), ((192, D), BF16),
        ((D, HID), BF16), ((D, HID), BF16), ((NS, HD, D), BF16), ((16, D), F32),
    ]
    specs = [vm() for _ in shapes]
    specs[1] = hbm()
    return pl.pallas_call(
        kernel_a,
        out_shape=[jax.ShapeDtypeStruct(*s) for s in shapes],
        in_specs=[vm(), hbm(), vm(), vm(), vm(), vm()],
        out_specs=specs,
        scratch_shapes=[
            pltpu.VMEM((NS, TOK, D), BF16),
            pltpu.VMEM((NF, PACK, 128), BF16),
            pltpu.VMEM((NS, 16, 128), BF16),
            pltpu.VMEM((192, D), BF16),
            pltpu.VMEM((NS, HD, HID), BF16),
            pltpu.VMEM((HD, D), BF16),
            pltpu.VMEM((NS * TOK, 128), BF16),
            pltpu.VMEM((NS, HD, TOK), BF16),
            pltpu.VMEM((NS, HD, TOK), BF16),
        ]
        + sems(22, (8, 2), 8) * 3
        + sems(8, 8, 8, 8, 16, 16, 3, 3, 16, 16, 16, 16)
        + [pltpu.SemaphoreType.DMA],
        compiler_params=params(0),
        name="gather_attend",
    )(hid, cot, pack, small, qvb, slope)


def kernel_m(
    n2_ref, cot_ref, up_ref, dn_ref, ub_ref,
    gn2, dtot, gup, gdn, gub,
    xa, act, gu, g_part, g_pair, g_total, g_got, d_part, d_pair,
    n_s, n_r, n_h, g1s, g1r, g2s, g2r, d1s, d1r,
):
    chips = Chips()
    sem = pltpu.get_barrier_semaphore()
    for other in (chips.sib, chips.device(chips.r), chips.device(chips.l), chips.device(chips.y)):
        pl.semaphore_signal(sem, inc=1, device_id={"seq": other}, device_id_type=MESH)
    pl.semaphore_wait(sem, 4)
    tokens = Gather(chips, n2_ref, xa, n_s, n_r, n_h)
    tokens.start()
    xa[chips.me] = n2_ref[...]
    grads = Reduce(chips, g_part, g_pair, g_total, g_got, g1s, g1r, g2s, g2r)
    downs = Reduce(chips, d_part, d_pair, dtot, None, d1s, d1r, None, None)
    gub[...] = jnp.zeros_like(gub)

    def put(side, chip, values):
        side.part[pl.ds(2 * chip, 2)] = values.astype(BF16).reshape(2, TOK, D)
        side.pairing(chip).start()

    def step(k):
        tokens.step(k)
        m = chips.at(k)
        rows = xa[pl.ds(2 * m, 2)].reshape(2 * TOK, D)
        upper = dot(rows, up_ref[...]) + ub_ref[...]
        square = upper * upper
        bend = jnp.tanh(0.7978845608 * upper * (1.0 + 0.044715 * square))
        half = 0.5 * (1.0 + bend)
        active = (upper * half).astype(BF16)
        slope = half + 0.5 * upper * (1.0 - bend * bend) * (0.7978845608 * (1.0 + 0.134145 * square))
        cots = cot_ref[pl.ds(2 * m, 2)].reshape(2 * TOK, D)
        grad = (dot(cots, dn_ref[...]) * slope).astype(BF16)
        at = pl.ds(pl.multiple_of(m * 256, 256), 256)
        act[at, :] = active
        gu[at, :] = grad
        gub[0:1, :] += jnp.sum(grad.astype(F32), axis=0, keepdims=True)
        put(grads, m, dot(grad, up_ref[...], 1, 1))
        put(downs, m, dot(active, dn_ref[...], 1, 1))

        @pl.when(k > 0)
        def _():
            grads.merge(chips.at(k - 1))
            downs.merge(chips.at(k - 1))

    loop(0, NF, step)
    grads.merge(chips.fy)
    grads.far()
    grads.sides()
    downs.merge(chips.fy)
    gup[...] = dot(xa[...].reshape(NS * TOK, D), gu[...], 0, 0).astype(BF16)
    grads.turn()
    gdn[...] = dot(cot_ref[...].reshape(NS * TOK, D), act[...], 0, 0).astype(BF16)
    grads.back()
    grads.across()
    gn2[...] = grads.finish()
    tokens.drain()
    grads.drain()
    loop(0, NF, lambda chip: downs.pairing(chip).wait_send())


def reduce_scratch(rows):
    return [pltpu.VMEM((NF, rows, D), BF16), pltpu.VMEM((NF, rows, D), BF16), pltpu.VMEM((7, rows, D), BF16)]


def run_m(n2, cot, up, dn, ub):
    shapes = [((TOK, D), F32), ((NF, TOK, D), BF16), ((D, HID), BF16), ((D, HID), BF16), ((8, HID), F32)]
    return pl.pallas_call(
        kernel_m,
        out_shape=[jax.ShapeDtypeStruct(*s) for s in shapes],
        in_specs=[vm()] * 5,
        out_specs=[vm()] * 5,
        scratch_shapes=[
            pltpu.VMEM((NS, TOK, D), BF16),
            pltpu.VMEM((NS * TOK, HID), BF16),
            pltpu.VMEM((NS * TOK, HID), BF16),
        ]
        + [pltpu.VMEM((NS, TOK, D), BF16)]
        + reduce_scratch(TOK)
        + [pltpu.VMEM((NS, TOK, D), BF16), pltpu.VMEM((NF, TOK, D), BF16)]
        + sems(22, (8, 2), 8, 8, 8, 16, 16, 8, 8),
        compiler_params=params(1),
        name="feed_forward",
    )(n2, cot, up, dn, ub)


def kernel_b(
    gc_ref, qkvt, qkvr, lse, wq, nrm, slope_ref, dtot, gpj, gdn_ref, gup_ref,
    gn1, gqkv, gsum, dsum, psum, weights,
    dct, gjt, kr, dk, dv, part, pair, total, got, d_total, d_got, p_pair, p_total, p_got, d1, pack, wgot,
    x_s, x_r, r1s, r1r, r2s, r2r, d2s, d2r, p1s, p1r, p2s, p2r, y_s, y_r, w_s, w_r, l_s,
):
    me, core, sib, row = places()
    chips = Chips()
    local = pltpu.make_async_copy(dtot, d_total, l_s)
    local.start()
    sem = barrier_seq_all(me)
    barrier_fsdp(sem, row)
    pl.semaphore_wait(sem, NS - 1 + NF - 1)
    downs = Reduce(chips, None, None, d_total, d_got, None, None, d2s, d2r)
    projs = Reduce(chips, gpj, p_pair, p_total, p_got, p1s, p1r, p2s, p2r)

    def block(other):
        return pl.ds(pl.multiple_of(other * HD, HD), HD)

    def down_to(k):
        other = lax.rem(me + k, NS)
        return remote(gdn_ref.at[block(other), :], d1.at[me], y_s.at[k], y_r.at[me], seq=other)

    def down_from(k):
        other = lax.rem(me + k, NS)
        remote(gdn_ref.at[block(me), :], d1.at[other], y_s.at[k], y_r.at[other], seq=other).wait_recv()

    def rows_to(k):
        other = lax.rem(row + k, NF)
        return remote(pack.at[other], wgot.at[row], w_s.at[k], w_r.at[row], fsdp=other)

    def rows_from(k):
        other = lax.rem(row + k, NF)
        remote(pack.at[other], wgot.at[other], w_s.at[k], w_r.at[other], fsdp=other).wait_recv()

    def send_weights():
        loop(1, NS, down_from)
        for f in range(NF):
            lanes = slice(f * 128, f * 128 + 128)
            for half in range(2):
                for piece in range(2):
                    at = (2 * half + piece) * 64
                    pack[f, at : at + 64, :] = d1[2 * f + half, :, piece * 128 : piece * 128 + 128]
            pack[f, 256:384, :] = gup_ref[lanes, 0:128]
            pack[f, 384:512, :] = gup_ref[lanes, 128:256]
        loop(1, NF, lambda k: rows_to(k).start())
        wgot[row] = pack[row]

    def merge_projs():
        loop(0, NF, projs.merge)
        projs.far()
        projs.sides()

    def ctx_to(k):
        other = lax.rem(me + k, NS)
        return remote(gc_ref.at[other], dct.at[me], x_s.at[k], x_r.at[me], seq=other)

    def ctx_from(k):
        other = lax.rem(me + k, NS)
        remote(gc_ref.at[me], dct.at[other], x_s.at[k], x_r.at[other], seq=other).wait_recv()

    loop(1, NS, lambda k: ctx_to(k).start())
    loop(0, NF, lambda chip: projs.pairing(chip).start())
    loop(1, NS, lambda k: down_to(k).start())
    local.wait()
    downs.far()
    downs.sides()
    dct[me] = gc_ref[me]
    d1[me] = gdn_ref[block(me), :]
    kr[:, HD:] = key_extras(NS * TOK)
    kr[:, 0:HD] = qkvr[1]
    dk[...] = jnp.zeros_like(dk)
    dv[...] = jnp.zeros_like(dv)
    extras = query_extras(slope_ref)
    loop(1, NS, ctx_from)
    between = {
        2: [downs.turn], 3: [merge_projs], 4: [downs.back, send_weights], 5: [downs.across, projs.turn],
        6: [projs.back, projs.across],
    }
    for j in range(NF):
        for relay in between.get(j, []):
            relay()
        n = (j + 1) * 256
        at = slice(j * 256, n)
        queries = jnp.concatenate([(qkvt[j, 0:64, :].astype(F32) * 0.125).astype(BF16), extras], axis=0)
        scores = dot(kr[0:n, :], queries)
        probs = jnp.exp(scores - lse[j : j + 1, :])
        kpos = lax.broadcasted_iota(jnp.int32, (256, 256), 0)
        qpos = lax.broadcasted_iota(jnp.int32, (256, 256), 1)
        last = jnp.where(kpos <= qpos, probs[n - 256 :], 0.0)
        probs = last if j == 0 else jnp.concatenate([probs[: n - 256], last], axis=0)
        gctx = jnp.concatenate([dct[2 * j], dct[2 * j + 1]], axis=1)
        gprobs = dot(qkvr[2, 0:n, :], gctx)
        inner = jnp.sum(probs * gprobs, axis=0, keepdims=True)
        gscores = (probs * (gprobs - inner) * 0.125).astype(BF16)
        gq = dot(qkvt[0, 64:128, :], gscores[0:256])
        for i in range(1, j + 1):
            gq += dot(qkvt[i, 64:128, :], gscores[i * 256 : i * 256 + 256])
        gjt[j, 0:64, :] = gq.astype(BF16)
        dk[0:n, :] += dot(gscores, qkvr[0, at, :])
        dv[0:n, :] += dot(probs.astype(BF16), gctx.astype(F32).T.astype(BF16))
    for j in range(NF):
        at = slice(j * 256, j * 256 + 256)
        gjt[j, 64:128, :] = dk[at, :].T.astype(BF16)
        gjt[j, 128:192, :] = dv[at, :].T.astype(BF16)

    norms = Reduce(chips, part, pair, total, got, r1s, r1r, r2s, r2r)

    def step(k):
        m = chips.at(NF - 1 - k)
        rows = gjt[m].astype(F32).T.astype(BF16)
        part[pl.ds(2 * m, 2)] = dot(rows, wq[...]).astype(BF16).reshape(2, TOK, D)
        norms.pairing(m).start()

        @pl.when(k > 0)
        def _():
            norms.merge(chips.at(NF - k))

        @pl.when(k == 1)
        def _():
            norms.begin(0, 1)

        @pl.when(k == 3)
        def _():
            norms.begin(2)

        @pl.when(k == 5)
        def _():
            norms.begin(5)
            norms.turn()

        @pl.when(k == 6)
        def _():
            norms.begin(3)

    loop(0, NF, step)
    norms.begin(4)
    norms.merge(chips.own)
    norms.back()
    norms.across()
    acc = jnp.zeros((192, D), F32)
    sums = jnp.zeros((192, 1), F32)
    for j in range(NF):
        acc += dot(gjt[j], nrm[2 * j : 2 * j + 2].reshape(2 * TOK, D))
        sums += jnp.sum(gjt[j].astype(F32), axis=1, keepdims=True)
    gqkv[...] = acc.astype(BF16)
    gsum[...] = jnp.broadcast_to(sums, (192, 128))
    loop(1, NF, rows_from)
    summed = wgot[0].astype(F32)
    for f in range(1, NF):
        summed += wgot[f].astype(F32)
    weights[...] = summed
    dsum[...] = downs.finish()
    psum[...] = projs.finish().astype(BF16)
    gn1[...] = norms.finish()
    norms.drain()
    downs.drain(False)
    projs.drain()
    loop(1, NS, lambda k: ctx_to(k).wait_send())
    loop(1, NS, lambda k: down_to(k).wait_send())
    loop(1, NF, lambda k: rows_to(k).wait_send())


def run_b(*operands):
    shapes = [
        ((TOK, D), F32), ((192, D), BF16), ((192, 128), F32), ((TOK, D), F32), ((HD, D), BF16), ((512, 128), F32)
    ]
    return pl.pallas_call(
        kernel_b,
        out_shape=[jax.ShapeDtypeStruct(*s) for s in shapes],
        in_specs=[hbm() if i == 7 else vm() for i in range(len(operands))],
        out_specs=[vm() for _ in shapes],
        scratch_shapes=[
            pltpu.VMEM((NS, HD, TOK), BF16),
            pltpu.VMEM((NF, 192, 256), BF16),
            pltpu.VMEM((NS * TOK, 128), BF16),
            pltpu.VMEM((NS * TOK, HD), F32),
            pltpu.VMEM((NS * TOK, HD), F32),
            pltpu.VMEM((NS, TOK, D), BF16),
        ]
        + reduce_scratch(TOK)
        + [pltpu.VMEM((NF, TOK, D), BF16), pltpu.VMEM((7, TOK, D), BF16)]
        + reduce_scratch(HD)
        + [pltpu.VMEM((NS, HD, HID), BF16), pltpu.VMEM((NF, 512, 128), BF16), pltpu.VMEM((NF, 512, 128), BF16)]
        + sems(16, 16, 8, 8, 16, 16, 16, 16, 8, 8, 16, 16, 16, 16, 8, 8)
        + [pltpu.SemaphoreType.DMA],
        compiler_params=params(2),
        name="attend_back",
    )(*operands)


def kernel_c(
    gqkv, psum, token_ref, local_ref,
    out, small,
    q1, m1, pack, got, m2, sgot,
    q_s, q_r, m_s, m_r, w_s, w_r, v_s, v_r,
):
    me, core, sib, row = places()
    sem = barrier_seq_all(me)
    barrier_fsdp(sem, row)
    pl.semaphore_wait(sem, NS - 1 + NF - 1)

    def tokens(k):
        other = lax.rem(me + k, NS)
        return remote(token_ref.at[other // 2], m1.at[me], m_s.at[k], m_r.at[me], seq=other)

    def q_block(kind):
        index = kind * H + me
        holder, slot = index // 3, lax.rem(index, 3)
        src = gqkv.at[pl.ds(kind * HD, HD), :]
        dst = q1.at[pl.ds(pl.multiple_of(slot * HD, HD), HD), :]
        return holder, slot, src, dst

    for kind in range(3):
        holder, slot, src, dst = q_block(kind)

        @pl.when(holder != me)
        def _():
            remote(src, dst, q_s.at[kind], q_r.at[slot], seq=holder).start()

        @pl.when(holder == me)
        def _():
            dst[...] = src[...]

    loop(1, NS, lambda k: tokens(k).start())
    m1[me] = token_ref[me // 2]
    for f in range(NF):
        pack[f, 192:256, :] = psum[:, f * 128 : f * 128 + 128]
    for slot in range(3):

        @pl.when(lax.rem(3 * me + slot, H) != me)
        def _():
            remote(
                gqkv.at[pl.ds(0, HD), :], q1.at[pl.ds(slot * HD, HD), :], q_s.at[0], q_r.at[slot], seq=sib
            ).wait_recv()

    for f in range(NF):
        pack[f, 0:192, :] = q1[:, f * 128 : f * 128 + 128]

    def rows(k):
        other = lax.rem(row + k, NF)
        return remote(pack.at[other], got.at[row], w_s.at[k], w_r.at[row], fsdp=other)

    def vectors(k):
        other = lax.rem(row + k, NF)
        return remote(m2, sgot.at[row], v_s.at[k], v_r.at[row], fsdp=other)

    loop(1, NF, lambda k: rows(k).start())
    got[row] = pack[row]

    def receive(k):
        other = lax.rem(me + k, NS)
        remote(token_ref.at[0], m1.at[other], m_s.at[k], m_r.at[other], seq=other).wait_recv()

    loop(1, NS, receive)
    local = m1[0]
    for p in range(1, NS):
        local += m1[p]
    m2[0:8, :] = local
    m2[8:16, :] = local_ref[...]
    loop(1, NF, lambda k: vectors(k).start())
    sgot[row] = m2[...]

    def receive_rows(k):
        other = lax.rem(row + k, NF)
        remote(m2, sgot.at[other], v_s.at[k], v_r.at[other], fsdp=other).wait_recv()
        remote(pack.at[other], got.at[other], w_s.at[k], w_r.at[other], fsdp=other).wait_recv()

    loop(1, NF, receive_rows)
    total = got[0].astype(F32)
    vector = sgot[0]
    for f in range(1, NF):
        total += got[f].astype(F32)
        vector += sgot[f]
    out[...] = total
    small[...] = vector
    loop(1, NS, lambda k: tokens(k).wait_send())
    loop(1, NF, lambda k: vectors(k).wait_send())
    loop(1, NF, lambda k: rows(k).wait_send())
    for kind in range(3):
        holder, slot, src, dst = q_block(kind)

        @pl.when(holder != me)
        def _():
            remote(src, dst, q_s.at[kind], q_r.at[slot], seq=holder).wait_send()


def run_c(*operands):
    shapes = [((256, 128), F32), ((16, 128), F32)]
    return pl.pallas_call(
        kernel_c,
        out_shape=[jax.ShapeDtypeStruct(*s) for s in shapes],
        in_specs=[vm() for _ in operands],
        out_specs=[vm() for _ in shapes],
        scratch_shapes=[
            pltpu.VMEM((192, D), BF16),
            pltpu.VMEM((NS, 8, 128), F32),
            pltpu.VMEM((NF, 256, 128), BF16),
            pltpu.VMEM((NF, 256, 128), BF16),
            pltpu.VMEM((16, 128), F32),
            pltpu.VMEM((NF, 16, 128), F32),
        ]
        + sems(3, 3, 16, 16, 8, 8, 8, 8),
        compiler_params=params(3),
        name="sum_weights",
    )(*operands)


def per_device(
    hidden_in, norm1_gain, norm1_shift, qkv_weight, query_bias, value_bias, proj_weight, proj_bias,
    norm2_gain, norm2_shift, up_weight, up_bias, down_weight, down_bias, out_cotangent,
):
    hid, cot = hidden_in[0], out_cotangent[0]
    me = lax.axis_index("seq")
    even = lax.rem(me, 2) == 0
    down_t = down_weight.T.reshape(HD, 4, 128).transpose(1, 0, 2).reshape(256, 128)
    up_r = up_weight.reshape(128, 2, 128).transpose(1, 0, 2).reshape(256, 128)
    pack = jnp.concatenate([qkv_weight.T, proj_weight.T, down_t, up_r], axis=0)
    vectors = jnp.stack([norm1_gain, norm1_shift, proj_bias, norm2_gain, norm2_shift, down_bias])
    none = jnp.zeros_like(vectors)
    vectors = jnp.concatenate([jnp.where(even, vectors, none), jnp.where(even, none, vectors)], axis=1)
    small = jnp.pad(vectors, ((0, 10), (0, 0)))
    qvb = jnp.concatenate([query_bias, jnp.zeros_like(query_bias), value_bias]).astype(F32)
    qvb = jnp.broadcast_to(qvb[:, None], (192, 128))
    slope = jnp.exp2(-8.0 * (me.astype(F32) + 1.0) / H)
    first = lax.reduce_precision(slope, 8, 7)
    second = lax.reduce_precision(slope - first, 8, 7)
    third = lax.reduce_precision(slope - first - second, 8, 7)
    parts = jnp.stack([first, second, third, first, second, third])
    slopes = jnp.pad(parts, (0, HD - 6)).astype(BF16)
    slopes = jnp.broadcast_to(slopes[:, None], (HD, 256))

    (nrm, cota, qkvt, qkvr, lse, middle, n2, ctx, wq, up, dn, pj, sm) = run_a(hid, cot, pack, small, qvb, slopes)
    gn2, downs, gup, gdn, gub = run_m(n2, cota, up, dn, up_bias.astype(F32)[None])

    pull = jax.vjp(layer_norm, middle, sm[3], sm[4])[1]
    grad_mid_norm, grad_gain_two, grad_shift_two = pull(gn2)
    cot32 = cot.astype(F32)
    grad_middle = cot32 + grad_mid_norm
    branch = grad_middle.astype(BF16)
    projection = pj.reshape(D, D)
    gpj = dot(branch, ctx, 0, 0).astype(BF16)
    gctx = dot(projection, branch, 0, 1).astype(BF16).reshape(NS, HD, TOK)
    gn1, gqkv, gsum, down_sum, psum, mlp = run_b(
        gctx, qkvt, qkvr, lse, wq, nrm, slopes, downs, gpj.reshape(NS, HD, D), gdn, gup
    )
    layer_out = middle + down_sum + sm[5]
    pull = jax.vjp(layer_norm, hid.astype(F32), sm[0], sm[1])[1]
    grad_in_norm, grad_gain_one, grad_shift_one = pull(gn1)
    input_grad = grad_middle + grad_in_norm

    nothing = jnp.zeros((D,), F32)
    token = jnp.stack(
        [
            grad_gain_one, grad_shift_one, jnp.sum(branch.astype(F32), axis=0), grad_gain_two, grad_shift_two,
            jnp.sum(cot32, axis=0), nothing, nothing,
        ]
    )
    token = token.reshape(8, 8, 128).transpose(1, 0, 2)
    head = jnp.concatenate([gsum[0:64, 0], gsum[128:192, 0]])[None]
    local = jnp.concatenate([head, gub[0].reshape(2, 128), jnp.zeros((5, 128), F32)], axis=0)
    out, vecs = run_c(gqkv, psum, token, local)
    mine = jnp.where(even, vecs[:6, :64], vecs[:6, 64:])
    return (
        layer_out.astype(BF16)[None],
        input_grad.astype(BF16)[None],
        mine[0],
        mine[1],
        out[0:192].T,
        vecs[8, :64],
        vecs[8, 64:],
        out[192:256].T,
        mine[2],
        mine[3],
        mine[4],
        mlp[256:512].reshape(2, 128, 128).transpose(1, 0, 2).reshape(128, 256),
        vecs[9:11].reshape(256),
        mlp[0:256].reshape(4, HD, 128).transpose(0, 2, 1).reshape(512, HD),
        mine[5],
    )


def solution(mesh):
    act, vec, mat = P("fsdp", "seq", None), P("seq"), P("fsdp", "seq")
    return jax.shard_map(
        per_device,
        mesh=mesh,
        in_specs=(act, vec, vec, mat, vec, vec, mat, vec, vec, vec, mat, vec, mat, vec, act),
        out_specs=(act, act, vec, vec, mat, vec, vec, mat, vec, vec, vec, mat, vec, mat, vec),
        check_vma=False,
    )
```

time: 408 us -> 300 us (0.74)
  Pallas kernels: 364 us -> 262 us
  local copies, waits for them, and re-layouts: 16.6 us -> 11.7 us
    pallas_call x1, Pallas kernels: 73.5 us -> 19.8 us  [run_c(): pl.pallas_call(kernel_c, out_shape=[jax.ShapeDtypeStruct(*s) for s in sha...]
    pallas_call x1, Pallas kernels: 98.7 us -> 66 us  [run_m(): pl.pallas_call(kernel_m, out_shape=[jax.ShapeDtypeStruct(*s) for s in sha...]
    pallas_call x1, Pallas kernels: 124 us -> 98.9 us  [run_a(): pl.pallas_call(kernel_a, out_shape=[jax.ShapeDtypeStruct(*s) for s in sha...]
    pallas_call x1, Pallas kernels: 67.9 us -> 77.2 us  [run_b(): pl.pallas_call(kernel_b, out_shape=[jax.ShapeDtypeStruct(*s) for s in sha...]
where the time goes in v2:
time: 300 us; the launch traced here: 297 us
  Pallas kernels  262 us (87%)
  other arithmetic  15 us (5%)
  local copies, waits for them, and re-layouts  11.7 us (4%)
  between operations  5.05 us (2%)
  matrix products  3.53 us (1%)
    pallas_call x1, Pallas kernels, run_a(): pl.pallas_call(kernel_a, out_shape=[jax.ShapeDtypeStruct(*s) for s in sha...  98.9 us
    pallas_call x1, Pallas kernels, run_b(): pl.pallas_call(kernel_b, out_shape=[jax.ShapeDtypeStruct(*s) for s in sha...  77.2 us
    pallas_call x1, Pallas kernels, run_m(): pl.pallas_call(kernel_m, out_shape=[jax.ShapeDtypeStruct(*s) for s in sha...  66 us
    pallas_call x1, Pallas kernels, run_c(): pl.pallas_call(kernel_c, out_shape=[jax.ShapeDtypeStruct(*s) for s in sha...  19.8 us

profile of v2, /device:TPU:0, one launch (start us, length us, event | category | flops | bytes accessed | tf_op | source)
XLA Modules:
  0.0 297.3 jit_solution(17401192895861819170)
XLA Ops:
  4.8 1.4 stack.71
  6.2 1.1 convert_reduce_fusion
  7.3 0.8 maximum_convert_fusion
  8.2 1.2 broadcast_in_dim.65
  9.4 0.8 stack.67
  11.5 0.9 copy_bitcast_fusion.3
  12.4 1.5 pad_maximum_fusion.pack_ref
  13.9 0.7 broadcast_in_dim.53.qvb_ref
  14.6 98.9 %gather_attend.1 = (bf16[16,128,1024]{2,1,0:T(8,128)(2,1)}, bf16[16,128,1024]{2,1,0:T(8,128)(2,1)}, bf16[8,192,256]{2,1,0:T(8,128)(2,1)}, bf16[3,2048,64]{2,1,0:...) custom-call(bf16[128,1024]{1,0:T(8,128)(2,1)} %bitcast.105, ...), custom_call_target="tpu_custom_call" | custom-call | tf_op jit(solution)/shard_map/gather_attend/pallas_call | solution.py:521
  113.6 1.2 reduce_sum.121
  114.7 1.2 multiply_reduce_fusion.2
  116.0 0.9 fusion.21
  116.9 66.0 %feed_forward.1 = (f32[128,1024]{1,0:T(8,128)}, bf16[8,128,1024]{2,1,0:T(8,128)(2,1)}, bf16[1024,256]{1,0:T(8,128)(2,1)}, bf16[1024,256]{1,0:T(8,128)(2,1)}, f32[8,256]{1,0:T(8,128)}) custom-call(bf16[128,1024]{1,0:T(8,128)(2,1)} %get-tuple-element.43.n2_ref, bf16[16,128,1024]{2,1,0:T(8,128)(2,1)} %get-tuple-element.44.cot_ref, ...), custom_call_target="tpu_custom_call" | custom-call | tf_op jit(solution)/shard_map/feed_forward/pallas_call | solution.py:613
  182.9 0.8 slice.68
  183.8 1.3 multiply_reduce_fusion
  185.1 1.3 fusion.19
  186.6 1.5 convolution_convert_fusion.1
  188.1 2.1 convolution_convert_fusion
  190.2 77.2 %attend_back.1 = (f32[128,1024]{1,0:T(8,128)}, bf16[192,1024]{1,0:T(8,128)(2,1)}, f32[192,128]{1,0:T(8,128)}, f32[128,1024]{1,0:T(8,128)}, bf16[64,1024]{1,0:T(8,128)(2,1)}, /*index=5*/f32[512,128]{1,0:T(8,128)}) custom-call(bf16[16,64,128]{2,1,0:T(8,128)(2,1)} %bitcast.108, bf16[8,192,256]{2,1,0:T(8,128)(2,1)} %get-tuple-element.49.qkvt, ...), custom_call_target="tpu_custom_call" | custom-call | tf_op jit(solution)/shard_map/attend_back/pallas_call | solution.py:799
  267.4 1.0 slice_reduce_fusion.1
  269.1 1.3 fusion.17
  270.5 1.4 fusion.7
  272.5 19.8 %sum_weights.1 = (f32[256,128]{1,0:T(8,128)}, f32[16,128]{1,0:T(8,128)}) custom-call(bf16[192,1024]{1,0:T(8,128)(2,1)} %get-tuple-element.60.gqkv, bf16[64,1024]{1,0:T(8,128)(2,1)} %get-tuple-element.61.psum, f32[8,8,128]{2,1,0:T(8,128)} %bitcast.113, f32[8,128]{1,0:T(8,128)} %maximum_maximum_fusion.local_ref), custom_call_target="tpu_custom_call" | custom-call | tf_op jit(solution)/shard_map/sum_weights/pallas_call | solution.py:921
  292.3 1.1 fusion.9
  (50 shorter events, 7.0 us)
Async XLA Ops:
  0.6 10.9 %copy-start = (bf16[128,256]{1,0:T(8,128)(2,1)S(1)}, bf16[128,256]{1,0:T(8,128)(2,1)}, u32[]{:S(2)}) copy-start(bf16[128,256]{1,0:T(8,128)(2,1)} %param.25) | copy-start | bytes 196612
  116.9 66.9 %copy-start.1 = (f32[128,1024]{1,0:T(8,128)S(1)}, f32[128,1024]{1,0:T(8,128)}, u32[]{:S(2)}) copy-start(f32[128,1024]{1,0:T(8,128)} %get-tuple-element.41) | copy-start | bytes 1572868
  182.9 3.5 %copy-start.5 = (bf16[1,128,1024]{2,1,0:T(8,128)(2,1)S(1)}, bf16[1,128,1024]{2,1,0:T(8,128)(2,1)}, u32[]{:S(2)}) copy-start(bf16[1,128,1024]{2,1,0:T(8,128)(2,1)} %param.29) | copy-start | bytes 786436
  182.9 3.7 %copy-start.3 = (bf16[16,64,1024]{2,1,0:T(8,128)(2,1)S(1)}, bf16[16,64,1024]{2,1,0:T(8,128)(2,1)}, u32[]{:S(2)}) copy-start(bf16[16,64,1024]{2,1,0:T(8,128)(2,1)} %get-tuple-element.42) | copy-start | bytes 6291460
  186.6 1.5 copy-start.7
  190.2 79.0 %copy-start.2 = (bf16[1,128,1024]{2,1,0:T(8,128)(2,1)S(1)}, bf16[1,128,1024]{2,1,0:T(8,128)(2,1)}, u32[]{:S(2)}) copy-start(bf16[1,128,1024]{2,1,0:T(8,128)(2,1)} %param.15) | copy-start | bytes 786436
  267.4 24.9 %copy-start.4 = (f32[128,1024]{1,0:T(8,128)S(1)}, f32[128,1024]{1,0:T(8,128)}, u32[]{:S(2)}) copy-start(f32[128,1024]{1,0:T(8,128)} %get-tuple-element.59) | copy-start | bytes 1572868
  267.4 24.9 %copy-start.6 = (f32[128,1024]{1,0:T(8,128)S(1)}, f32[128,1024]{1,0:T(8,128)}, u32[]{:S(2)}) copy-start(f32[128,1024]{1,0:T(8,128)} %get-tuple-element.58) | copy-start | bytes 1572868
  271.8 24.1 %copy-start.8 = (f32[512,128]{1,0:T(8,128)S(1)}, f32[512,128]{1,0:T(8,128)}, u32[]{:S(2)}) copy-start(f32[512,128]{1,0:T(8,128)} %get-tuple-element.66) | copy-start | bytes 786436
  292.3 1.1 copy-start.10
  292.3 2.4 copy-start.9

commit v3 on v2

--- a/solution.py
+++ b/solution.py
@@ -32,6 +32,19 @@
     return centered * lax.rsqrt(spread + 1e-05) * gain + shift
 
 
+def norm_back(values, gain, grad):
+    average = jnp.mean(values, axis=-1, keepdims=True)
+    centered = values - average
+    spread = jnp.mean(centered * centered, axis=-1, keepdims=True)
+    inverse = lax.rsqrt(spread + 1e-05)
+    normed = centered * inverse
+    scaled = grad * gain
+    mean = jnp.mean(scaled, axis=-1, keepdims=True)
+    slant = jnp.mean(scaled * normed, axis=-1, keepdims=True)
+    back = inverse * (scaled - mean - normed * slant)
+    return back, jnp.sum(grad * normed, axis=0, keepdims=True), jnp.sum(grad, axis=0, keepdims=True)
+
+
 def remote(src, dst, send, recv, **where):
     return pltpu.make_async_remote_copy(
         src_ref=src, dst_ref=dst, send_sem=send, recv_sem=recv, device_id=where, device_id_type=MESH
@@ -164,11 +177,6 @@
         self.hand(chip).start()
 
     def step(self, k):
-        @pl.when(k == 1)
-        def _():
-            self.pass_x()
-            self.pass_y()
-
         @pl.when(k == 2)
         def _():
             self.take("r")
@@ -280,6 +288,93 @@
             self.message(i).wait_send()
 
 
+class Rows:
+    def __init__(self, src, out, rows, send, recv):
+        self.src, self.out, self.rows, self.send, self.recv = src, out, rows, send, recv
+        self.row = lax.axis_index("fsdp")
+        self.mate = self.row + 1 - 2 * lax.rem(self.row, 2)
+
+    def message(self, k, second):
+        if second:
+            group = self.mate
+            src = self.out.at[group, self.rows]
+            slot = k + 3
+        else:
+            group = self.row
+            src = self.src.at[self.rows]
+            slot = k
+        to = self.mate if k == 0 else lax.rem(self.row + 2 * k, NF)
+        return remote(src, self.out.at[group, self.rows], self.send.at[slot], self.recv.at[group], fsdp=to)
+
+    def wait(self, group):
+        dst = self.out.at[group, self.rows]
+        remote(dst, dst, self.send.at[0], self.recv.at[group], fsdp=self.mate).wait_recv()
+
+    def start(self):
+        for k in range(4):
+            self.message(k, False).start()
+
+    def pass_on(self):
+        self.wait(self.mate)
+        for k in range(1, 4):
+            self.message(k, True).start()
+
+    def finish(self):
+        for k in range(1, 4):
+            self.wait(lax.rem(self.row + 2 * k, NF))
+            self.wait(lax.rem(self.mate + 2 * k, NF))
+
+    def drain(self):
+        for k in range(4):
+            self.message(k, False).wait_send()
+        for k in range(1, 4):
+            self.message(k, True).wait_send()
+
+
+class RowSums:
+    def __init__(self, pack, got, part, cross, send, recv):
+        self.pack, self.got, self.part, self.cross, self.send, self.recv = pack, got, part, cross, send, recv
+        self.row = lax.axis_index("fsdp")
+        self.high = lax.rem(self.row, 2)
+        self.z = self.row // 2
+
+    def message(self, k):
+        to = lax.rem(self.row + 2 * k, NF)
+        src = self.pack.at[pl.ds(2 * (to // 2), 2)]
+        return remote(src, self.got.at[k], self.send.at[k], self.recv.at[k], fsdp=to)
+
+    def last(self):
+        to = self.row + 1 - 2 * self.high
+        return remote(self.part.at[1], self.cross, self.send.at[0], self.recv.at[0], fsdp=to)
+
+    def start(self):
+        for k in range(1, 4):
+            self.message(k).start()
+
+    def middle(self, keep):
+        for k in range(1, 4):
+            self.message(k).wait_recv()
+
+        def total(which):
+            value = self.pack[2 * self.z + which].astype(F32)
+            for k in range(1, 4):
+                value += self.got[k, which].astype(F32)
+            return value
+
+        keep[...] = total(self.high)
+        self.part[1] = total(1 - self.high).astype(BF16)
+        self.last().start()
+
+    def finish(self, keep):
+        self.last().wait_recv()
+        return keep[...] + self.cross[...].astype(F32)
+
+    def drain(self):
+        for k in range(1, 4):
+            self.message(k).wait_send()
+        self.last().wait_send()
+
+
 def key_extras(rows):
     lane = lax.broadcasted_iota(jnp.int32, (rows, HD), 1)
     pos = lax.broadcasted_iota(jnp.int32, (rows, HD), 0)
@@ -288,54 +383,61 @@
     return value.astype(F32).astype(BF16)
 
 
-def query_extras(slope_ref):
-    return jnp.broadcast_to(slope_ref[...], (HD, 256))
+def query_extras(me):
+    row = lax.broadcasted_iota(jnp.int32, (HD, 256), 0)
+    slope = jnp.exp2(jnp.full((HD, 256), 0.0, F32) + (-8.0 / H) * (me + 1).astype(F32))
+    first = slope.astype(BF16).astype(F32)
+    second = (slope - first).astype(BF16).astype(F32)
+    third = slope - first - second
+    part = lax.rem(row, 3)
+    value = jnp.where(part == 0, first, jnp.where(part == 1, second, third))
+    return jnp.where(row < 6, value, 0.0).astype(BF16)
 
 
 def kernel_a(
-    hid_ref, cot_ref, pack_ref, sml_ref, qvb_ref, slope_ref,
+    hid_ref, cot_ref, wqkv_ref, wproj_ref, wup_ref, wdown_ref, vec_ref,
     nrm, cota, qkvt, qkvr, lse, mid, n2, ctxr, wq, up, dn, pj, sm,
-    hid, wf, smb, wqo, dno, pjo, kr, ctxo, ctxt,
+    hid, wf, smb, wqo, dno, pjo, kr, ctxo, ctxt, pack_ref, sml_ref,
     h_s, h_r, h_h, c_s, c_r, c_h, p_s, p_r, p_h, w_s, w_r, o_s, o_r, m_s, m_r, q_s, q_r, d_s, d_r, x_s, x_r, l_s,
 ):
     me, core, sib, row = places()
     sem = barrier_seq_all(me)
     barrier_fsdp(sem, row)
+    vectors = vec_ref[...].astype(F32)
+    pack_ref[0:192, :] = wqkv_ref[...].astype(F32).T.astype(BF16)
+    pack_ref[192:256, :] = wproj_ref[...].astype(F32).T.astype(BF16)
+    down_t = wdown_ref[...].astype(F32).T.astype(BF16)
+    for piece in range(4):
+        pack_ref[256 + piece * 64 : 320 + piece * 64, :] = down_t[:, piece * 128 : piece * 128 + 128]
+    pack_ref[512:640, :] = wup_ref[:, 0:128]
+    pack_ref[640:768, :] = wup_ref[:, 128:256]
+    blank = jnp.zeros((16, HD), F32)
+    left = jnp.concatenate([vectors, blank], axis=1)
+    right = jnp.concatenate([blank, vectors], axis=1)
+    sml_ref[...] = jnp.where(core == 0, left, right).astype(BF16)
+    columns = vectors.T
+    qvb = jnp.concatenate([columns[:, 6:7], jnp.zeros((HD, 1), F32), columns[:, 7:8]], axis=0)
     pl.semaphore_wait(sem, NS - 1 + NF - 1)
-
     chips = Chips()
-    first, others = pl.ds(0, 192), pl.ds(192, PACK - 192)
-
-    def qkv_to(k):
-        return remote(pack_ref.at[first], wf.at[row, first], w_s.at[k], w_r.at[row], fsdp=lax.rem(row + k, NF))
-
-    def rest_to(k):
-        return remote(pack_ref.at[others], wf.at[row, others], o_s.at[k], o_r.at[row], fsdp=lax.rem(row + k, NF))
+    qkv_rows = Rows(pack_ref, wf, pl.ds(0, 192), w_s, w_r)
+    other_rows = Rows(pack_ref, wf, pl.ds(192, PACK - 192), o_s, o_r)
 
     def small_to(k):
         return remote(sml_ref, smb.at[me], m_s.at[k], m_r.at[me], seq=lax.rem(me + k, NS))
 
-    loop(1, NF, lambda k: qkv_to(k).start())
-    loop(1, NS, lambda k: small_to(k).start())
+    qkv_rows.start()
     hidden = Gather(chips, hid_ref, hid, h_s, h_r, h_h)
     hidden.start()
-    loop(1, NF, lambda k: rest_to(k).start())
+    loop(1, NS, lambda k: small_to(k).start())
     cot_own = pltpu.make_async_copy(cot_ref, cota.at[me], l_s)
     cot_own.start()
     wf[row] = pack_ref[...]
     smb[me] = sml_ref[...]
     hid[me] = hid_ref[...]
     kr[:, HD:] = key_extras(NS * TOK)
-
-    def qkv_from(k):
-        other = lax.rem(row + k, NF)
-        remote(pack_ref.at[first], wf.at[other, first], w_s.at[k], w_r.at[other], fsdp=other).wait_recv()
-
-    def rest_from(k):
-        other = lax.rem(row + k, NF)
-        remote(pack_ref.at[others], wf.at[other, others], o_s.at[k], o_r.at[other], fsdp=other).wait_recv()
-
-    loop(1, NF, qkv_from)
+    qkv_rows.pass_on()
+    other_rows.start()
+    qkv_rows.finish()
     for f in range(NF):
         wqo[:, f * 128 : f * 128 + 128] = wf[f, 0:192, :]
 
@@ -369,6 +471,10 @@
             dno.at[me], dn.at[pl.ds(pl.multiple_of(other * HD, HD), HD), :], d_s.at[k], d_r.at[other], seq=other
         ).wait_recv()
 
+    hidden.pass_x()
+    hidden.pass_y()
+    other_rows.pass_on()
+
     def small_from(k):
         other = lax.rem(me + k, NS)
         remote(sml_ref, smb.at[other], m_s.at[k], m_r.at[other], seq=other).wait_recv()
@@ -385,13 +491,41 @@
                 wqo.at[pl.ds(0, HD), :], wq.at[pl.ds(kind * HD, HD), :], q_s.at[0], q_r.at[kind], seq=sib
             ).wait_recv()
 
+    proj = Gather(chips, pjo, pj, p_s, p_r, p_h)
+    cot = Gather(chips, cot_ref, cota, c_s, c_r, c_h)
+
+    def send_rest():
+        other_rows.finish()
+        for f in range(NF):
+            lanes = slice(f * 128, f * 128 + 128)
+            pjo[:, lanes] = wf[f, 192:256, :]
+            up[lanes, 0:128] = wf[f, 512:640, :]
+            up[lanes, 128:256] = wf[f, 640:768, :]
+            for half in range(2):
+                for piece in range(2):
+                    at = 256 + (2 * half + piece) * 64
+                    dno[2 * f + half, :, piece * 128 : piece * 128 + 128] = wf[f, at : at + 64, :]
+        proj.start()
+        loop(1, NS, lambda k: down_to(k).start())
+        dn[pl.ds(pl.multiple_of(me * HD, HD), HD), :] = dno[me]
+        pj[me] = pjo[...]
+
     def norm_and_project(k):
         hidden.step(k)
+
+        @pl.when(k == 4)
+        def _():
+            send_rest()
+
+        @pl.when(k == 6)
+        def _():
+            cot.start()
+
         m = chips.at(k)
         values = hid[pl.ds(2 * m, 2)].reshape(2 * TOK, D).astype(F32)
         normed = layer_norm(values, sm[0:1, :], sm[1:2, :]).astype(BF16)
         nrm[pl.ds(2 * m, 2)] = normed.reshape(2, TOK, D)
-        block = dot(wq[...], normed, 1, 1) + qvb_ref[:, 0:1]
+        block = dot(wq[...], normed, 1, 1) + qvb
         qkvt[m] = block.astype(BF16)
         at = pl.ds(pl.multiple_of(m * 256, 256), 256)
         qkvr[0, at, :] = block[0:64].T.astype(BF16)
@@ -401,30 +535,12 @@
         qkvr[2, at, :] = block[128:192].T.astype(BF16)
 
     loop(0, NF, norm_and_project)
-    loop(1, NF, rest_from)
-    for f in range(NF):
-        lanes = slice(f * 128, f * 128 + 128)
-        pjo[:, lanes] = wf[f, 192:256, :]
-        up[lanes, 0:128] = wf[f, 512:640, :]
-        up[lanes, 128:256] = wf[f, 640:768, :]
-        for half in range(2):
-            for piece in range(2):
-                at = 256 + (2 * half + piece) * 64
-                dno[2 * f + half, :, piece * 128 : piece * 128 + 128] = wf[f, at : at + 64, :]
-    proj = Gather(chips, pjo, pj, p_s, p_r, p_h)
-    proj.start()
-    loop(1, NS, lambda k: down_to(k).start())
-    dn[pl.ds(pl.multiple_of(me * HD, HD), HD), :] = dno[me]
-    pj[me] = pjo[...]
-    cot = Gather(chips, cot_ref, cota, c_s, c_r, c_h)
-    cot.start()
-
-    extras = query_extras(slope_ref)
+    extras = query_extras(me)
 
     def ctx_to(j):
         return remote(ctxo.at[j], ctxt.at[me], x_s.at[j], x_r.at[me], seq=j)
 
-    between = {1: [proj.pass_x], 2: [proj.pass_y], 4: [proj.pass_f], 5: [cot.pass_x], 6: [cot.pass_y]}
+    between = {0: [proj.pass_x], 2: [proj.pass_y], 4: [proj.pass_f], 5: [cot.pass_x], 6: [cot.pass_y], 7: [proj.finish]}
     for j in range(NF):
         for relay in between.get(j, []):
             relay()
@@ -456,8 +572,6 @@
             def _():
                 ctxt[target] = ctxo[target]
 
-    proj.finish()
-
     def ctx_from(k):
         other = lax.rem(me + k, NS)
         remote(ctxo.at[other], ctxt.at[other], x_s.at[other], x_r.at[other], seq=other).wait_recv()
@@ -476,8 +590,8 @@
     hidden.drain()
     cot.drain()
     proj.drain()
-    loop(1, NF, lambda k: qkv_to(k).wait_send())
-    loop(1, NF, lambda k: rest_to(k).wait_send())
+    qkv_rows.drain()
+    other_rows.drain()
     loop(1, NS, lambda k: small_to(k).wait_send())
     loop(1, NS, lambda k: down_to(k).wait_send())
     for j in range(3):
@@ -510,7 +624,7 @@
     return pltpu.CompilerParams(collective_id=number, has_side_effects=True, vmem_limit_bytes=56 * MIB)
 
 
-def run_a(hid, cot, pack, small, qvb, slope):
+def run_a(*operands):
     shapes = [
         ((NS, TOK, D), BF16), ((NS, TOK, D), BF16), ((NF, 192, 256), BF16), ((3, NS * TOK, HD), BF16),
         ((NF, 256), F32), ((TOK, D), F32), ((TOK, D), BF16), ((TOK, D), BF16), ((192, D), BF16),
@@ -521,7 +635,7 @@
     return pl.pallas_call(
         kernel_a,
         out_shape=[jax.ShapeDtypeStruct(*s) for s in shapes],
-        in_specs=[vm(), hbm(), vm(), vm(), vm(), vm()],
+        in_specs=[hbm() if i == 1 else vm() for i in range(len(operands))],
         out_specs=specs,
         scratch_shapes=[
             pltpu.VMEM((NS, TOK, D), BF16),
@@ -533,18 +647,20 @@
             pltpu.VMEM((NS * TOK, 128), BF16),
             pltpu.VMEM((NS, HD, TOK), BF16),
             pltpu.VMEM((NS, HD, TOK), BF16),
+            pltpu.VMEM((PACK, 128), BF16),
+            pltpu.VMEM((16, 128), BF16),
         ]
         + sems(22, (8, 2), 8) * 3
         + sems(8, 8, 8, 8, 16, 16, 3, 3, 16, 16, 16, 16)
         + [pltpu.SemaphoreType.DMA],
         compiler_params=params(0),
         name="gather_attend",
-    )(hid, cot, pack, small, qvb, slope)
+    )(*operands)
 
 
 def kernel_m(
-    n2_ref, cot_ref, up_ref, dn_ref, ub_ref,
-    gn2, dtot, gup, gdn, gub,
+    n2_ref, cot_ref, up_ref, dn_ref, ub_ref, mid_ref, sm_ref, pj_ref,
+    gmid, branch, gct, tok, dtot, gup, gdn, gub,
     xa, act, gu, g_part, g_pair, g_total, g_got, d_part, d_pair,
     n_s, n_r, n_h, g1s, g1r, g2s, g2r, d1s, d1r,
 ):
@@ -565,10 +681,15 @@
         side.pairing(chip).start()
 
     def step(k):
+        @pl.when(k == 1)
+        def _():
+            tokens.pass_x()
+            tokens.pass_y()
+
         tokens.step(k)
         m = chips.at(k)
         rows = xa[pl.ds(2 * m, 2)].reshape(2 * TOK, D)
-        upper = dot(rows, up_ref[...]) + ub_ref[...]
+        upper = dot(rows, up_ref[...]) + ub_ref[...].astype(F32)
         square = upper * upper
         bend = jnp.tanh(0.7978845608 * upper * (1.0 + 0.044715 * square))
         half = 0.5 * (1.0 + bend)
@@ -598,7 +719,16 @@
     gdn[...] = dot(cot_ref[...].reshape(NS * TOK, D), act[...], 0, 0).astype(BF16)
     grads.back()
     grads.across()
-    gn2[...] = grads.finish()
+    tok[...] = jnp.zeros_like(tok)
+    cot = cot_ref[chips.me].astype(F32)
+    tok[5:6, :] = jnp.sum(cot, axis=0, keepdims=True)
+    back, tok[3:4, :], tok[4:5, :] = norm_back(mid_ref[...], sm_ref[3:4, :], grads.finish())
+    total = cot + back
+    gmid[...] = total
+    low = total.astype(BF16)
+    branch[...] = low
+    tok[2:3, :] = jnp.sum(low.astype(F32), axis=0, keepdims=True)
+    gct[...] = dot(low, pj_ref[...].reshape(D, D)).T.astype(BF16).reshape(NS, HD, TOK)
     tokens.drain()
     grads.drain()
     loop(0, NF, lambda chip: downs.pairing(chip).wait_send())
@@ -608,13 +738,16 @@
     return [pltpu.VMEM((NF, rows, D), BF16), pltpu.VMEM((NF, rows, D), BF16), pltpu.VMEM((7, rows, D), BF16)]
 
 
-def run_m(n2, cot, up, dn, ub):
-    shapes = [((TOK, D), F32), ((NF, TOK, D), BF16), ((D, HID), BF16), ((D, HID), BF16), ((8, HID), F32)]
+def run_m(*operands):
+    shapes = [
+        ((TOK, D), F32), ((TOK, D), BF16), ((NS, HD, TOK), BF16), ((8, D), F32), ((NF, TOK, D), BF16),
+        ((D, HID), BF16), ((D, HID), BF16), ((8, HID), F32),
+    ]
     return pl.pallas_call(
         kernel_m,
         out_shape=[jax.ShapeDtypeStruct(*s) for s in shapes],
-        in_specs=[vm()] * 5,
-        out_specs=[vm()] * 5,
+        in_specs=[vm() for _ in operands],
+        out_specs=[vm() for _ in shapes],
         scratch_shapes=[
             pltpu.VMEM((NS, TOK, D), BF16),
             pltpu.VMEM((NS * TOK, HID), BF16),
@@ -626,14 +759,16 @@
         + sems(22, (8, 2), 8, 8, 8, 16, 16, 8, 8),
         compiler_params=params(1),
         name="feed_forward",
-    )(n2, cot, up, dn, ub)
+    )(*operands)
 
 
 def kernel_b(
-    gc_ref, qkvt, qkvr, lse, wq, nrm, slope_ref, dtot, gpj, gdn_ref, gup_ref,
-    gn1, gqkv, gsum, dsum, psum, weights,
-    dct, gjt, kr, dk, dv, part, pair, total, got, d_total, d_got, p_pair, p_total, p_got, d1, pack, wgot,
-    x_s, x_r, r1s, r1r, r2s, r2r, d2s, d2r, p1s, p1r, p2s, p2r, y_s, y_r, w_s, w_r, l_s,
+    gc_ref, qkvt, qkvr, lse, wq, nrm, branch, dtot, ctx_ref, gdn_ref, gup_ref, hid_ref, gmid, mid, sm, tok, gub,
+    layer_out, input_grad, weights, small,
+    dct, gjt, kr, dk, dv, part, pair, total, got, d_total, d_got, gpj, p_pair, p_total, p_got, d1,
+    u_pack, u_got, u_part, u_cross, u_keep, t_pack, t_got, t_part, t_cross, t_keep, gqkv, q1, tiles, m1, m2, sgot,
+    x_s, x_r, r1s, r1r, r2s, r2r, d2s, d2r, p1s, p1r, p2s, p2r, y_s, y_r, u_s, u_r, t_s, t_r, q_s, q_r, m_s, m_r,
+    v_s, v_r, l_s,
 ):
     me, core, sib, row = places()
     chips = Chips()
@@ -644,6 +779,8 @@
     pl.semaphore_wait(sem, NS - 1 + NF - 1)
     downs = Reduce(chips, None, None, d_total, d_got, None, None, d2s, d2r)
     projs = Reduce(chips, gpj, p_pair, p_total, p_got, p1s, p1r, p2s, p2r)
+    ups = RowSums(u_pack, u_got, u_part, u_cross, u_s, u_r)
+    rest = RowSums(t_pack, t_got, t_part, t_cross, t_s, t_r)
 
     def block(other):
         return pl.ds(pl.multiple_of(other * HD, HD), HD)
@@ -655,14 +792,6 @@
     def down_from(k):
         other = lax.rem(me + k, NS)
         remote(gdn_ref.at[block(me), :], d1.at[other], y_s.at[k], y_r.at[other], seq=other).wait_recv()
-
-    def rows_to(k):
-        other = lax.rem(row + k, NF)
-        return remote(pack.at[other], wgot.at[row], w_s.at[k], w_r.at[row], fsdp=other)
-
-    def rows_from(k):
-        other = lax.rem(row + k, NF)
-        remote(pack.at[other], wgot.at[other], w_s.at[k], w_r.at[other], fsdp=other).wait_recv()
 
     def send_weights():
         loop(1, NS, down_from)
@@ -671,17 +800,36 @@
             for half in range(2):
                 for piece in range(2):
                     at = (2 * half + piece) * 64
-                    pack[f, at : at + 64, :] = d1[2 * f + half, :, piece * 128 : piece * 128 + 128]
-            pack[f, 256:384, :] = gup_ref[lanes, 0:128]
-            pack[f, 384:512, :] = gup_ref[lanes, 128:256]
-        loop(1, NF, lambda k: rows_to(k).start())
-        wgot[row] = pack[row]
+                    u_pack[f, at : at + 64, :] = d1[2 * f + half, :, piece * 128 : piece * 128 + 128]
+            u_pack[f, 256:384, :] = gup_ref[lanes, 0:128]
+            u_pack[f, 384:512, :] = gup_ref[lanes, 128:256]
+        ups.start()
 
     def merge_projs():
         loop(0, NF, projs.merge)
         projs.far()
         projs.sides()
 
+    def q_block(kind):
+        index = kind * H + me
+        holder, slot = index // 3, lax.rem(index, 3)
+        return holder, slot, gqkv.at[pl.ds(kind * HD, HD), :], q1.at[block(slot), :]
+
+    def tokens(k):
+        other = lax.rem(me + k, NS)
+        return remote(tiles.at[other // 2], m1.at[me], m_s.at[k], m_r.at[me], seq=other)
+
+    def tokens_from(k):
+        other = lax.rem(me + k, NS)
+        remote(tiles.at[0], m1.at[other], m_s.at[k], m_r.at[other], seq=other).wait_recv()
+
+    def vectors(k):
+        return remote(m2, sgot.at[row], v_s.at[k], v_r.at[row], fsdp=lax.rem(row + k, NF))
+
+    def vectors_from(k):
+        other = lax.rem(row + k, NF)
+        remote(m2, sgot.at[other], v_s.at[k], v_r.at[other], fsdp=other).wait_recv()
+
     def ctx_to(k):
         other = lax.rem(me + k, NS)
         return remote(gc_ref.at[other], dct.at[me], x_s.at[k], x_r.at[me], seq=other)
@@ -691,23 +839,24 @@
         remote(gc_ref.at[me], dct.at[other], x_s.at[k], x_r.at[other], seq=other).wait_recv()
 
     loop(1, NS, lambda k: ctx_to(k).start())
-    loop(0, NF, lambda chip: projs.pairing(chip).start())
-    loop(1, NS, lambda k: down_to(k).start())
-    local.wait()
-    downs.far()
-    downs.sides()
     dct[me] = gc_ref[me]
     d1[me] = gdn_ref[block(me), :]
     kr[:, HD:] = key_extras(NS * TOK)
     kr[:, 0:HD] = qkvr[1]
     dk[...] = jnp.zeros_like(dk)
     dv[...] = jnp.zeros_like(dv)
-    extras = query_extras(slope_ref)
+    extras = query_extras(me)
+    for f in range(NF):
+        lanes = slice(f * 128, f * 128 + 128)
+        columns = branch[:, lanes].astype(F32).T.astype(BF16)
+        gpj[2 * f : 2 * f + 2] = dot(columns, ctx_ref[...]).astype(BF16).reshape(2, HD, D)
     loop(1, NS, ctx_from)
-    between = {
-        2: [downs.turn], 3: [merge_projs], 4: [downs.back, send_weights], 5: [downs.across, projs.turn],
-        6: [projs.back, projs.across],
-    }
+    local.wait()
+    downs.far()
+    downs.sides()
+    loop(0, NF, lambda chip: projs.pairing(chip).start())
+    loop(1, NS, lambda k: down_to(k).start())
+    between = {5: [merge_projs], 7: [downs.turn]}
     for j in range(NF):
         for relay in between.get(j, []):
             relay()
@@ -735,67 +884,131 @@
         gjt[j, 64:128, :] = dk[at, :].T.astype(BF16)
         gjt[j, 128:192, :] = dv[at, :].T.astype(BF16)
 
-    norms = Reduce(chips, part, pair, total, got, r1s, r1r, r2s, r2r)
-
-    def step(k):
-        m = chips.at(NF - 1 - k)
-        rows = gjt[m].astype(F32).T.astype(BF16)
-        part[pl.ds(2 * m, 2)] = dot(rows, wq[...]).astype(BF16).reshape(2, TOK, D)
-        norms.pairing(m).start()
-
-        @pl.when(k > 0)
-        def _():
-            norms.merge(chips.at(NF - k))
-
-        @pl.when(k == 1)
-        def _():
-            norms.begin(0, 1)
-
-        @pl.when(k == 3)
-        def _():
-            norms.begin(2)
-
-        @pl.when(k == 5)
-        def _():
-            norms.begin(5)
-            norms.turn()
-
-        @pl.when(k == 6)
-        def _():
-            norms.begin(3)
-
-    loop(0, NF, step)
-    norms.begin(4)
-    norms.merge(chips.own)
-    norms.back()
-    norms.across()
+    send_weights()
     acc = jnp.zeros((192, D), F32)
     sums = jnp.zeros((192, 1), F32)
     for j in range(NF):
         acc += dot(gjt[j], nrm[2 * j : 2 * j + 2].reshape(2 * TOK, D))
         sums += jnp.sum(gjt[j].astype(F32), axis=1, keepdims=True)
     gqkv[...] = acc.astype(BF16)
-    gsum[...] = jnp.broadcast_to(sums, (192, 128))
-    loop(1, NF, rows_from)
-    summed = wgot[0].astype(F32)
+    m2[...] = jnp.zeros_like(m2)
+    line = jnp.broadcast_to(sums, (192, 128)).T
+    m2[8:9, 0:64] = line[0:1, 0:64]
+    m2[8:9, 64:128] = line[0:1, 128:192]
+    m2[9:10, :] = gub[0:1, 0:128]
+    m2[10:11, :] = gub[0:1, 128:256]
+    for kind in range(3):
+        holder, slot, src, dst = q_block(kind)
+
+        @pl.when(holder != me)
+        def _():
+            remote(src, dst, q_s.at[kind], q_r.at[slot], seq=holder).start()
+
+        @pl.when(holder == me)
+        def _():
+            dst[...] = src[...]
+
+    norms = Reduce(chips, part, pair, total, got, r1s, r1r, r2s, r2r)
+    downs.back()
+    projs.turn()
+    during = {
+        1: [lambda: norms.begin(0, 1)],
+        2: [downs.across, projs.back],
+        3: [lambda: norms.begin(2)],
+        4: [projs.across],
+        5: [lambda: norms.begin(5), norms.turn],
+        6: [lambda: norms.begin(3)],
+    }
+
+    def step(k):
+        m = chips.at(NF - 1 - k)
+        rows = gjt[m].astype(F32).T.astype(BF16)
+        part[pl.ds(2 * m, 2)] = dot(rows, wq[...]).astype(BF16).reshape(2, TOK, D)
+        norms.pairing(m).start()
+
+        @pl.when(k > 0)
+        def _():
+            norms.merge(chips.at(NF - k))
+
+        for at, events in during.items():
+
+            @pl.when(k == at)
+            def _():
+                for event in events:
+                    event()
+
+    loop(0, NF, step)
+    norms.begin(4)
+    norms.merge(chips.own)
+    norms.back()
+    ups.middle(u_keep)
+    for slot in range(3):
+
+        @pl.when(lax.rem(3 * me + slot, H) != me)
+        def _():
+            remote(
+                gqkv.at[pl.ds(0, HD), :], q1.at[pl.ds(slot * HD, HD), :], q_s.at[0], q_r.at[slot], seq=sib
+            ).wait_recv()
+
+    proj_sum = projs.finish().astype(BF16)
+    for f in range(NF):
+        lanes = slice(f * 128, f * 128 + 128)
+        t_pack[f, 0:192, :] = q1[:, lanes]
+        t_pack[f, 192:256, :] = proj_sum[:, lanes]
+    rest.start()
+    norms.across()
+    layer_out[...] = (mid[...] + downs.finish() + sm[5:6, :]).astype(BF16)
+    back, gain, shift = norm_back(hid_ref[...].astype(F32), sm[0:1, :], norms.finish())
+    input_grad[...] = (gmid[...] + back).astype(BF16)
+    line = jnp.concatenate([gain, shift, tok[2:8, :]], axis=0)
+    for t in range(NF):
+        tiles[t] = line[:, t * 128 : t * 128 + 128]
+    loop(1, NS, lambda k: tokens(k).start())
+    m1[me] = tiles[me // 2]
+    rest.middle(t_keep)
+    weights[256:768, :] = ups.finish(u_keep)
+    loop(1, NS, tokens_from)
+    vector = m1[0]
+    for p in range(1, NS):
+        vector += m1[p]
+    m2[0:8, :] = vector
+    loop(1, NF, lambda k: vectors(k).start())
+    sgot[row] = m2[...]
+    weights[0:256, :] = rest.finish(t_keep)
+    loop(1, NF, vectors_from)
+    vector = sgot[0]
     for f in range(1, NF):
-        summed += wgot[f].astype(F32)
-    weights[...] = summed
-    dsum[...] = downs.finish()
-    psum[...] = projs.finish().astype(BF16)
-    gn1[...] = norms.finish()
+        vector += sgot[f]
+    small[...] = vector
     norms.drain()
     downs.drain(False)
     projs.drain()
+    ups.drain()
+    rest.drain()
     loop(1, NS, lambda k: ctx_to(k).wait_send())
     loop(1, NS, lambda k: down_to(k).wait_send())
-    loop(1, NF, lambda k: rows_to(k).wait_send())
+    loop(1, NS, lambda k: tokens(k).wait_send())
+    loop(1, NF, lambda k: vectors(k).wait_send())
+    for kind in range(3):
+        holder, slot, src, dst = q_block(kind)
+
+        @pl.when(holder != me)
+        def _():
+            remote(src, dst, q_s.at[kind], q_r.at[slot], seq=holder).wait_send()
+
+
+def row_scratch(rows):
+    return [
+        pltpu.VMEM((NF, rows, 128), BF16),
+        pltpu.VMEM((4, 2, rows, 128), BF16),
+        pltpu.VMEM((2, rows, 128), BF16),
+        pltpu.VMEM((rows, 128), BF16),
+        pltpu.VMEM((rows, 128), F32),
+    ]
 
 
 def run_b(*operands):
-    shapes = [
-        ((TOK, D), F32), ((192, D), BF16), ((192, 128), F32), ((TOK, D), F32), ((HD, D), BF16), ((512, 128), F32)
-    ]
+    shapes = [((TOK, D), BF16), ((TOK, D), BF16), ((PACK, 128), F32), ((16, 128), F32)]
     return pl.pallas_call(
         kernel_b,
         out_shape=[jax.ShapeDtypeStruct(*s) for s in shapes],
@@ -810,130 +1023,23 @@
             pltpu.VMEM((NS, TOK, D), BF16),
         ]
         + reduce_scratch(TOK)
-        + [pltpu.VMEM((NF, TOK, D), BF16), pltpu.VMEM((7, TOK, D), BF16)]
+        + [pltpu.VMEM((NF, TOK, D), BF16), pltpu.VMEM((7, TOK, D), BF16), pltpu.VMEM((NS, HD, D), BF16)]
         + reduce_scratch(HD)
-        + [pltpu.VMEM((NS, HD, HID), BF16), pltpu.VMEM((NF, 512, 128), BF16), pltpu.VMEM((NF, 512, 128), BF16)]
-        + sems(16, 16, 8, 8, 16, 16, 16, 16, 8, 8, 16, 16, 16, 16, 8, 8)
+        + [pltpu.VMEM((NS, HD, HID), BF16)]
+        + row_scratch(512)
+        + row_scratch(256)
+        + [
+            pltpu.VMEM((192, D), BF16),
+            pltpu.VMEM((192, D), BF16),
+            pltpu.VMEM((NF, 8, 128), F32),
+            pltpu.VMEM((NS, 8, 128), F32),
+            pltpu.VMEM((16, 128), F32),
+            pltpu.VMEM((NF, 16, 128), F32),
+        ]
+        + sems(16, 16, 8, 8, 16, 16, 16, 16, 8, 8, 16, 16, 16, 16, 4, 4, 4, 4, 3, 3, 16, 16, 8, 8)
         + [pltpu.SemaphoreType.DMA],
         compiler_params=params(2),
         name="attend_back",
-    )(*operands)
-
-
-def kernel_c(
-    gqkv, psum, token_ref, local_ref,
-    out, small,
-    q1, m1, pack, got, m2, sgot,
-    q_s, q_r, m_s, m_r, w_s, w_r, v_s, v_r,
-):
-    me, core, sib, row = places()
-    sem = barrier_seq_all(me)
-    barrier_fsdp(sem, row)
-    pl.semaphore_wait(sem, NS - 1 + NF - 1)
-
-    def tokens(k):
-        other = lax.rem(me + k, NS)
-        return remote(token_ref.at[other // 2], m1.at[me], m_s.at[k], m_r.at[me], seq=other)
-
-    def q_block(kind):
-        index = kind * H + me
-        holder, slot = index // 3, lax.rem(index, 3)
-        src = gqkv.at[pl.ds(kind * HD, HD), :]
-        dst = q1.at[pl.ds(pl.multiple_of(slot * HD, HD), HD), :]
-        return holder, slot, src, dst
-
-    for kind in range(3):
-        holder, slot, src, dst = q_block(kind)
-
-        @pl.when(holder != me)
-        def _():
-            remote(src, dst, q_s.at[kind], q_r.at[slot], seq=holder).start()
-
-        @pl.when(holder == me)
-        def _():
-            dst[...] = src[...]
-
-    loop(1, NS, lambda k: tokens(k).start())
-    m1[me] = token_ref[me // 2]
-    for f in range(NF):
-        pack[f, 192:256, :] = psum[:, f * 128 : f * 128 + 128]
-    for slot in range(3):
-
-        @pl.when(lax.rem(3 * me + slot, H) != me)
-        def _():
-            remote(
-                gqkv.at[pl.ds(0, HD), :], q1.at[pl.ds(slot * HD, HD), :], q_s.at[0], q_r.at[slot], seq=sib
-            ).wait_recv()
-
-    for f in range(NF):
-        pack[f, 0:192, :] = q1[:, f * 128 : f * 128 + 128]
-
-    def rows(k):
-        other = lax.rem(row + k, NF)
-        return remote(pack.at[other], got.at[row], w_s.at[k], w_r.at[row], fsdp=other)
-
-    def vectors(k):
-        other = lax.rem(row + k, NF)
-        return remote(m2, sgot.at[row], v_s.at[k], v_r.at[row], fsdp=other)
-
-    loop(1, NF, lambda k: rows(k).start())
-    got[row] = pack[row]
-
-    def receive(k):
-        other = lax.rem(me + k, NS)
-        remote(token_ref.at[0], m1.at[other], m_s.at[k], m_r.at[other], seq=other).wait_recv()
-
-    loop(1, NS, receive)
-    local = m1[0]
-    for p in range(1, NS):
-        local += m1[p]
-    m2[0:8, :] = local
-    m2[8:16, :] = local_ref[...]
-    loop(1, NF, lambda k: vectors(k).start())
-    sgot[row] = m2[...]
-
-    def receive_rows(k):
-        other = lax.rem(row + k, NF)
-        remote(m2, sgot.at[other], v_s.at[k], v_r.at[other], fsdp=other).wait_recv()
-        remote(pack.at[other], got.at[other], w_s.at[k], w_r.at[other], fsdp=other).wait_recv()
-
-    loop(1, NF, receive_rows)
-    total = got[0].astype(F32)
-    vector = sgot[0]
-    for f in range(1, NF):
-        total += got[f].astype(F32)
-        vector += sgot[f]
-    out[...] = total
-    small[...] = vector
-    loop(1, NS, lambda k: tokens(k).wait_send())
-    loop(1, NF, lambda k: vectors(k).wait_send())
-    loop(1, NF, lambda k: rows(k).wait_send())
-    for kind in range(3):
-        holder, slot, src, dst = q_block(kind)
-
-        @pl.when(holder != me)
-        def _():
-            remote(src, dst, q_s.at[kind], q_r.at[slot], seq=holder).wait_send()
-
-
-def run_c(*operands):
-    shapes = [((256, 128), F32), ((16, 128), F32)]
-    return pl.pallas_call(
-        kernel_c,
-        out_shape=[jax.ShapeDtypeStruct(*s) for s in shapes],
-        in_specs=[vm() for _ in operands],
-        out_specs=[vm() for _ in shapes],
-        scratch_shapes=[
-            pltpu.VMEM((192, D), BF16),
-            pltpu.VMEM((NS, 8, 128), F32),
-            pltpu.VMEM((NF, 256, 128), BF16),
-            pltpu.VMEM((NF, 256, 128), BF16),
-            pltpu.VMEM((16, 128), F32),
-            pltpu.VMEM((NF, 16, 128), F32),
-        ]
-        + sems(3, 3, 16, 16, 8, 8, 8, 8),
-        compiler_params=params(3),
-        name="sum_weights",
     )(*operands)
 
 
@@ -943,58 +1049,22 @@
 ):
     hid, cot = hidden_in[0], out_cotangent[0]
     me = lax.axis_index("seq")
-    even = lax.rem(me, 2) == 0
-    down_t = down_weight.T.reshape(HD, 4, 128).transpose(1, 0, 2).reshape(256, 128)
-    up_r = up_weight.reshape(128, 2, 128).transpose(1, 0, 2).reshape(256, 128)
-    pack = jnp.concatenate([qkv_weight.T, proj_weight.T, down_t, up_r], axis=0)
-    vectors = jnp.stack([norm1_gain, norm1_shift, proj_bias, norm2_gain, norm2_shift, down_bias])
-    none = jnp.zeros_like(vectors)
-    vectors = jnp.concatenate([jnp.where(even, vectors, none), jnp.where(even, none, vectors)], axis=1)
-    small = jnp.pad(vectors, ((0, 10), (0, 0)))
-    qvb = jnp.concatenate([query_bias, jnp.zeros_like(query_bias), value_bias]).astype(F32)
-    qvb = jnp.broadcast_to(qvb[:, None], (192, 128))
-    slope = jnp.exp2(-8.0 * (me.astype(F32) + 1.0) / H)
-    first = lax.reduce_precision(slope, 8, 7)
-    second = lax.reduce_precision(slope - first, 8, 7)
-    third = lax.reduce_precision(slope - first - second, 8, 7)
-    parts = jnp.stack([first, second, third, first, second, third])
-    slopes = jnp.pad(parts, (0, HD - 6)).astype(BF16)
-    slopes = jnp.broadcast_to(slopes[:, None], (HD, 256))
-
-    (nrm, cota, qkvt, qkvr, lse, middle, n2, ctx, wq, up, dn, pj, sm) = run_a(hid, cot, pack, small, qvb, slopes)
-    gn2, downs, gup, gdn, gub = run_m(n2, cota, up, dn, up_bias.astype(F32)[None])
-
-    pull = jax.vjp(layer_norm, middle, sm[3], sm[4])[1]
-    grad_mid_norm, grad_gain_two, grad_shift_two = pull(gn2)
-    cot32 = cot.astype(F32)
-    grad_middle = cot32 + grad_mid_norm
-    branch = grad_middle.astype(BF16)
-    projection = pj.reshape(D, D)
-    gpj = dot(branch, ctx, 0, 0).astype(BF16)
-    gctx = dot(projection, branch, 0, 1).astype(BF16).reshape(NS, HD, TOK)
-    gn1, gqkv, gsum, down_sum, psum, mlp = run_b(
-        gctx, qkvt, qkvr, lse, wq, nrm, slopes, downs, gpj.reshape(NS, HD, D), gdn, gup
+    nothing = jnp.zeros_like(norm1_gain)
+    vectors = jnp.stack(
+        [norm1_gain, norm1_shift, proj_bias, norm2_gain, norm2_shift, down_bias, query_bias, value_bias]
+        + [nothing] * 8
     )
-    layer_out = middle + down_sum + sm[5]
-    pull = jax.vjp(layer_norm, hid.astype(F32), sm[0], sm[1])[1]
-    grad_in_norm, grad_gain_one, grad_shift_one = pull(gn1)
-    input_grad = grad_middle + grad_in_norm
-
-    nothing = jnp.zeros((D,), F32)
-    token = jnp.stack(
-        [
-            grad_gain_one, grad_shift_one, jnp.sum(branch.astype(F32), axis=0), grad_gain_two, grad_shift_two,
-            jnp.sum(cot32, axis=0), nothing, nothing,
-        ]
+    (nrm, cota, qkvt, qkvr, lse, middle, n2, ctx, wq, up, dn, pj, sm) = run_a(
+        hid, cot, qkv_weight, proj_weight, up_weight, down_weight, vectors
     )
-    token = token.reshape(8, 8, 128).transpose(1, 0, 2)
-    head = jnp.concatenate([gsum[0:64, 0], gsum[128:192, 0]])[None]
-    local = jnp.concatenate([head, gub[0].reshape(2, 128), jnp.zeros((5, 128), F32)], axis=0)
-    out, vecs = run_c(gqkv, psum, token, local)
-    mine = jnp.where(even, vecs[:6, :64], vecs[:6, 64:])
+    gmid, branch, gctx, tok, downs, gup, gdn, gub = run_m(n2, cota, up, dn, up_bias[None], middle, sm, pj)
+    layer_out, input_grad, out, vecs = run_b(
+        gctx, qkvt, qkvr, lse, wq, nrm, branch, downs, ctx, gdn, gup, hid, gmid, middle, sm, tok, gub
+    )
+    mine = jnp.where(lax.rem(me, 2) == 0, vecs[:6, :64], vecs[:6, 64:])
     return (
-        layer_out.astype(BF16)[None],
-        input_grad.astype(BF16)[None],
+        layer_out[None],
+        input_grad[None],
         mine[0],
         mine[1],
         out[0:192].T,
@@ -1004,9 +1074,9 @@
         mine[2],
         mine[3],
         mine[4],
-        mlp[256:512].reshape(2, 128, 128).transpose(1, 0, 2).reshape(128, 256),
+        out[512:768].reshape(2, 128, 128).transpose(1, 0, 2).reshape(128, 256),
         vecs[9:11].reshape(256),
-        mlp[0:256].reshape(4, HD, 128).transpose(0, 2, 1).reshape(512, HD),
+        out[256:512].reshape(4, HD, 128).transpose(0, 2, 1).reshape(512, HD),
         mine[5],
     )
 

time: 300 us -> 251 us (0.84)
  Pallas kernels: 262 us -> 231 us
  other arithmetic: 15 us -> 0.83 us
  local copies, waits for them, and re-layouts: 11.7 us -> 17.9 us
  between operations: 5.05 us -> 0.7 us
  matrix products: 3.53 us -> 0 us
    pallas_call x1 -> x0, Pallas kernels: 19.8 us -> none  [run_c(): pl.pallas_call(kernel_c, out_shape=[jax.ShapeDtypeStruct(*s) for s in sha...]
    pallas_call x1, Pallas kernels: 98.9 us -> 81.1 us  [run_a(): pl.pallas_call(kernel_a, out_shape=[jax.ShapeDtypeStruct(*s) for s in sha...]
    reduce_sum x8 -> x0, other arithmetic: 8.91 us -> none  [the longest x3 3.98 us: layer_norm(): return centered * lax.rsqrt(spread + 1e-05) * gain + shift]
    unnamed x22 -> x7, local copies, waits for them, and re-layouts: 0.05 us -> 6.94 us
    pallas_call x1, Pallas kernels: 77.2 us -> 81.5 us  [run_b(): pl.pallas_call(kernel_b, out_shape=[jax.ShapeDtypeStruct(*s) for s in sha...]
    dot_general x2 -> x0, matrix products: 3.53 us -> none  [dot(): lax.dot_general(left, right, (((lc,), (rc,)), ((), ())), preferred_elemen...]
where the time goes in v3:
time: 251 us
  Pallas kernels  231 us (92%)
  local copies, waits for them, and re-layouts  17.9 us (7%)
    pallas_call x1, Pallas kernels, run_b(): pl.pallas_call(kernel_b, out_shape=[jax.ShapeDtypeStruct(*s) for s in sha...  81.5 us
    pallas_call x1, Pallas kernels, run_a(): pl.pallas_call(kernel_a, out_shape=[jax.ShapeDtypeStruct(*s) for s in sha...  81.1 us
    pallas_call x1, Pallas kernels, run_m(): pl.pallas_call(kernel_m, out_shape=[jax.ShapeDtypeStruct(*s) for s in sha...  68.8 us
    unnamed x7, local copies, waits for them, and re-layouts  6.94 us

profile of v3, /device:TPU:0, one launch (start us, length us, event | category | flops | bytes accessed | tf_op | source)
XLA Modules:
  0.0 250.8 jit_solution(13454585728516408441)
XLA Ops:
  0.6 1.6 copy.32.wdown_ref
  2.2 1.5 copy.30.wqkv_ref
  3.8 1.4 copy.31.wproj_ref
  5.2 1.9 stack.39.vec_ref
  7.2 81.1 %gather_attend.1 = (bf16[16,128,1024]{2,1,0:T(8,128)(2,1)}, bf16[16,128,1024]{2,1,0:T(8,128)(2,1)}, bf16[8,192,256]{2,1,0:T(8,128)(2,1)}, bf16[3,2048,64]{2,1,0:...) custom-call(bf16[128,1024]{1,0:T(8,128)(2,1)} %bitcast.48, ...), custom_call_target="tpu_custom_call" | custom-call | tf_op jit(solution)/shard_map/gather_attend/pallas_call | solution.py:635
  88.3 1.2 broadcast_in_dim.9.ub_ref
  89.5 68.8 %feed_forward.1 = (f32[128,1024]{1,0:T(8,128)}, bf16[128,1024]{1,0:T(8,128)(2,1)}, bf16[16,64,128]{2,1,0:T(8,128)(2,1)}, f32[8,1024]{1,0:T(8,128)}, bf16[8,128,1...) custom-call(bf16[128,1024]{1,0:T(8,128)(2,1)} %get-tuple-element.40.n2_ref, ...), custom_call_target="tpu_custom_call" | custom-call | tf_op jit(solution)/shard_map/feed_forward/pallas_call | solution.py:746
  158.3 81.5 %attend_back.1 = (bf16[128,1024]{1,0:T(8,128)(2,1)}, bf16[128,1024]{1,0:T(8,128)(2,1)}, f32[768,128]{1,0:T(8,128)}, f32[16,128]{1,0:T(8,128)}) custom-call(bf16[16,64,128]{2,1,0:T(8,128)(2,1)} %get-tuple-element.47.gc_ref, bf16[8,192,256]{2,1,0:T(8,128)(2,1)} %get-tuple-element.48.qkvt, bf16[3,2048,64]{2,1,0:T(8,128)(2,1)} %get-tuple-element.49.qkvr, ...), custom_call_target="tpu_custom_call" | custom-call | tf_op jit(solution)/shard_map/attend_back/pallas_call | solution.py:1012
  239.8 0.0 copy-start
  239.8 0.8 slice_select_fusion
  240.6 1.3 slice_bitcast_fusion.3
  242.0 1.0 fusion
  243.0 0.7 copy.39
  243.6 0.7 copy.40
  244.3 1.5 slice_bitcast_fusion
  245.8 1.4 slice_bitcast_fusion.1
  247.2 1.2 slice_bitcast_fusion.2
  248.5 1.7 copy.43
  250.1 0.0 copy-done
  250.1 0.7 copy.44
  (1 shorter events, 0.0 us)
Async XLA Ops:
  239.8 10.3 %copy-start = (bf16[128,1024]{1,0:T(8,128)(2,1)S(1)}, bf16[128,1024]{1,0:T(8,128)(2,1)}, u32[]{:S(2)}) copy-start(bf16[128,1024]{1,0:T(8,128)(2,1)} %get-tuple-element.62) | copy-start | bytes 786436

commit v4 on v3

--- a/solution.py
+++ b/solution.py
@@ -396,19 +396,21 @@
 
 def kernel_a(
     hid_ref, cot_ref, wqkv_ref, wproj_ref, wup_ref, wdown_ref, vec_ref,
-    nrm, cota, qkvt, qkvr, lse, mid, n2, ctxr, wq, up, dn, pj, sm,
-    hid, wf, smb, wqo, dno, pjo, kr, ctxo, ctxt, pack_ref, sml_ref,
-    h_s, h_r, h_h, c_s, c_r, c_h, p_s, p_r, p_h, w_s, w_r, o_s, o_r, m_s, m_r, q_s, q_r, d_s, d_r, x_s, x_r, l_s,
+    nrm, cota, qkvt, qkvr, lse, mid, n2, ctxr, wq, up, dn, pj, sm, ub,
+    hid, wf, smb, wqo, dno, pjo, kr, ctxo, ctxt, pack_ref, sml_ref, normed_all,
+    h_s, h_r, h_h, c_s, c_r, c_h, p_s, p_r, p_h, w_s, w_r, o_s, o_r, m_s, m_r, q_s, q_r, d_s, d_r, x_s, x_r, n_c, l_s,
 ):
     me, core, sib, row = places()
     sem = barrier_seq_all(me)
     barrier_fsdp(sem, row)
-    vectors = vec_ref[...].astype(F32)
-    pack_ref[0:192, :] = wqkv_ref[...].astype(F32).T.astype(BF16)
-    pack_ref[192:256, :] = wproj_ref[...].astype(F32).T.astype(BF16)
-    down_t = wdown_ref[...].astype(F32).T.astype(BF16)
+    rows = vec_ref[...].astype(F32)
+    vectors = jnp.concatenate([rows[0:8], jnp.zeros((8, HD), F32)], axis=0)
+    for i in range(4):
+        ub[0:1, i * HD : i * HD + HD] = rows[8 + i : 9 + i]
+    pack_ref[0:192, :] = wqkv_ref[...]
+    pack_ref[192:256, :] = wproj_ref[...]
     for piece in range(4):
-        pack_ref[256 + piece * 64 : 320 + piece * 64, :] = down_t[:, piece * 128 : piece * 128 + 128]
+        pack_ref[256 + piece * 64 : 320 + piece * 64, :] = wdown_ref[:, piece * 128 : piece * 128 + 128]
     pack_ref[512:640, :] = wup_ref[:, 0:128]
     pack_ref[640:768, :] = wup_ref[:, 128:256]
     blank = jnp.zeros((16, HD), F32)
@@ -510,6 +512,10 @@
         dn[pl.ds(pl.multiple_of(me * HD, HD), HD), :] = dno[me]
         pj[me] = pjo[...]
 
+    def keep(m):
+        pair = pl.ds(2 * m, 2)
+        return pltpu.make_async_copy(normed_all.at[pair], nrm.at[pair], n_c.at[m])
+
     def norm_and_project(k):
         hidden.step(k)
 
@@ -517,14 +523,16 @@
         def _():
             send_rest()
 
-        @pl.when(k == 6)
+        @pl.when(k == 3)
         def _():
             cot.start()
 
         m = chips.at(k)
         values = hid[pl.ds(2 * m, 2)].reshape(2 * TOK, D).astype(F32)
-        normed = layer_norm(values, sm[0:1, :], sm[1:2, :]).astype(BF16)
-        nrm[pl.ds(2 * m, 2)] = normed.reshape(2, TOK, D)
+        standard = layer_norm(values, 1.0, 0.0)
+        normed = (standard * sm[0:1, :] + sm[1:2, :]).astype(BF16)
+        normed_all[pl.ds(2 * m, 2)] = standard.astype(BF16).reshape(2, TOK, D)
+        keep(m).start()
         block = dot(wq[...], normed, 1, 1) + qvb
         qkvt[m] = block.astype(BF16)
         at = pl.ds(pl.multiple_of(m * 256, 256), 256)
@@ -540,7 +548,7 @@
     def ctx_to(j):
         return remote(ctxo.at[j], ctxt.at[me], x_s.at[j], x_r.at[me], seq=j)
 
-    between = {0: [proj.pass_x], 2: [proj.pass_y], 4: [proj.pass_f], 5: [cot.pass_x], 6: [cot.pass_y], 7: [proj.finish]}
+    between = {0: [proj.pass_x, proj.pass_y], 4: [proj.pass_f, cot.pass_x], 5: [cot.pass_y]}
     for j in range(NF):
         for relay in between.get(j, []):
             relay()
@@ -572,6 +580,9 @@
             def _():
                 ctxt[target] = ctxo[target]
 
+    cot.pass_f()
+    proj.finish()
+
     def ctx_from(k):
         other = lax.rem(me + k, NS)
         remote(ctxo.at[other], ctxt.at[other], x_s.at[other], x_r.at[other], seq=other).wait_recv()
@@ -583,10 +594,10 @@
     mid[...] = middle
     n2[...] = layer_norm(middle, sm[3:4, :], sm[4:5, :]).astype(BF16)
 
-    cot.pass_f()
     loop(1, NS, down_from)
     cot.finish()
     cot_own.wait()
+    loop(0, NF, lambda m: keep(m).wait())
     hidden.drain()
     cot.drain()
     proj.drain()
@@ -628,10 +639,9 @@
     shapes = [
         ((NS, TOK, D), BF16), ((NS, TOK, D), BF16), ((NF, 192, 256), BF16), ((3, NS * TOK, HD), BF16),
         ((NF, 256), F32), ((TOK, D), F32), ((TOK, D), BF16), ((TOK, D), BF16), ((192, D), BF16),
-        ((D, HID), BF16), ((D, HID), BF16), ((NS, HD, D), BF16), ((16, D), F32),
+        ((D, HID), BF16), ((D, HID), BF16), ((NS, HD, D), BF16), ((16, D), F32), ((8, HID), F32),
     ]
-    specs = [vm() for _ in shapes]
-    specs[1] = hbm()
+    specs = [hbm() if i < 2 else vm() for i in range(len(shapes))]
     return pl.pallas_call(
         kernel_a,
         out_shape=[jax.ShapeDtypeStruct(*s) for s in shapes],
@@ -649,9 +659,10 @@
             pltpu.VMEM((NS, HD, TOK), BF16),
             pltpu.VMEM((PACK, 128), BF16),
             pltpu.VMEM((16, 128), BF16),
+            pltpu.VMEM((NS, TOK, D), BF16),
         ]
         + sems(22, (8, 2), 8) * 3
-        + sems(8, 8, 8, 8, 16, 16, 3, 3, 16, 16, 16, 16)
+        + sems(8, 8, 8, 8, 16, 16, 3, 3, 16, 16, 16, 16, 8)
         + [pltpu.SemaphoreType.DMA],
         compiler_params=params(0),
         name="gather_attend",
@@ -659,12 +670,14 @@
 
 
 def kernel_m(
-    n2_ref, cot_ref, up_ref, dn_ref, ub_ref, mid_ref, sm_ref, pj_ref,
+    n2_ref, cot_hbm, up_ref, dn_ref, ub_ref, mid_ref, sm_ref, pj_ref,
     gmid, branch, gct, tok, dtot, gup, gdn, gub,
-    xa, act, gu, g_part, g_pair, g_total, g_got, d_part, d_pair,
-    n_s, n_r, n_h, g1s, g1r, g2s, g2r, d1s, d1r,
+    xa, act, gu, g_part, g_pair, g_total, g_got, d_part, d_pair, cot_ref,
+    n_s, n_r, n_h, g1s, g1r, g2s, g2r, d1s, d1r, l_s,
 ):
     chips = Chips()
+    cots_in = pltpu.make_async_copy(cot_hbm, cot_ref, l_s)
+    cots_in.start()
     sem = pltpu.get_barrier_semaphore()
     for other in (chips.sib, chips.device(chips.r), chips.device(chips.l), chips.device(chips.y)):
         pl.semaphore_signal(sem, inc=1, device_id={"seq": other}, device_id_type=MESH)
@@ -675,6 +688,7 @@
     grads = Reduce(chips, g_part, g_pair, g_total, g_got, g1s, g1r, g2s, g2r)
     downs = Reduce(chips, d_part, d_pair, dtot, None, d1s, d1r, None, None)
     gub[...] = jnp.zeros_like(gub)
+    cots_in.wait()
 
     def put(side, chip, values):
         side.part[pl.ds(2 * chip, 2)] = values.astype(BF16).reshape(2, TOK, D)
@@ -689,7 +703,7 @@
         tokens.step(k)
         m = chips.at(k)
         rows = xa[pl.ds(2 * m, 2)].reshape(2 * TOK, D)
-        upper = dot(rows, up_ref[...]) + ub_ref[...].astype(F32)
+        upper = dot(rows, up_ref[...]) + ub_ref[0:1, :]
         square = upper * upper
         bend = jnp.tanh(0.7978845608 * upper * (1.0 + 0.044715 * square))
         half = 0.5 * (1.0 + bend)
@@ -709,10 +723,15 @@
             grads.merge(chips.at(k - 1))
             downs.merge(chips.at(k - 1))
 
+        for at, message in ((3, 4), (4, 3), (5, 5), (6, 2)):
+
+            @pl.when(k == at)
+            def _():
+                grads.begin(message)
+
     loop(0, NF, step)
     grads.merge(chips.fy)
     grads.far()
-    grads.sides()
     downs.merge(chips.fy)
     gup[...] = dot(xa[...].reshape(NS * TOK, D), gu[...], 0, 0).astype(BF16)
     grads.turn()
@@ -746,7 +765,7 @@
     return pl.pallas_call(
         kernel_m,
         out_shape=[jax.ShapeDtypeStruct(*s) for s in shapes],
-        in_specs=[vm() for _ in operands],
+        in_specs=[hbm() if i == 1 else vm() for i in range(len(operands))],
         out_specs=[vm() for _ in shapes],
         scratch_shapes=[
             pltpu.VMEM((NS, TOK, D), BF16),
@@ -755,25 +774,28 @@
         ]
         + [pltpu.VMEM((NS, TOK, D), BF16)]
         + reduce_scratch(TOK)
-        + [pltpu.VMEM((NS, TOK, D), BF16), pltpu.VMEM((NF, TOK, D), BF16)]
-        + sems(22, (8, 2), 8, 8, 8, 16, 16, 8, 8),
+        + [pltpu.VMEM((NS, TOK, D), BF16), pltpu.VMEM((NF, TOK, D), BF16), pltpu.VMEM((NS, TOK, D), BF16)]
+        + sems(22, (8, 2), 8, 8, 8, 16, 16, 8, 8)
+        + [pltpu.SemaphoreType.DMA],
         compiler_params=params(1),
         name="feed_forward",
     )(*operands)
 
 
 def kernel_b(
-    gc_ref, qkvt, qkvr, lse, wq, nrm, branch, dtot, ctx_ref, gdn_ref, gup_ref, hid_ref, gmid, mid, sm, tok, gub,
-    layer_out, input_grad, weights, small,
+    gc_ref, qkvt, qkvr, lse, wq, nrm_hbm, branch, dtot, ctx_ref, gdn_ref, gup_ref, hid_ref, gmid, mid, sm, tok, gub,
+    layer_out, input_grad, w_qkv, w_proj, w_up, w_down, small,
     dct, gjt, kr, dk, dv, part, pair, total, got, d_total, d_got, gpj, p_pair, p_total, p_got, d1,
-    u_pack, u_got, u_part, u_cross, u_keep, t_pack, t_got, t_part, t_cross, t_keep, gqkv, q1, tiles, m1, m2, sgot,
+    u_pack, u_got, u_part, u_cross, u_keep, t_pack, t_got, t_part, t_cross, t_keep, gqkv, q1, tiles, m1, m2, sgot, nrm,
     x_s, x_r, r1s, r1r, r2s, r2r, d2s, d2r, p1s, p1r, p2s, p2r, y_s, y_r, u_s, u_r, t_s, t_r, q_s, q_r, m_s, m_r,
-    v_s, v_r, l_s,
+    v_s, v_r, l_s, n_c,
 ):
     me, core, sib, row = places()
     chips = Chips()
     local = pltpu.make_async_copy(dtot, d_total, l_s)
     local.start()
+    normed_in = pltpu.make_async_copy(nrm_hbm, nrm, n_c)
+    normed_in.start()
     sem = barrier_seq_all(me)
     barrier_fsdp(sem, row)
     pl.semaphore_wait(sem, NS - 1 + NF - 1)
@@ -850,13 +872,14 @@
         lanes = slice(f * 128, f * 128 + 128)
         columns = branch[:, lanes].astype(F32).T.astype(BF16)
         gpj[2 * f : 2 * f + 2] = dot(columns, ctx_ref[...]).astype(BF16).reshape(2, HD, D)
+    loop(1, NS, lambda k: down_to(k).start())
+    loop(0, NF, lambda chip: projs.pairing(chip).start())
+    local.wait()
+    normed_in.wait()
     loop(1, NS, ctx_from)
-    local.wait()
     downs.far()
     downs.sides()
-    loop(0, NF, lambda chip: projs.pairing(chip).start())
-    loop(1, NS, lambda k: down_to(k).start())
-    between = {5: [merge_projs], 7: [downs.turn]}
+    between = {3: [send_weights], 5: [merge_projs], 7: [downs.turn]}
     for j in range(NF):
         for relay in between.get(j, []):
             relay()
@@ -884,13 +907,20 @@
         gjt[j, 64:128, :] = dk[at, :].T.astype(BF16)
         gjt[j, 128:192, :] = dv[at, :].T.astype(BF16)
 
-    send_weights()
     acc = jnp.zeros((192, D), F32)
     sums = jnp.zeros((192, 1), F32)
     for j in range(NF):
         acc += dot(gjt[j], nrm[2 * j : 2 * j + 2].reshape(2 * TOK, D))
         sums += jnp.sum(gjt[j].astype(F32), axis=1, keepdims=True)
-    gqkv[...] = acc.astype(BF16)
+    gqkv[...] = (acc * sm[0:1, :] + sums * sm[1:2, :]).astype(BF16)
+    head = wq[...].astype(F32)
+    gain = jnp.sum(acc * head, axis=0, keepdims=True)
+    shift = jnp.sum(sums * head, axis=0, keepdims=True)
+    line = jnp.concatenate([gain, shift, tok[2:8, :]], axis=0)
+    for t in range(NF):
+        tiles[t] = line[:, t * 128 : t * 128 + 128]
+    loop(1, NS, lambda k: tokens(k).start())
+    m1[me] = tiles[me // 2]
     m2[...] = jnp.zeros_like(m2)
     line = jnp.broadcast_to(sums, (192, 128)).T
     m2[8:9, 0:64] = line[0:1, 0:64]
@@ -910,11 +940,10 @@
 
     norms = Reduce(chips, part, pair, total, got, r1s, r1r, r2s, r2r)
     downs.back()
-    projs.turn()
     during = {
-        1: [lambda: norms.begin(0, 1)],
-        2: [downs.across, projs.back],
-        3: [lambda: norms.begin(2)],
+        1: [lambda: norms.begin(0, 1), projs.turn],
+        2: [downs.across],
+        3: [lambda: norms.begin(2), projs.back],
         4: [projs.across],
         5: [lambda: norms.begin(5), norms.turn],
         6: [lambda: norms.begin(3)],
@@ -940,8 +969,15 @@
     loop(0, NF, step)
     norms.begin(4)
     norms.merge(chips.own)
+    ups.middle(u_keep)
+    loop(1, NS, tokens_from)
+    vector = m1[0]
+    for p in range(1, NS):
+        vector += m1[p]
+    m2[0:8, :] = vector
+    loop(1, NF, lambda k: vectors(k).start())
+    sgot[row] = m2[...]
     norms.back()
-    ups.middle(u_keep)
     for slot in range(3):
 
         @pl.when(lax.rem(3 * me + slot, H) != me)
@@ -958,28 +994,22 @@
     rest.start()
     norms.across()
     layer_out[...] = (mid[...] + downs.finish() + sm[5:6, :]).astype(BF16)
-    back, gain, shift = norm_back(hid_ref[...].astype(F32), sm[0:1, :], norms.finish())
-    input_grad[...] = (gmid[...] + back).astype(BF16)
-    line = jnp.concatenate([gain, shift, tok[2:8, :]], axis=0)
-    for t in range(NF):
-        tiles[t] = line[:, t * 128 : t * 128 + 128]
-    loop(1, NS, lambda k: tokens(k).start())
-    m1[me] = tiles[me // 2]
     rest.middle(t_keep)
-    weights[256:768, :] = ups.finish(u_keep)
-    loop(1, NS, tokens_from)
-    vector = m1[0]
-    for p in range(1, NS):
-        vector += m1[p]
-    m2[0:8, :] = vector
-    loop(1, NF, lambda k: vectors(k).start())
-    sgot[row] = m2[...]
-    weights[0:256, :] = rest.finish(t_keep)
+    rows = ups.finish(u_keep)
+    for piece in range(4):
+        w_down[:, piece * 128 : piece * 128 + 128] = rows[piece * HD : piece * HD + HD]
+    w_up[:, 0:128] = rows[256:384]
+    w_up[:, 128:256] = rows[384:512]
+    rows = rest.finish(t_keep)
+    w_qkv[...] = rows[0:192]
+    w_proj[...] = rows[192:256]
     loop(1, NF, vectors_from)
     vector = sgot[0]
     for f in range(1, NF):
         vector += sgot[f]
     small[...] = vector
+    back, _, _ = norm_back(hid_ref[...].astype(F32), sm[0:1, :], norms.finish())
+    input_grad[...] = (gmid[...] + back).astype(BF16)
     norms.drain()
     downs.drain(False)
     projs.drain()
@@ -1008,11 +1038,14 @@
 
 
 def run_b(*operands):
-    shapes = [((TOK, D), BF16), ((TOK, D), BF16), ((PACK, 128), F32), ((16, 128), F32)]
+    shapes = [
+        ((TOK, D), BF16), ((TOK, D), BF16), ((192, 128), F32), ((HD, 128), F32), ((128, HID), F32), ((HD, 512), F32),
+        ((16, 128), F32),
+    ]
     return pl.pallas_call(
         kernel_b,
         out_shape=[jax.ShapeDtypeStruct(*s) for s in shapes],
-        in_specs=[hbm() if i == 7 else vm() for i in range(len(operands))],
+        in_specs=[hbm() if i in (5, 7) else vm() for i in range(len(operands))],
         out_specs=[vm() for _ in shapes],
         scratch_shapes=[
             pltpu.VMEM((NS, HD, TOK), BF16),
@@ -1035,9 +1068,10 @@
             pltpu.VMEM((NS, 8, 128), F32),
             pltpu.VMEM((16, 128), F32),
             pltpu.VMEM((NF, 16, 128), F32),
+            pltpu.VMEM((NS, TOK, D), BF16),
         ]
         + sems(16, 16, 8, 8, 16, 16, 16, 16, 8, 8, 16, 16, 16, 16, 4, 4, 4, 4, 3, 3, 16, 16, 8, 8)
-        + [pltpu.SemaphoreType.DMA],
+        + [pltpu.SemaphoreType.DMA, pltpu.SemaphoreType.DMA],
         compiler_params=params(2),
         name="attend_back",
     )(*operands)
@@ -1049,16 +1083,13 @@
 ):
     hid, cot = hidden_in[0], out_cotangent[0]
     me = lax.axis_index("seq")
-    nothing = jnp.zeros_like(norm1_gain)
-    vectors = jnp.stack(
-        [norm1_gain, norm1_shift, proj_bias, norm2_gain, norm2_shift, down_bias, query_bias, value_bias]
-        + [nothing] * 8
+    vectors = [norm1_gain, norm1_shift, proj_bias, norm2_gain, norm2_shift, down_bias, query_bias, value_bias]
+    vectors = jnp.concatenate([v[None] for v in vectors] + [up_bias.reshape(4, HD)], axis=0)
+    (nrm, cota, qkvt, qkvr, lse, middle, n2, ctx, wq, up, dn, pj, sm, ub) = run_a(
+        hid, cot, qkv_weight.T, proj_weight.T, up_weight, down_weight.T, vectors
     )
-    (nrm, cota, qkvt, qkvr, lse, middle, n2, ctx, wq, up, dn, pj, sm) = run_a(
-        hid, cot, qkv_weight, proj_weight, up_weight, down_weight, vectors
-    )
-    gmid, branch, gctx, tok, downs, gup, gdn, gub = run_m(n2, cota, up, dn, up_bias[None], middle, sm, pj)
-    layer_out, input_grad, out, vecs = run_b(
+    gmid, branch, gctx, tok, downs, gup, gdn, gub = run_m(n2, cota, up, dn, ub, middle, sm, pj)
+    layer_out, input_grad, w_qkv, w_proj, w_up, w_down, vecs = run_b(
         gctx, qkvt, qkvr, lse, wq, nrm, branch, downs, ctx, gdn, gup, hid, gmid, middle, sm, tok, gub
     )
     mine = jnp.where(lax.rem(me, 2) == 0, vecs[:6, :64], vecs[:6, 64:])
@@ -1067,16 +1098,16 @@
         input_grad[None],
         mine[0],
         mine[1],
-        out[0:192].T,
+        w_qkv.T,
         vecs[8, :64],
         vecs[8, 64:],
-        out[192:256].T,
+        w_proj.T,
         mine[2],
         mine[3],
         mine[4],
-        out[512:768].reshape(2, 128, 128).transpose(1, 0, 2).reshape(128, 256),
+        w_up,
         vecs[9:11].reshape(256),
-        out[256:512].reshape(4, HD, 128).transpose(0, 2, 1).reshape(512, HD),
+        w_down.T,
         mine[5],
     )
 

time: 251 us -> 225 us (0.90)
  Pallas kernels: 231 us -> 208 us
  local copies, waits for them, and re-layouts: 17.9 us -> 14.7 us
    pallas_call x1, Pallas kernels: 68.8 us -> 59.2 us  [run_m(): pl.pallas_call(kernel_m, out_shape=[jax.ShapeDtypeStruct(*s) for s in sha...]
    pallas_call x1, Pallas kernels: 81.5 us -> 72.6 us  [run_b(): pl.pallas_call(kernel_b, out_shape=[jax.ShapeDtypeStruct(*s) for s in sha...]
    pallas_call x1, Pallas kernels: 81.1 us -> 76.6 us  [run_a(): pl.pallas_call(kernel_a, out_shape=[jax.ShapeDtypeStruct(*s) for s in sha...]
    transpose x2 -> x0, local copies, waits for them, and re-layouts: 2.91 us -> none  [the longest x1 1.54 us: per_device(): out[0:192]]
    unnamed x7 -> x6, local copies, waits for them, and re-layouts: 6.94 us -> 9.38 us
where the time goes in v4:
time: 225 us
  Pallas kernels  208 us (92%)
  local copies, waits for them, and re-layouts  14.7 us (7%)
    pallas_call x1, Pallas kernels, run_a(): pl.pallas_call(kernel_a, out_shape=[jax.ShapeDtypeStruct(*s) for s in sha...  76.6 us
    pallas_call x1, Pallas kernels, run_b(): pl.pallas_call(kernel_b, out_shape=[jax.ShapeDtypeStruct(*s) for s in sha...  72.6 us
    pallas_call x1, Pallas kernels, run_m(): pl.pallas_call(kernel_m, out_shape=[jax.ShapeDtypeStruct(*s) for s in sha...  59.2 us
    unnamed x6, local copies, waits for them, and re-layouts  9.38 us

profile of v4, /device:TPU:0, one launch (start us, length us, event | category | flops | bytes accessed | tf_op | source)
XLA Modules:
  0.0 224.5 jit_solution(13170390153179767642)
XLA Ops:
  0.6 0.7 reshape.36
  1.4 2.0 concatenate.3.vec_ref
  3.3 76.6 %gather_attend.1 = (bf16[16,128,1024]{2,1,0:T(8,128)(2,1)}, bf16[16,128,1024]{2,1,0:T(8,128)(2,1)}, bf16[8,192,256]{2,1,0:T(8,128)(2,1)}, bf16[3,2048,64]{2,1,0:...) custom-call(bf16[128,1024]{1,0:T(8,128)(2,1)} %bitcast.36, ...), custom_call_target="tpu_custom_call" | custom-call | tf_op jit(solution)/shard_map/gather_attend/pallas_call | solution.py:645
  80.0 59.2 %feed_forward.1 = (f32[128,1024]{1,0:T(8,128)}, bf16[128,1024]{1,0:T(8,128)(2,1)}, bf16[16,64,128]{2,1,0:T(8,128)(2,1)}, f32[8,1024]{1,0:T(8,128)}, bf16[8,128,1...) custom-call(bf16[128,1024]{1,0:T(8,128)(2,1)} %get-tuple-element.44.n2_ref, ...), custom_call_target="tpu_custom_call" | custom-call | tf_op jit(solution)/shard_map/feed_forward/pallas_call | solution.py:765
  139.2 72.6 %attend_back.1 = (bf16[128,1024]{1,0:T(8,128)(2,1)}, bf16[128,1024]{1,0:T(8,128)(2,1)}, f32[192,128]{1,0:T(8,128)}, f32[64,128]{1,0:T(8,128)}, f32[128,256]{1,0:...) custom-call(bf16[16,64,128]{2,1,0:T(8,128)(2,1)} %get-tuple-element.52.gc_ref, ...), custom_call_target="tpu_custom_call" | custom-call | tf_op jit(solution)/shard_map/attend_back/pallas_call | solution.py:1045
  211.7 0.8 slice_select_fusion
  212.6 1.3 slice_bitcast_fusion.1
  213.9 1.2 slice_bitcast_fusion
  215.1 1.7 copy.36
  216.8 1.7 copy.37
  218.5 1.5 copy.38
  220.0 1.4 copy.39
  221.4 1.6 copy.40
  223.0 1.6 copy.41

commit v5 on v4

--- a/solution.py
+++ b/solution.py
@@ -396,9 +396,12 @@
 
 def kernel_a(
     hid_ref, cot_ref, wqkv_ref, wproj_ref, wup_ref, wdown_ref, vec_ref,
-    nrm, cota, qkvt, qkvr, lse, mid, n2, ctxr, wq, up, dn, pj, sm, ub,
-    hid, wf, smb, wqo, dno, pjo, kr, ctxo, ctxt, pack_ref, sml_ref, normed_all,
-    h_s, h_r, h_h, c_s, c_r, c_h, p_s, p_r, p_h, w_s, w_r, o_s, o_r, m_s, m_r, q_s, q_r, d_s, d_r, x_s, x_r, n_c, l_s,
+    nrm, qkvt, qkvr, lse, mid, ctxr, wq, sm, gmid, branch, gct, tok, dtot, gup, gdn, gub,
+    hid, wf, smb, wqo, dno, pjo, kr, ctxo, ctxt, pack_ref, sml_ref, normed_all, cota, n2, up, dn, pj, ub,
+    xa, act, gu, g_part, g_pair, g_total, g_got, d_part, d_pair,
+    h_s, h_r, h_h, c_s, c_r, c_h, p_s, p_r, p_h, n_s, n_r, n_h,
+    w_s, w_r, o_s, o_r, m_s, m_r, q_s, q_r, d_s, d_r, x_s, x_r, n_c,
+    g1s, g1r, g2s, g2r, d1s, d1r,
 ):
     me, core, sib, row = places()
     sem = barrier_seq_all(me)
@@ -431,11 +434,10 @@
     hidden = Gather(chips, hid_ref, hid, h_s, h_r, h_h)
     hidden.start()
     loop(1, NS, lambda k: small_to(k).start())
-    cot_own = pltpu.make_async_copy(cot_ref, cota.at[me], l_s)
-    cot_own.start()
     wf[row] = pack_ref[...]
     smb[me] = sml_ref[...]
     hid[me] = hid_ref[...]
+    cota[me] = cot_ref[...]
     kr[:, HD:] = key_extras(NS * TOK)
     qkv_rows.pass_on()
     other_rows.start()
@@ -548,7 +550,7 @@
     def ctx_to(j):
         return remote(ctxo.at[j], ctxt.at[me], x_s.at[j], x_r.at[me], seq=j)
 
-    between = {0: [proj.pass_x, proj.pass_y], 4: [proj.pass_f, cot.pass_x], 5: [cot.pass_y]}
+    between = {0: [proj.pass_x, proj.pass_y], 3: [cot.pass_x], 4: [proj.pass_f, cot.pass_y]}
     for j in range(NF):
         for relay in between.get(j, []):
             relay()
@@ -594,9 +596,73 @@
     mid[...] = middle
     n2[...] = layer_norm(middle, sm[3:4, :], sm[4:5, :]).astype(BF16)
 
+    tokens = Gather(chips, n2, xa, n_s, n_r, n_h)
+    tokens.start()
+    xa[chips.me] = n2[...]
+    grads = Reduce(chips, g_part, g_pair, g_total, g_got, g1s, g1r, g2s, g2r)
+    downs = Reduce(chips, d_part, d_pair, dtot, None, d1s, d1r, None, None)
+    gub[...] = jnp.zeros_like(gub)
     loop(1, NS, down_from)
     cot.finish()
-    cot_own.wait()
+
+    def put(side, chip, values):
+        side.part[pl.ds(2 * chip, 2)] = values.astype(BF16).reshape(2, TOK, D)
+        side.pairing(chip).start()
+
+    def feed(k):
+        @pl.when(k == 1)
+        def _():
+            tokens.pass_x()
+            tokens.pass_y()
+
+        tokens.step(k)
+        m = chips.at(k)
+        rows = xa[pl.ds(2 * m, 2)].reshape(2 * TOK, D)
+        upper = dot(rows, up[...]) + ub[0:1, :]
+        square = upper * upper
+        bend = jnp.tanh(0.7978845608 * upper * (1.0 + 0.044715 * square))
+        half = 0.5 * (1.0 + bend)
+        active = (upper * half).astype(BF16)
+        slope = half + 0.5 * upper * (1.0 - bend * bend) * (0.7978845608 * (1.0 + 0.134145 * square))
+        cots = cota[pl.ds(2 * m, 2)].reshape(2 * TOK, D)
+        grad = (dot(cots, dn[...]) * slope).astype(BF16)
+        at = pl.ds(pl.multiple_of(m * 256, 256), 256)
+        act[at, :] = active
+        gu[at, :] = grad
+        gub[0:1, :] += jnp.sum(grad.astype(F32), axis=0, keepdims=True)
+        put(grads, m, dot(grad, up[...], 1, 1))
+        put(downs, m, dot(active, dn[...], 1, 1))
+
+        @pl.when(k > 0)
+        def _():
+            grads.merge(chips.at(k - 1))
+            downs.merge(chips.at(k - 1))
+
+        for at, message in ((3, 4), (4, 3), (5, 5), (6, 2)):
+
+            @pl.when(k == at)
+            def _():
+                grads.begin(message)
+
+    loop(0, NF, feed)
+    grads.merge(chips.fy)
+    grads.far()
+    downs.merge(chips.fy)
+    gup[...] = dot(xa[...].reshape(NS * TOK, D), gu[...], 0, 0).astype(BF16)
+    grads.turn()
+    gdn[...] = dot(cota[...].reshape(NS * TOK, D), act[...], 0, 0).astype(BF16)
+    grads.back()
+    grads.across()
+    tok[...] = jnp.zeros_like(tok)
+    own_cot = cota[chips.me].astype(F32)
+    tok[5:6, :] = jnp.sum(own_cot, axis=0, keepdims=True)
+    back, tok[3:4, :], tok[4:5, :] = norm_back(mid[...], sm[3:4, :], grads.finish())
+    total = own_cot + back
+    gmid[...] = total
+    low = total.astype(BF16)
+    branch[...] = low
+    tok[2:3, :] = jnp.sum(low.astype(F32), axis=0, keepdims=True)
+    gct[...] = dot(low, pj[...].reshape(D, D)).T.astype(BF16).reshape(NS, HD, TOK)
     loop(0, NF, lambda m: keep(m).wait())
     hidden.drain()
     cot.drain()
@@ -617,6 +683,9 @@
         remote(ctxo.at[other], ctxt.at[me], x_s.at[other], x_r.at[me], seq=other).wait_send()
 
     loop(1, NS, ctx_sent)
+    tokens.drain()
+    grads.drain()
+    loop(0, NF, lambda chip: downs.pairing(chip).wait_send())
 
 
 def vm():
@@ -632,21 +701,24 @@
 
 
 def params(number):
-    return pltpu.CompilerParams(collective_id=number, has_side_effects=True, vmem_limit_bytes=56 * MIB)
+    return pltpu.CompilerParams(collective_id=number, has_side_effects=True, vmem_limit_bytes=62 * MIB)
+
+
+def reduce_scratch(rows):
+    return [pltpu.VMEM((NF, rows, D), BF16), pltpu.VMEM((NF, rows, D), BF16), pltpu.VMEM((7, rows, D), BF16)]
 
 
 def run_a(*operands):
     shapes = [
-        ((NS, TOK, D), BF16), ((NS, TOK, D), BF16), ((NF, 192, 256), BF16), ((3, NS * TOK, HD), BF16),
-        ((NF, 256), F32), ((TOK, D), F32), ((TOK, D), BF16), ((TOK, D), BF16), ((192, D), BF16),
-        ((D, HID), BF16), ((D, HID), BF16), ((NS, HD, D), BF16), ((16, D), F32), ((8, HID), F32),
+        ((NS, TOK, D), BF16), ((NF, 192, 256), BF16), ((3, NS * TOK, HD), BF16), ((NF, 256), F32), ((TOK, D), F32),
+        ((TOK, D), BF16), ((192, D), BF16), ((16, D), F32), ((TOK, D), F32), ((TOK, D), BF16), ((NS, HD, TOK), BF16),
+        ((8, D), F32), ((NF, TOK, D), BF16), ((D, HID), BF16), ((D, HID), BF16), ((8, HID), F32),
     ]
-    specs = [hbm() if i < 2 else vm() for i in range(len(shapes))]
     return pl.pallas_call(
         kernel_a,
         out_shape=[jax.ShapeDtypeStruct(*s) for s in shapes],
-        in_specs=[hbm() if i == 1 else vm() for i in range(len(operands))],
-        out_specs=specs,
+        in_specs=[vm() for _ in operands],
+        out_specs=[hbm() if i == 0 else vm() for i in range(len(shapes))],
         scratch_shapes=[
             pltpu.VMEM((NS, TOK, D), BF16),
             pltpu.VMEM((NF, PACK, 128), BF16),
@@ -660,125 +732,23 @@
             pltpu.VMEM((PACK, 128), BF16),
             pltpu.VMEM((16, 128), BF16),
             pltpu.VMEM((NS, TOK, D), BF16),
-        ]
-        + sems(22, (8, 2), 8) * 3
-        + sems(8, 8, 8, 8, 16, 16, 3, 3, 16, 16, 16, 16, 8)
-        + [pltpu.SemaphoreType.DMA],
-        compiler_params=params(0),
-        name="gather_attend",
-    )(*operands)
-
-
-def kernel_m(
-    n2_ref, cot_hbm, up_ref, dn_ref, ub_ref, mid_ref, sm_ref, pj_ref,
-    gmid, branch, gct, tok, dtot, gup, gdn, gub,
-    xa, act, gu, g_part, g_pair, g_total, g_got, d_part, d_pair, cot_ref,
-    n_s, n_r, n_h, g1s, g1r, g2s, g2r, d1s, d1r, l_s,
-):
-    chips = Chips()
-    cots_in = pltpu.make_async_copy(cot_hbm, cot_ref, l_s)
-    cots_in.start()
-    sem = pltpu.get_barrier_semaphore()
-    for other in (chips.sib, chips.device(chips.r), chips.device(chips.l), chips.device(chips.y)):
-        pl.semaphore_signal(sem, inc=1, device_id={"seq": other}, device_id_type=MESH)
-    pl.semaphore_wait(sem, 4)
-    tokens = Gather(chips, n2_ref, xa, n_s, n_r, n_h)
-    tokens.start()
-    xa[chips.me] = n2_ref[...]
-    grads = Reduce(chips, g_part, g_pair, g_total, g_got, g1s, g1r, g2s, g2r)
-    downs = Reduce(chips, d_part, d_pair, dtot, None, d1s, d1r, None, None)
-    gub[...] = jnp.zeros_like(gub)
-    cots_in.wait()
-
-    def put(side, chip, values):
-        side.part[pl.ds(2 * chip, 2)] = values.astype(BF16).reshape(2, TOK, D)
-        side.pairing(chip).start()
-
-    def step(k):
-        @pl.when(k == 1)
-        def _():
-            tokens.pass_x()
-            tokens.pass_y()
-
-        tokens.step(k)
-        m = chips.at(k)
-        rows = xa[pl.ds(2 * m, 2)].reshape(2 * TOK, D)
-        upper = dot(rows, up_ref[...]) + ub_ref[0:1, :]
-        square = upper * upper
-        bend = jnp.tanh(0.7978845608 * upper * (1.0 + 0.044715 * square))
-        half = 0.5 * (1.0 + bend)
-        active = (upper * half).astype(BF16)
-        slope = half + 0.5 * upper * (1.0 - bend * bend) * (0.7978845608 * (1.0 + 0.134145 * square))
-        cots = cot_ref[pl.ds(2 * m, 2)].reshape(2 * TOK, D)
-        grad = (dot(cots, dn_ref[...]) * slope).astype(BF16)
-        at = pl.ds(pl.multiple_of(m * 256, 256), 256)
-        act[at, :] = active
-        gu[at, :] = grad
-        gub[0:1, :] += jnp.sum(grad.astype(F32), axis=0, keepdims=True)
-        put(grads, m, dot(grad, up_ref[...], 1, 1))
-        put(downs, m, dot(active, dn_ref[...], 1, 1))
-
-        @pl.when(k > 0)
-        def _():
-            grads.merge(chips.at(k - 1))
-            downs.merge(chips.at(k - 1))
-
-        for at, message in ((3, 4), (4, 3), (5, 5), (6, 2)):
-
-            @pl.when(k == at)
-            def _():
-                grads.begin(message)
-
-    loop(0, NF, step)
-    grads.merge(chips.fy)
-    grads.far()
-    downs.merge(chips.fy)
-    gup[...] = dot(xa[...].reshape(NS * TOK, D), gu[...], 0, 0).astype(BF16)
-    grads.turn()
-    gdn[...] = dot(cot_ref[...].reshape(NS * TOK, D), act[...], 0, 0).astype(BF16)
-    grads.back()
-    grads.across()
-    tok[...] = jnp.zeros_like(tok)
-    cot = cot_ref[chips.me].astype(F32)
-    tok[5:6, :] = jnp.sum(cot, axis=0, keepdims=True)
-    back, tok[3:4, :], tok[4:5, :] = norm_back(mid_ref[...], sm_ref[3:4, :], grads.finish())
-    total = cot + back
-    gmid[...] = total
-    low = total.astype(BF16)
-    branch[...] = low
-    tok[2:3, :] = jnp.sum(low.astype(F32), axis=0, keepdims=True)
-    gct[...] = dot(low, pj_ref[...].reshape(D, D)).T.astype(BF16).reshape(NS, HD, TOK)
-    tokens.drain()
-    grads.drain()
-    loop(0, NF, lambda chip: downs.pairing(chip).wait_send())
-
-
-def reduce_scratch(rows):
-    return [pltpu.VMEM((NF, rows, D), BF16), pltpu.VMEM((NF, rows, D), BF16), pltpu.VMEM((7, rows, D), BF16)]
-
-
-def run_m(*operands):
-    shapes = [
-        ((TOK, D), F32), ((TOK, D), BF16), ((NS, HD, TOK), BF16), ((8, D), F32), ((NF, TOK, D), BF16),
-        ((D, HID), BF16), ((D, HID), BF16), ((8, HID), F32),
-    ]
-    return pl.pallas_call(
-        kernel_m,
-        out_shape=[jax.ShapeDtypeStruct(*s) for s in shapes],
-        in_specs=[hbm() if i == 1 else vm() for i in range(len(operands))],
-        out_specs=[vm() for _ in shapes],
-        scratch_shapes=[
+            pltpu.VMEM((NS, TOK, D), BF16),
+            pltpu.VMEM((TOK, D), BF16),
+            pltpu.VMEM((D, HID), BF16),
+            pltpu.VMEM((D, HID), BF16),
+            pltpu.VMEM((NS, HD, D), BF16),
+            pltpu.VMEM((8, HID), F32),
             pltpu.VMEM((NS, TOK, D), BF16),
             pltpu.VMEM((NS * TOK, HID), BF16),
             pltpu.VMEM((NS * TOK, HID), BF16),
+            pltpu.VMEM((NS, TOK, D), BF16),
         ]
-        + [pltpu.VMEM((NS, TOK, D), BF16)]
         + reduce_scratch(TOK)
-        + [pltpu.VMEM((NS, TOK, D), BF16), pltpu.VMEM((NF, TOK, D), BF16), pltpu.VMEM((NS, TOK, D), BF16)]
-        + sems(22, (8, 2), 8, 8, 8, 16, 16, 8, 8)
-        + [pltpu.SemaphoreType.DMA],
-        compiler_params=params(1),
-        name="feed_forward",
+        + [pltpu.VMEM((NS, TOK, D), BF16), pltpu.VMEM((NF, TOK, D), BF16)]
+        + sems(22, (8, 2), 8) * 4
+        + sems(8, 8, 8, 8, 16, 16, 3, 3, 16, 16, 16, 16, 8, 8, 8, 16, 16, 8, 8),
+        compiler_params=params(0),
+        name="forward_and_feed",
     )(*operands)
 
 
@@ -1077,38 +1047,56 @@
     )(*operands)
 
 
+def kernel_f(*refs):
+    half = len(refs) // 2
+    for src, dst in zip(refs[: half - 1], refs[half:-1]):
+        dst[...] = src[...]
+    values = refs[half - 1][...]
+    mine = jnp.where(lax.rem(lax.axis_index("seq"), 2) == 0, values[0:8, 0:HD], values[0:8, HD:])
+    refs[-1][...] = values
+    refs[-1][0:8, 0:HD] = mine
+
+
+def run_f(*operands):
+    return pl.pallas_call(
+        kernel_f,
+        out_shape=[jax.ShapeDtypeStruct(o.shape, o.dtype) for o in operands],
+        in_specs=[vm() for _ in operands],
+        out_specs=[vm() for _ in operands],
+        name="finish",
+    )(*operands)
+
+
 def per_device(
     hidden_in, norm1_gain, norm1_shift, qkv_weight, query_bias, value_bias, proj_weight, proj_bias,
     norm2_gain, norm2_shift, up_weight, up_bias, down_weight, down_bias, out_cotangent,
 ):
     hid, cot = hidden_in[0], out_cotangent[0]
-    me = lax.axis_index("seq")
     vectors = [norm1_gain, norm1_shift, proj_bias, norm2_gain, norm2_shift, down_bias, query_bias, value_bias]
     vectors = jnp.concatenate([v[None] for v in vectors] + [up_bias.reshape(4, HD)], axis=0)
-    (nrm, cota, qkvt, qkvr, lse, middle, n2, ctx, wq, up, dn, pj, sm, ub) = run_a(
+    (nrm, qkvt, qkvr, lse, middle, ctx, wq, sm, gmid, branch, gctx, tok, downs, gup, gdn, gub) = run_a(
         hid, cot, qkv_weight.T, proj_weight.T, up_weight, down_weight.T, vectors
     )
-    gmid, branch, gctx, tok, downs, gup, gdn, gub = run_m(n2, cota, up, dn, ub, middle, sm, pj)
-    layer_out, input_grad, w_qkv, w_proj, w_up, w_down, vecs = run_b(
+    results = run_b(
         gctx, qkvt, qkvr, lse, wq, nrm, branch, downs, ctx, gdn, gup, hid, gmid, middle, sm, tok, gub
     )
-    mine = jnp.where(lax.rem(me, 2) == 0, vecs[:6, :64], vecs[:6, 64:])
+    layer_out, input_grad, w_qkv, w_proj, w_up, w_down, vecs = run_f(*results)
     return (
         layer_out[None],
         input_grad[None],
-        mine[0],
-        mine[1],
+        vecs[0, :64],
+        vecs[1, :64],
         w_qkv.T,
         vecs[8, :64],
         vecs[8, 64:],
         w_proj.T,
-        mine[2],
-        mine[3],
-        mine[4],
+        vecs[2, :64],
+        vecs[3, :64],
+        vecs[4, :64],
         w_up,
         vecs[9:11].reshape(256),
         w_down.T,
-        mine[5],
+        vecs[5, :64],
     )
 
 

time: 225 us -> 209 us (0.929)
  local copies, waits for them, and re-layouts: 14.7 us -> 5.41 us
  Pallas kernels: 208 us -> 202 us
    pallas_call x1, Pallas kernels: 59.2 us -> 2.12 us  [run_f(): pl.pallas_call(kernel_f, out_shape=[jax.ShapeDtypeStruct(o.shape, o.dtype...]
    pallas_call x1, Pallas kernels: 76.6 us -> 127 us  [run_a(): pl.pallas_call(kernel_a, out_shape=[jax.ShapeDtypeStruct(*s) for s in sha...]
    unnamed x6 -> x0, local copies, waits for them, and re-layouts: 9.38 us -> none
where the time goes in v5:
time: 209 us
  Pallas kernels  202 us (97%)
  local copies, waits for them, and re-layouts  5.41 us (3%)
    pallas_call x1, Pallas kernels, run_a(): pl.pallas_call(kernel_a, out_shape=[jax.ShapeDtypeStruct(*s) for s in sha...  127 us
    pallas_call x1, Pallas kernels, run_b(): pl.pallas_call(kernel_b, out_shape=[jax.ShapeDtypeStruct(*s) for s in sha...  73.7 us

profile of v5, /device:TPU:0, one launch (start us, length us, event | category | flops | bytes accessed | tf_op | source)
XLA Modules:
  0.0 208.5 jit_solution(2878873790016321701)
XLA Ops:
  0.6 0.7 reshape.36
  1.4 2.0 concatenate.3.vec_ref
  3.3 126.5 %forward_and_feed.1 = (bf16[16,128,1024]{2,1,0:T(8,128)(2,1)}, bf16[8,192,256]{2,1,0:T(8,128)(2,1)}, bf16[3,2048,64]{2,1,0:T(8,128)(2,1)}, f32[8,256]{1,0:T(8,12...) custom-call(bf16[128,1024]{1,0:T(8,128)(2,1)} %bitcast.36, ...), custom_call_target="tpu_custom_call" | custom-call | tf_op jit(solution)/shard_map/forward_and_feed/pallas_call | solution.py:717
  129.9 73.7 %attend_back.1 = (bf16[128,1024]{1,0:T(8,128)(2,1)}, bf16[128,1024]{1,0:T(8,128)(2,1)}, f32[192,128]{1,0:T(8,128)}, f32[64,128]{1,0:T(8,128)}, f32[128,256]{1,0:...) custom-call(bf16[16,64,128]{2,1,0:T(8,128)(2,1)} %get-tuple-element.45.gc_ref, ...), custom_call_target="tpu_custom_call" | custom-call | tf_op jit(solution)/shard_map/attend_back/pallas_call | solution.py:1015
  203.6 2.1 %finish.1 = (bf16[128,1024]{1,0:T(8,128)(2,1)}, bf16[128,1024]{1,0:T(8,128)(2,1)}, f32[192,128]{1,0:T(8,128)}, f32[64,128]{1,0:T(8,128)}, f32[128,256]{1,0:T(8,1...) custom-call(bf16[128,1024]{1,0:T(8,128)(2,1)} %get-tuple-element.61.refs_0_, bf16[128,1024]{1,0:T(8,128)(2,1)} %get-tuple-element.62.refs_1_, ...), custom_call_target="tpu_custom_call" | custom-call | tf_op jit(solution)/shard_map/finish/pallas_call | solution.py:1061
  205.7 1.2 slice_bitcast_fusion
  206.9 1.5 slice_bitcast_fusion.1

commit v6 on v5

--- a/solution.py
+++ b/solution.py
@@ -753,18 +753,22 @@
 
 
 def kernel_b(
-    gc_ref, qkvt, qkvr, lse, wq, nrm_hbm, branch, dtot, ctx_ref, gdn_ref, gup_ref, hid_ref, gmid, mid, sm, tok, gub,
+    gc_ref, qkvt_hbm, qkvr_hbm, lse, wq, nrm_hbm, branch, dtot, ctx_ref, gdn_ref, gup_ref, hid_ref, gmid, mid, sm, tok, gub,
     layer_out, input_grad, w_qkv, w_proj, w_up, w_down, small,
     dct, gjt, kr, dk, dv, part, pair, total, got, d_total, d_got, gpj, p_pair, p_total, p_got, d1,
-    u_pack, u_got, u_part, u_cross, u_keep, t_pack, t_got, t_part, t_cross, t_keep, gqkv, q1, tiles, m1, m2, sgot, nrm,
+    u_pack, u_got, u_part, u_cross, u_keep, t_pack, t_got, t_part, t_cross, t_keep, gqkv, q1, tiles, m1, m2, sgot, nrm, qkvt, qkvr,
     x_s, x_r, r1s, r1r, r2s, r2r, d2s, d2r, p1s, p1r, p2s, p2r, y_s, y_r, u_s, u_r, t_s, t_r, q_s, q_r, m_s, m_r,
-    v_s, v_r, l_s, n_c,
+    v_s, v_r, l_s, n_c, f_c, r_c,
 ):
     me, core, sib, row = places()
     chips = Chips()
     local = pltpu.make_async_copy(dtot, d_total, l_s)
     local.start()
     normed_in = pltpu.make_async_copy(nrm_hbm, nrm, n_c)
+    flat_in = pltpu.make_async_copy(qkvt_hbm, qkvt, f_c)
+    rows_in = pltpu.make_async_copy(qkvr_hbm, qkvr, r_c)
+    rows_in.start()
+    flat_in.start()
     normed_in.start()
     sem = barrier_seq_all(me)
     barrier_fsdp(sem, row)
@@ -834,6 +838,8 @@
     dct[me] = gc_ref[me]
     d1[me] = gdn_ref[block(me), :]
     kr[:, HD:] = key_extras(NS * TOK)
+    rows_in.wait()
+    flat_in.wait()
     kr[:, 0:HD] = qkvr[1]
     dk[...] = jnp.zeros_like(dk)
     dv[...] = jnp.zeros_like(dv)
@@ -970,6 +976,8 @@
         w_down[:, piece * 128 : piece * 128 + 128] = rows[piece * HD : piece * HD + HD]
     w_up[:, 0:128] = rows[256:384]
     w_up[:, 128:256] = rows[384:512]
+    back, _, _ = norm_back(hid_ref[...].astype(F32), sm[0:1, :], norms.finish())
+    input_grad[...] = (gmid[...] + back).astype(BF16)
     rows = rest.finish(t_keep)
     w_qkv[...] = rows[0:192]
     w_proj[...] = rows[192:256]
@@ -978,8 +986,6 @@
     for f in range(1, NF):
         vector += sgot[f]
     small[...] = vector
-    back, _, _ = norm_back(hid_ref[...].astype(F32), sm[0:1, :], norms.finish())
-    input_grad[...] = (gmid[...] + back).astype(BF16)
     norms.drain()
     downs.drain(False)
     projs.drain()
@@ -1015,7 +1021,7 @@
     return pl.pallas_call(
         kernel_b,
         out_shape=[jax.ShapeDtypeStruct(*s) for s in shapes],
-        in_specs=[hbm() if i in (5, 7) else vm() for i in range(len(operands))],
+        in_specs=[hbm() if i in (1, 2, 5, 7) else vm() for i in range(len(operands))],
         out_specs=[vm() for _ in shapes],
         scratch_shapes=[
             pltpu.VMEM((NS, HD, TOK), BF16),
@@ -1039,9 +1045,11 @@
             pltpu.VMEM((16, 128), F32),
             pltpu.VMEM((NF, 16, 128), F32),
             pltpu.VMEM((NS, TOK, D), BF16),
+            pltpu.VMEM((NF, 192, 256), BF16),
+            pltpu.VMEM((3, NS * TOK, HD), BF16),
         ]
         + sems(16, 16, 8, 8, 16, 16, 16, 16, 8, 8, 16, 16, 16, 16, 4, 4, 4, 4, 3, 3, 16, 16, 8, 8)
-        + [pltpu.SemaphoreType.DMA, pltpu.SemaphoreType.DMA],
+        + [pltpu.SemaphoreType.DMA] * 4,
         compiler_params=params(2),
         name="attend_back",
     )(*operands)

time: 209 us -> 208 us (level)
  no operation moved by 1% of the time
where the time goes in v6:
time: 208 us
  Pallas kernels  201 us (97%)
  local copies, waits for them, and re-layouts  5.41 us (3%)
    pallas_call x1, Pallas kernels, run_a(): pl.pallas_call(kernel_a, out_shape=[jax.ShapeDtypeStruct(*s) for s in sha...  127 us
    pallas_call x1, Pallas kernels, run_b(): pl.pallas_call(kernel_b, out_shape=[jax.ShapeDtypeStruct(*s) for s in sha...  72.7 us

profile of v6, /device:TPU:0, one launch (start us, length us, event | category | flops | bytes accessed | tf_op | source)
XLA Modules:
  0.0 207.5 jit_solution(14032464521898008234)
XLA Ops:
  0.6 0.7 reshape.36
  1.4 2.0 concatenate.3.vec_ref
  3.3 126.5 %forward_and_feed.1 = (bf16[16,128,1024]{2,1,0:T(8,128)(2,1)}, bf16[8,192,256]{2,1,0:T(8,128)(2,1)}, bf16[3,2048,64]{2,1,0:T(8,128)(2,1)}, f32[8,256]{1,0:T(8,12...) custom-call(bf16[128,1024]{1,0:T(8,128)(2,1)} %bitcast.36, ...), custom_call_target="tpu_custom_call" | custom-call | tf_op jit(solution)/shard_map/forward_and_feed/pallas_call | solution.py:717
  129.9 72.7 %attend_back.1 = (bf16[128,1024]{1,0:T(8,128)(2,1)}, bf16[128,1024]{1,0:T(8,128)(2,1)}, f32[192,128]{1,0:T(8,128)}, f32[64,128]{1,0:T(8,128)}, f32[128,256]{1,0:...) custom-call(bf16[16,64,128]{2,1,0:T(8,128)(2,1)} %get-tuple-element.45.gc_ref, ...), custom_call_target="tpu_custom_call" | custom-call | tf_op jit(solution)/shard_map/attend_back/pallas_call | solution.py:1021
  202.5 2.1 %finish.1 = (bf16[128,1024]{1,0:T(8,128)(2,1)}, bf16[128,1024]{1,0:T(8,128)(2,1)}, f32[192,128]{1,0:T(8,128)}, f32[64,128]{1,0:T(8,128)}, f32[128,256]{1,0:T(8,1...) custom-call(bf16[128,1024]{1,0:T(8,128)(2,1)} %get-tuple-element.61.refs_0_, bf16[128,1024]{1,0:T(8,128)(2,1)} %get-tuple-element.62.refs_1_, ...), custom_call_target="tpu_custom_call" | custom-call | tf_op jit(solution)/shard_map/finish/pallas_call | solution.py:1069
  204.6 1.2 slice_bitcast_fusion
  205.9 1.5 slice_bitcast_fusion.1
